TPU v7x, 32 devices: a whole 2x2x4 slice. The times are simulated.
32 devices in a mesh: dp: 8 (over y, x, core), tensor: 4 (over z).
Axes of the slice: x: 2, y: 2, z: 4, core: 2. Of those that a mesh axis runs over, the one named last changes fastest.
Arguments:
- latent: bfloat16 [8192, 1408], P(('dp', 'tensor')), may hold values from -6 to 6
- skip_in: bfloat16 [8192, 1408], P(('dp', 'tensor')), may hold values from -6 to 6
- text_tokens: bfloat16 [2560, 1408], P(('dp', 'tensor')), may hold values from -6 to 6
- time_embed: float32 [8, 1408], P('dp'), may hold values from -6 to 6
- t_index: int32 [8], P('dp'), may hold values from 0 to 999
- grid_pos: int32 [2, 8192], P(None, 'dp'), may hold values from 0 to 127, as said below
- skip_weight: bfloat16 [2816, 1408], P('dp'), may hold values from -0.109375 to 0.109375
- mod_weight: bfloat16 [1408, 1408], P('dp'), may hold values from -0.15625 to 0.15625
- vectors: bfloat16 [25, 1408], P(None, 'dp'), may hold values from -0.75 to 1.5
- up_bias: bfloat16 [6144], P('dp'), may hold values from -2 to 2
- qkv_weight: bfloat16 [1408, 3, 1408], P('dp', None, 'tensor'), may hold values from -0.15625 to 0.15625
- proj_weight: bfloat16 [1408, 1408], P('tensor', 'dp'), may hold values from -0.625 to 0.625
- query_weight: bfloat16 [1408, 1408], P('dp', 'tensor'), may hold values from -0.15625 to 0.15625
- text_weight: bfloat16 [1408, 2, 1408], P('dp', None, 'tensor'), may hold values from -0.15625 to 0.15625
- cross_weight: bfloat16 [1408, 1408], P('tensor', 'dp'), may hold values from -0.4375 to 0.4375
- up_weight: bfloat16 [1408, 6144], P('dp', 'tensor'), may hold values from -0.15625 to 0.15625
- down_weight: bfloat16 [6144, 1408], P('tensor', 'dp'), may hold values from -0.3125 to 0.3125
- out_grad: bfloat16 [8192, 1408], P(('dp', 'tensor')), may hold values from -6 to 6
Outputs:
- block_out: bfloat16 [8192, 1408], P(('dp', 'tensor'))
- latent_grad: float32 [8192, 1408], P(('dp', 'tensor'))
- skip_grad: float32 [8192, 1408], P(('dp', 'tensor'))
- text_grad: float32 [2560, 1408], P(('dp', 'tensor'))
- time_grad: float32 [8, 1408], P('dp', 'tensor')
- skip_weight_grad: float32 [2816, 1408], P('dp')
- mod_weight_grad: float32 [1408, 1408], P('dp')
- vectors_grad: float32 [25, 1408], P(None, 'dp')
- up_bias_grad: float32 [6144], P('dp')
- qkv_weight_grad: float32 [1408, 3, 1408], P('dp', None, 'tensor')
- proj_weight_grad: float32 [1408, 1408], P('tensor', 'dp')
- query_weight_grad: float32 [1408, 1408], P('dp', 'tensor')
- text_weight_grad: float32 [1408, 2, 1408], P('dp', None, 'tensor')
- cross_weight_grad: float32 [1408, 1408], P('tensor', 'dp')
- up_weight_grad: float32 [1408, 6144], P('dp', 'tensor')
- down_weight_grad: float32 [6144, 1408], P('tensor', 'dp')
Inputs may be any that keep to these rules, and one draw needn't show every extreme that they name: `grid_pos`: token i of an image lies at row i // w and column i % w of a grid whose width w is a power of two from 8 to 64, chosen for each image; some image has w = 8 and another w = 64.
All inputs are finite; a program needn't handle non-finite values.
Results may differ from a plain program's by a relative error of at most 0.029.
Values may be sent and summed in bfloat16 or wider, within the bound.
A program may use at most 384 MiB of HBM per device.

v0:
```python
import math

import jax
import jax.numpy as jnp
from jax import lax
from jax.sharding import PartitionSpec as P

HEADS = 16
HD = 88


EPSILON = 1e-06
HIGHEST = lax.Precision.HIGHEST
FLOAT = jnp.float32
BFLOAT = jnp.bfloat16


def layer_norm(values, norm_gain, norm_bias):
    centred = values - jnp.mean(values, axis=-1, keepdims=True)
    variance = jnp.mean(centred * centred, axis=-1, keepdims=True)
    return centred * lax.rsqrt(variance + EPSILON) * norm_gain + norm_bias


def head_norm(values, norm_gain):
    centred = values - jnp.mean(values, axis=-1, keepdims=True)
    variance = jnp.mean(centred * centred, axis=-1, keepdims=True)
    return centred * lax.rsqrt(variance + EPSILON) * norm_gain


def rotate(values, grid_rows, grid_cols):
    half_dim = values.shape[-1] // 2
    quarter = half_dim // 2
    inverse = 10000.0 ** (-jnp.arange(quarter, dtype=FLOAT) / quarter)
    pieces = []
    for position, offset in ((grid_rows, 0), (grid_cols, half_dim)):
        angles = position.astype(FLOAT)[:, None] * inverse[None, :]
        cosine = jnp.cos(angles)[:, None, :]
        sine_part = jnp.sin(angles)[:, None, :]
        front_part = values[..., offset : offset + quarter]
        back_part = values[..., offset + quarter : offset + half_dim]
        pieces.append(front_part * cosine - back_part * sine_part)
        pieces.append(back_part * cosine + front_part * sine_part)
    return jnp.concatenate(pieces, axis=-1)


def silu(values):
    return values / (1.0 + jnp.exp(-values))


def gelu(values):
    inner = math.sqrt(2.0 / math.pi) * (values + 0.044715 * values * values * values)
    return 0.5 * values * (1.0 + jnp.tanh(inner))


def attend_forward(queries, keys, values_in, scale):
    length, heads, depth = queries.shape
    rows_block = min(512, length)

    def one_block(query_block):
        scores = jnp.einsum("qhd,khd->hqk", query_block, keys, preferred_element_type=FLOAT) * scale
        row_peak = jnp.max(scores, axis=-1, keepdims=True)
        powers = jnp.exp(scores - row_peak)
        totals = jnp.sum(powers, axis=-1, keepdims=True)
        weights = (powers / totals).astype(BFLOAT)
        mixed = jnp.einsum("hqk,khd->qhd", weights, values_in, preferred_element_type=FLOAT)
        return (mixed, (row_peak + jnp.log(totals))[..., 0])

    blocks = queries.reshape(length // rows_block, rows_block, heads, depth)
    mixed, log_sums = lax.map(one_block, blocks)
    return (mixed.reshape(length, heads * depth), log_sums)


def attend_backward(queries, keys, values_in, log_sums, grad_out, scale):
    length, heads, depth = queries.shape
    rows_block = min(512, length)
    count = length // rows_block

    def one_block(carry, item):
        grad_keys, grad_values = carry
        query_block, log_block, grad_block = item
        scores = jnp.einsum("qhd,khd->hqk", query_block, keys, preferred_element_type=FLOAT) * scale
        probs = jnp.exp(scores - log_block[..., None])
        grad_probs = jnp.einsum("qhd,khd->hqk", grad_block, values_in, preferred_element_type=FLOAT)
        inner = jnp.sum(probs * grad_probs, axis=-1, keepdims=True)
        grad_scores = (probs * (grad_probs - inner)).astype(BFLOAT)
        grad_query = (
            jnp.einsum("hqk,khd->qhd", grad_scores, keys, preferred_element_type=FLOAT) * scale
        )
        grad_keys = (
            grad_keys
            + jnp.einsum("hqk,qhd->khd", grad_scores, query_block, preferred_element_type=FLOAT)
            * scale
        )
        grad_values = grad_values + jnp.einsum(
            "hqk,qhd->khd", probs.astype(BFLOAT), grad_block, preferred_element_type=FLOAT
        )
        return ((grad_keys, grad_values), grad_query)

    start_carry = (jnp.zeros(keys.shape, FLOAT), jnp.zeros(values_in.shape, FLOAT))
    items = (
        queries.reshape(count, rows_block, heads, depth),
        log_sums,
        grad_out.reshape(count, rows_block, heads, depth),
    )
    (grad_keys, grad_values), grad_queries = lax.scan(one_block, start_carry, items)
    return (grad_queries.reshape(length, heads, depth), grad_keys, grad_values)


def gather_weights(
    w_skip, w_mod, vectors, up_bias, w_qkv, w_proj, w_query, w_text, w_cross, w_up, w_down
):
    return (
        lax.all_gather(w_skip, "dp", axis=0, tiled=True),
        lax.all_gather(w_mod, "dp", axis=0, tiled=True),
        lax.all_gather(vectors, "dp", axis=1, tiled=True),
        lax.all_gather(up_bias, "dp", axis=0, tiled=True),
        lax.all_gather(w_qkv, "dp", axis=0, tiled=True),
        lax.all_gather(w_proj, "dp", axis=1, tiled=True),
        lax.all_gather(w_query, "dp", axis=0, tiled=True),
        lax.all_gather(w_text, "dp", axis=0, tiled=True),
        lax.all_gather(w_cross, "dp", axis=1, tiled=True),
        lax.all_gather(w_up, "dp", axis=0, tiled=True),
        lax.all_gather(w_down, "dp", axis=1, tiled=True),
    )


def sum_grads(pieces, dims):
    count = lax.axis_size("dp")
    flat = []
    for piece, dim in zip(pieces, dims):
        if dim == 0:
            flat.append(piece.reshape(count, -1))
        else:
            moved = piece.reshape(piece.shape[0], count, piece.shape[1] // count)
            flat.append(jnp.transpose(moved, (1, 0, 2)).reshape(count, -1))
    sizes_list = [item.shape[1] for item in flat]
    packed = jnp.concatenate(flat, axis=1)
    summed = lax.psum_scatter(
        packed.astype(jnp.bfloat16), "dp", scatter_dimension=0, tiled=True
    ).astype(jnp.float32)[0]
    results = []
    offset = 0
    for piece, dim, length in zip(pieces, dims, sizes_list):
        segment = summed[offset : offset + length]
        offset = offset + length
        if dim == 0:
            results.append(segment.reshape((piece.shape[0] // count,) + piece.shape[1:]))
        else:
            results.append(segment.reshape(piece.shape[0], piece.shape[1] // count))
    return tuple(results)


def on_device(
    latent,
    skip_in,
    text_tokens,
    time_embed,
    t_index,
    grid_pos,
    skip_weight,
    mod_weight,
    vectors,
    up_bias,
    qkv_weight,
    proj_weight,
    query_weight,
    text_weight,
    cross_weight,
    up_weight,
    down_weight,
    out_grad,
):
    split = lax.axis_size("tensor")
    place = lax.axis_index("tensor")
    width = latent.shape[1]
    local_rows = latent.shape[0]
    text_here = text_tokens.shape[0]
    heads_here = HEADS // split
    span = heads_here * HD
    head_start = place * span
    scale = 1.0 / math.sqrt(HD)
    gathered = gather_weights(
        skip_weight,
        mod_weight,
        vectors,
        up_bias,
        qkv_weight,
        proj_weight,
        query_weight,
        text_weight,
        cross_weight,
        up_weight,
        down_weight,
    )
    w_skip, w_mod, vector_table, bias_all, w_qkv, w_proj, w_query, w_text, w_cross, w_up, w_down = (
        gathered
    )
    table = vector_table.astype(FLOAT)

    def head_slice(index):
        return lax.dynamic_slice_in_dim(table[index], head_start, span, 0)

    def head_gains(index):
        return head_slice(index).reshape(heads_here, HD)

    def head_view(values):
        return values.reshape(values.shape[0], heads_here, HD)

    hidden_here = w_up.shape[1]
    hidden_start = place * hidden_here
    hidden_bias = lax.dynamic_slice_in_dim(bias_all.astype(FLOAT), hidden_start, hidden_here, 0)
    grid_rows = grid_pos[0]
    grid_cols = grid_pos[1]
    half_dim = width // 2
    frequencies = jnp.exp(-math.log(10000.0) * jnp.arange(half_dim, dtype=FLOAT) / half_dim)
    angles = t_index.astype(FLOAT)[:, None] * frequencies[None, :]
    condition = time_embed + jnp.concatenate([jnp.cos(angles), jnp.sin(angles)], axis=-1)
    silu_low = silu(condition).astype(BFLOAT)
    shift = jnp.dot(silu_low, w_mod, preferred_element_type=FLOAT) + table[5]
    joined = jnp.concatenate([latent.astype(FLOAT), skip_in.astype(FLOAT)], axis=-1)
    joined_gain = jnp.concatenate([table[0], table[1]])
    joined_bias = jnp.concatenate([table[2], table[3]])
    normed_low = layer_norm(joined, joined_gain, joined_bias).astype(BFLOAT)
    stream_one = jnp.dot(normed_low, w_skip, preferred_element_type=FLOAT) + table[4]
    attn_low = (layer_norm(stream_one, table[6], table[7]) + shift).astype(BFLOAT)
    attn_full, text_full, cot_full = (
        lax.all_gather(attn_low, "tensor", axis=0, tiled=True),
        lax.all_gather(text_tokens, "tensor", axis=0, tiled=True),
        lax.all_gather(out_grad, "tensor", axis=0, tiled=True),
    )
    length = attn_full.shape[0]
    qkv_bias = jnp.stack([head_slice(8), head_slice(9), head_slice(10)])
    projected = jnp.einsum("sd,dkh->skh", attn_full, w_qkv, preferred_element_type=FLOAT) + qkv_bias

    def prepare(raw_part, norm_gain):
        return rotate(head_norm(head_view(raw_part), norm_gain), grid_rows, grid_cols)

    queries = prepare(projected[:, 0], head_gains(12)).astype(BFLOAT)
    keys = prepare(projected[:, 1], head_gains(13)).astype(BFLOAT)
    values_self = head_view(projected[:, 2]).astype(BFLOAT)
    mixed, log_sums = attend_forward(queries, keys, values_self, scale)
    mixed_low = mixed.astype(BFLOAT)
    stream_two = (
        stream_one
        + lax.psum_scatter(
            jnp.dot(mixed_low, w_proj, preferred_element_type=FLOAT).astype(jnp.bfloat16),
            "tensor",
            scatter_dimension=0,
            tiled=True,
        ).astype(jnp.float32)
        + table[11]
    )
    cross_low = layer_norm(stream_two, table[14], table[15]).astype(BFLOAT)
    cross_full = lax.all_gather(cross_low, "tensor", axis=0, tiled=True)
    cross_raw = jnp.dot(cross_full, w_query, preferred_element_type=FLOAT) + head_slice(16)
    text_raw = jnp.einsum(
        "md,dkh->mkh", text_full, w_text, preferred_element_type=FLOAT
    ) + jnp.stack([head_slice(17), head_slice(18)])
    cross_queries = head_norm(head_view(cross_raw), head_gains(20)).astype(BFLOAT)
    text_keys = head_norm(head_view(text_raw[:, 0]), head_gains(21)).astype(BFLOAT)
    text_values = head_view(text_raw[:, 1]).astype(BFLOAT)
    cross_mixed, cross_logs = attend_forward(cross_queries, text_keys, text_values, scale)
    cross_mixed_low = cross_mixed.astype(BFLOAT)
    stream_three = (
        stream_two
        + lax.psum_scatter(
            jnp.dot(cross_mixed_low, w_cross, preferred_element_type=FLOAT).astype(jnp.bfloat16),
            "tensor",
            scatter_dimension=0,
            tiled=True,
        ).astype(jnp.float32)
        + table[19]
    )
    mlp_low = layer_norm(stream_three, table[22], table[23]).astype(BFLOAT)
    mlp_full = lax.all_gather(mlp_low, "tensor", axis=0, tiled=True)
    hidden_pre = jnp.dot(mlp_full, w_up, preferred_element_type=FLOAT) + hidden_bias
    hidden_low = gelu(hidden_pre).astype(BFLOAT)
    block_out = (
        stream_three
        + lax.psum_scatter(
            jnp.dot(hidden_low, w_down, preferred_element_type=FLOAT).astype(jnp.bfloat16),
            "tensor",
            scatter_dimension=0,
            tiled=True,
        ).astype(jnp.float32)
        + table[24]
    ).astype(BFLOAT)
    gathered = gather_weights(
        skip_weight,
        mod_weight,
        vectors,
        up_bias,
        qkv_weight,
        proj_weight,
        query_weight,
        text_weight,
        cross_weight,
        up_weight,
        down_weight,
    )
    w_skip, w_mod, vector_table, bias_all, w_qkv, w_proj, w_query, w_text, w_cross, w_up, w_down = (
        gathered
    )
    rows_grad = {}

    def spread(part):
        return lax.dynamic_update_slice_in_dim(
            jnp.zeros((width,), FLOAT), part.reshape(-1), head_start, 0
        )

    cot_here = out_grad.astype(FLOAT)
    rows_grad[24] = jnp.sum(cot_here, axis=0)
    grad_hidden = jnp.einsum("sd,hd->sh", cot_full, w_down, preferred_element_type=FLOAT)
    grad_down = jnp.einsum("sh,sd->hd", hidden_low, cot_full, preferred_element_type=FLOAT)
    grad_pre = jax.vjp(gelu, hidden_pre)[1](grad_hidden)[0]
    pre_low = grad_pre.astype(BFLOAT)
    grad_up = jnp.einsum("sd,sh->dh", mlp_full, pre_low, preferred_element_type=FLOAT)
    grad_hidden_bias = jnp.sum(pre_low, axis=0, dtype=FLOAT)
    mlp_back_term = jnp.einsum("sh,dh->sd", pre_low, w_up, preferred_element_type=FLOAT)
    grad_mlp_in = lax.psum_scatter(
        mlp_back_term.astype(jnp.bfloat16), "tensor", scatter_dimension=0, tiled=True
    ).astype(jnp.float32)
    into_three, rows_grad[22], rows_grad[23] = jax.vjp(
        layer_norm, stream_three, table[22], table[23]
    )[1](grad_mlp_in)
    grad_three = cot_here + into_three
    three_low = grad_three.astype(BFLOAT)
    three_full = lax.all_gather(three_low, "tensor", axis=0, tiled=True)
    rows_grad[19] = jnp.sum(grad_three, axis=0)
    grad_cross = jnp.einsum("sh,sd->hd", cross_mixed_low, three_full, preferred_element_type=FLOAT)
    grad_cross_mixed = jnp.einsum(
        "sd,hd->sh", three_full, w_cross, preferred_element_type=FLOAT
    ).astype(BFLOAT)
    grad_cq, grad_ck, grad_cv = attend_backward(
        cross_queries, text_keys, text_values, cross_logs, head_view(grad_cross_mixed), scale
    )
    into_cq, gain_cq = jax.vjp(head_norm, head_view(cross_raw), head_gains(20))[1](grad_cq)
    into_ck, gain_ck = jax.vjp(head_norm, head_view(text_raw[:, 0]), head_gains(21))[1](grad_ck)
    rows_grad[20] = spread(gain_cq)
    rows_grad[21] = spread(gain_ck)
    text_length = text_full.shape[0]
    cq_low = into_cq.reshape(length, span).astype(BFLOAT)
    ckv_low = jnp.stack(
        [into_ck.reshape(text_length, span), grad_cv.reshape(text_length, span)], axis=1
    ).astype(BFLOAT)
    rows_grad[16] = spread(jnp.sum(cq_low, axis=0, dtype=FLOAT))
    text_sums = jnp.sum(ckv_low, axis=0, dtype=FLOAT)
    rows_grad[17] = spread(text_sums[0])
    rows_grad[18] = spread(text_sums[1])
    grad_query = jnp.einsum("sd,sh->dh", cross_full, cq_low, preferred_element_type=FLOAT)
    grad_text = jnp.einsum("md,mkh->dkh", text_full, ckv_low, preferred_element_type=FLOAT)
    cross_back_term = jnp.einsum("sh,dh->sd", cq_low, w_query, preferred_element_type=FLOAT)
    text_back_term = jnp.einsum("mkh,dkh->md", ckv_low, w_text, preferred_element_type=FLOAT)
    cross_packed = jnp.concatenate(
        [
            cross_back_term.reshape(split, local_rows, width),
            text_back_term.reshape(split, text_here, width),
        ],
        axis=1,
    )
    cross_summed = lax.psum_scatter(
        cross_packed.astype(jnp.bfloat16), "tensor", scatter_dimension=0, tiled=True
    ).astype(jnp.float32)[0]
    grad_cross_in = cross_summed[:local_rows]
    text_grad = cross_summed[local_rows:]
    into_two, rows_grad[14], rows_grad[15] = jax.vjp(layer_norm, stream_two, table[14], table[15])[
        1
    ](grad_cross_in)
    grad_two = grad_three + into_two
    two_low = grad_two.astype(BFLOAT)
    two_full = lax.all_gather(two_low, "tensor", axis=0, tiled=True)
    rows_grad[11] = jnp.sum(grad_two, axis=0)
    grad_proj = jnp.einsum("sh,sd->hd", mixed_low, two_full, preferred_element_type=FLOAT)
    grad_mixed = jnp.einsum("sd,hd->sh", two_full, w_proj, preferred_element_type=FLOAT).astype(
        BFLOAT
    )
    grad_q, grad_k, grad_v = attend_backward(
        queries, keys, values_self, log_sums, head_view(grad_mixed), scale
    )
    into_q, gain_q = jax.vjp(prepare, projected[:, 0], head_gains(12))[1](grad_q)
    into_k, gain_k = jax.vjp(prepare, projected[:, 1], head_gains(13))[1](grad_k)
    rows_grad[12] = spread(gain_q)
    rows_grad[13] = spread(gain_k)
    qkv_low = jnp.stack([into_q, into_k, grad_v.reshape(length, span)], axis=1).astype(BFLOAT)
    qkv_sums = jnp.sum(qkv_low, axis=0, dtype=FLOAT)
    rows_grad[8] = spread(qkv_sums[0])
    rows_grad[9] = spread(qkv_sums[1])
    rows_grad[10] = spread(qkv_sums[2])
    grad_qkv = jnp.einsum("sd,skh->dkh", attn_full, qkv_low, preferred_element_type=FLOAT)
    attn_back_term = jnp.einsum("skh,dkh->sd", qkv_low, w_qkv, preferred_element_type=FLOAT)
    shift_part = jnp.sum(attn_back_term, axis=0)
    rows_grad[5] = shift_part
    into_silu = jnp.dot(w_mod.astype(FLOAT), shift_part, precision=HIGHEST)
    embed_part = jax.vjp(silu, condition)[1](into_silu[None, :])[0]
    grad_mod = silu_low.astype(FLOAT).reshape(-1)[:, None] * shift_part[None, :]
    token_span = local_rows * width
    attn_packed = jnp.concatenate(
        [attn_back_term.reshape(split, token_span), embed_part.reshape(split, width // split)],
        axis=1,
    )
    attn_summed = lax.psum_scatter(
        attn_packed.astype(jnp.bfloat16), "tensor", scatter_dimension=0, tiled=True
    ).astype(jnp.float32)[0]
    grad_attn_in = attn_summed[:token_span].reshape(local_rows, width)
    time_grad = attn_summed[token_span:].reshape(1, width // split)
    into_one, rows_grad[6], rows_grad[7] = jax.vjp(layer_norm, stream_one, table[6], table[7])[1](
        grad_attn_in
    )
    grad_one = grad_two + into_one
    rows_grad[4] = jnp.sum(grad_one, axis=0)
    one_low = grad_one.astype(BFLOAT)
    grad_skip_w = jnp.einsum("sc,sd->cd", normed_low, one_low, preferred_element_type=FLOAT)
    grad_joined = jnp.einsum("sd,cd->sc", one_low, w_skip, preferred_element_type=FLOAT)
    into_joined, gain_joined, bias_joined = jax.vjp(layer_norm, joined, joined_gain, joined_bias)[
        1
    ](grad_joined)
    rows_grad[0] = gain_joined[:width]
    rows_grad[1] = gain_joined[width:]
    rows_grad[2] = bias_joined[:width]
    rows_grad[3] = bias_joined[width:]
    latent_grad = into_joined[:, :width]
    skip_grad = into_joined[:, width:]
    table_grad = jnp.stack([rows_grad[index] for index in range(25)])
    bias_grad_all = lax.dynamic_update_slice_in_dim(
        jnp.zeros((bias_all.shape[0],), FLOAT), grad_hidden_bias, hidden_start, 0
    )
    summed = sum_grads(
        (
            grad_skip_w,
            grad_mod,
            table_grad,
            bias_grad_all,
            grad_qkv,
            grad_proj,
            grad_query,
            grad_text,
            grad_cross,
            grad_up,
            grad_down,
        ),
        (0, 0, 1, 0, 0, 1, 0, 0, 1, 0, 1),
    )
    sharded = (summed[4], summed[5], summed[6], summed[7], summed[8], summed[9], summed[10])
    shared = (
        lax.psum(summed[0].astype(jnp.bfloat16), "tensor").astype(jnp.float32),
        lax.psum(summed[1].astype(jnp.bfloat16), "tensor").astype(jnp.float32),
        lax.psum(summed[2].astype(jnp.bfloat16), "tensor").astype(jnp.float32),
        lax.psum(summed[3].astype(jnp.bfloat16), "tensor").astype(jnp.float32),
    )
    return (
        block_out,
        latent_grad,
        skip_grad,
        text_grad,
        time_grad,
        shared[0],
        shared[1],
        shared[2],
        shared[3],
        sharded[0],
        sharded[1],
        sharded[2],
        sharded[3],
        sharded[4],
        sharded[5],
        sharded[6],
    )


def solution(mesh):
    placed = (
        P(("dp", "tensor"), None),
        P(("dp", "tensor"), None),
        P(("dp", "tensor"), None),
        P("dp", None),
        P("dp"),
        P(None, "dp"),
        P("dp", None),
        P("dp", None),
        P(None, "dp"),
        P("dp"),
        P("dp", None, "tensor"),
        P("tensor", "dp"),
        P("dp", "tensor"),
        P("dp", None, "tensor"),
        P("tensor", "dp"),
        P("dp", "tensor"),
        P("tensor", "dp"),
        P(("dp", "tensor"), None),
    )
    return jax.shard_map(
        on_device,
        mesh=mesh,
        in_specs=placed,
        out_specs=(
            P(("dp", "tensor"), None),
            P(("dp", "tensor"), None),
            P(("dp", "tensor"), None),
            P(("dp", "tensor"), None),
            P("dp", "tensor"),
            P("dp", None),
            P("dp", None),
            P(None, "dp"),
            P("dp"),
            P("dp", None, "tensor"),
            P("tensor", "dp"),
            P("dp", "tensor"),
            P("dp", None, "tensor"),
            P("tensor", "dp"),
            P("dp", "tensor"),
            P("tensor", "dp"),
        ),
        check_vma=False,
    )
```

profile of v0, /device:TPU:24, one launch (start us, length us, event | category | flops | bytes accessed | tf_op | source)
XLA Modules:
  0.0 1925.3 jit_solution(14295627003892416189)
XLA Ops:
  24.6 22.1 %all-gather.17.cloned.1.call-done = bf16[1408,1408]{1,0:T(8,128)(2,1)} async-done(((bf16[176,1408]{1,0:T(8,128)(2,1)}), bf16[1408,1408]{1,0:T(8,128)(2,1)}) %all-gather.17.cloned.1.call-update) | async-done | bytes 3964944 | tf_op jit(solution)/shard_map/all_gather | solution.py:114
  49.5 51.6 %all-gather.15.cloned.1.call-done = bf16[2816,1408]{1,0:T(8,128)(2,1)} async-done(((bf16[352,1408]{1,0:T(8,128)(2,1)}), bf16[2816,1408]{1,0:T(8,128)(2,1)}) %all-gather.15.cloned.1.call-update) | async-done | bytes 7929872 | tf_op jit(solution)/shard_map/all_gather | solution.py:113
  137.1 58.6 %all-gather.19.cloned.1.call-done = bf16[1024,1408]{1,0:T(8,128)(2,1)} async-done(((bf16[256,1408]{1,0:T(8,128)(2,1)}), bf16[1024,1408]{1,0:T(8,128)(2,1)}) %all-gather.19.cloned.1.call-update) | async-done | bytes 2883600 | tf_op jit(solution)/shard_map/all_gather | solution.py:227
  233.0 54.5 %reduce-scatter.6.cloned.1.call-done = bf16[256,1408]{1,0:T(8,128)(2,1)} async-done(((bf16[1024,1408]{1,0:T(8,128)(2,1)}), bf16[256,1408]{1,0:T(8,128)(2,1)}) %reduce-scatter.6.cloned.1.call-update) | async-done | bytes 720912 | tf_op jit(solution)/shard_map/reduce_scatter | solution.py:245
  305.3 17.2 all_gather.73
  322.5 29.2 %all_gather.71 = bf16[320,1408]{1,0:T(8,128)(2,1)S(1)} all-gather(bf16[80,1408]{1,0:T(8,128)(2,1)S(1)} %copy-done.81), channel_id=1, replica_groups=mesh['dp'=8,'tensor'=4] {'tensor'}, dimensions={0}, use_global_device_ids=true | all-gather | bytes 1126400 | tf_op jit(solution)/shard_map/all_gather | solution.py:228
  355.4 33.6 %all-gather.23.cloned.1.call-done = bf16[1024,1408]{1,0:T(8,128)(2,1)} async-done(((bf16[256,1408]{1,0:T(8,128)(2,1)}), bf16[1024,1408]{1,0:T(8,128)(2,1)}) %all-gather.23.cloned.1.call-update) | async-done | bytes 2883600 | tf_op jit(solution)/shard_map/all_gather | solution.py:254
  407.5 54.1 %reduce-scatter.8.cloned.1.call-done = bf16[256,1408]{1,0:T(8,128)(2,1)} async-done(((bf16[1024,1408]{1,0:T(8,128)(2,1)}), bf16[256,1408]{1,0:T(8,128)(2,1)}) %reduce-scatter.8.cloned.1.call-update) | async-done | bytes 720912 | tf_op jit(solution)/shard_map/reduce_scatter | solution.py:266
  476.3 25.8 %all-gather.29.cloned.1.call-done = bf16[1408,1536]{1,0:T(8,128)(2,1)} async-done(((bf16[176,1536]{1,0:T(8,128)(2,1)}), bf16[1408,1536]{1,0:T(8,128)(2,1)}) %all-gather.29.cloned.1.call-update) | async-done | bytes 4325392 | tf_op jit(solution)/shard_map/all_gather | solution.py:122
  502.1 58.6 %all-gather.27.cloned.1.call-done = bf16[1024,1408]{1,0:T(8,128)(2,1)} async-done(((bf16[256,1408]{1,0:T(8,128)(2,1)}), bf16[1024,1408]{1,0:T(8,128)(2,1)}) %all-gather.27.cloned.1.call-update) | async-done | bytes 2883600 | tf_op jit(solution)/shard_map/all_gather | solution.py:275
  570.2 50.1 %all-gather.33.cloned.1.call-done = bf16[1024,1408]{1,0:T(8,128)(2,1)} async-done(((bf16[256,1408]{1,0:T(8,128)(2,1)}), bf16[1024,1408]{1,0:T(8,128)(2,1)}) %all-gather.33.cloned.1.call-update) | async-done | bytes 2883600 | tf_op jit(solution)/shard_map/all_gather | solution.py:229
  620.2 40.3 %all-gather.31.cloned.1.call-done = bf16[1536,1408]{0,1:T(8,128)(2,1)} async-done(((bf16[1536,176]{0,1:T(8,128)(2,1)}), bf16[1536,1408]{0,1:T(8,128)(2,1)}) %all-gather.31.cloned.1.call-update) | async-done | bytes 4325392 | tf_op jit(solution)/shard_map/all_gather | solution.py:123
  694.7 44.7 %reduce-scatter.12.cloned.1.call-done = bf16[256,1408]{1,0:T(8,128)(2,1)} async-done(((bf16[1024,1408]{1,0:T(8,128)(2,1)}), bf16[256,1408]{1,0:T(8,128)(2,1)}) %reduce-scatter.12.cloned.1.call-update) | async-done | bytes 720912 | tf_op jit(solution)/shard_map/reduce_scatter | solution.py:320
  742.2 55.4 %reduce-scatter.10.cloned.1.call-done = bf16[256,1408]{1,0:T(8,128)(2,1)} async-done(((bf16[1024,1408]{1,0:T(8,128)(2,1)}), bf16[256,1408]{1,0:T(8,128)(2,1)}) %reduce-scatter.10.cloned.1.call-update) | async-done | bytes 720912 | tf_op jit(solution)/shard_map/reduce_scatter | solution.py:280
  802.7 58.0 %all-gather.35.cloned.1.call-done = bf16[1024,1408]{1,0:T(8,128)(2,1)} async-done(((bf16[256,1408]{1,0:T(8,128)(2,1)}), bf16[1024,1408]{1,0:T(8,128)(2,1)}) %all-gather.35.cloned.1.call-update) | async-done | bytes 2883600 | tf_op jit(solution)/shard_map/all_gather | solution.py:328
  900.8 70.7 %reduce-scatter.14.cloned.1.call-done = bf16[1,336,1408]{2,1,0:T(8,128)(2,1)} async-done(((bf16[4,336,1408]{2,1,0:T(8,128)(2,1)}), bf16[1,336,1408]{2,1,0:T(8,128)(2,1)}) %reduce-scatter.14.cloned.1.call-update) | async-done | bytes 946192 | tf_op jit(solution)/shard_map/reduce_scatter | solution.py:361
  1082.0 62.6 %while.61 = (s32[]{:T(128)}, f32[1024,4,88]{0,2,1:T(8,128)S(1)}, f32[1024,4,88]{0,2,1:T(8,128)}, f32[2,512,4,88]{1,0,3,2:T(2,128)}, bf16[2,512,4,88]{1,3,2,0:T(8...) while((s32[]{:T(128)}, f32[1024,4,88]{0,2,1:T(8,128)S(1)}, ...), condition=%wide.region_43.44_spmd.clone.clone, body=%wide.region_41.43_spmd.clone.sunk.clone | while | flops 1872640000 | bytes 75948160 | solution.py:105
  1244.5 50.9 %all-reduce.16.cloned.1.call-done = bf16[4,360800]{1,0:T(4,128)(2,1)} async-done(((bf16[4,360800]{1,0:T(4,128)(2,1)}), bf16[4,360800]{1,0:T(4,128)(2,1)}) %all-reduce.16.cloned.1.call-update) | async-done | bytes 2886416
  1363.5 16.4 dynamic-update-slice.4
  1411.0 23.6 %dynamic-update-slice.9 = bf16[8,1784880]{1,0:T(8,128)(2,1)} dynamic-update-slice(bf16[8,1784880]{1,0:T(8,128)(2,1)} %dynamic-update-slice.8, bf16[8,270336]{1,0:T(8,128)(2,1)} %reshape.856, s32[]{} %constant.251, s32[]{} %constant.260) | dynamic-update-slice | bytes 8650756
  1434.6 23.3 %dynamic-update-slice.10 = bf16[8,1784880]{1,0:T(8,128)(2,1)} dynamic-update-slice(bf16[8,1784880]{1,0:T(8,128)(2,1)} %dynamic-update-slice.9, bf16[8,270336]{1,0:T(8,128)(2,1)} %reshape.858, s32[]{} %constant.251, s32[]{} %constant.261) | dynamic-update-slice | bytes 8650756 | tf_op jit(solution)/shard_map/concatenate | solution.py:137
  1466.5 337.1 %all-reduce.18.cloned.1.call-done = bf16[8,1784880]{1,0:T(8,128)(2,1)} async-done(((bf16[8,1784880]{1,0:T(8,128)(2,1)}), bf16[8,1784880]{1,0:T(8,128)(2,1)}) %all-reduce.18.cloned.1.call-update) | async-done | bytes 28558096
  1817.6 20.8 %dynamic-slice_reduce_fusion = bf16[495616]{0:T(1024)(128)(2,1)S(1)} fusion(bf16[8,1784880]{1,0:T(8,128)(2,1)} %all-reduce.18.cloned.1.call-done, u32[]{:T(128)} %bitcast.73), kind=kLoop, calls=%fused_computation.138 | loop fusion | bytes 1982468 | tf_op jit(solution)/shard_map/slice | solution.py:144
  1857.2 16.8 all-reduce.10
  (804 shorter events, 726.0 us)
Async XLA Ops:
  7.2 39.5 %all-gather.17.cloned.1.call-start = ((), (), s32[]{:S(2)}) async-start(), calls=%async_computation.6 | async-start | bytes 4460544 | tf_op jit(solution)/shard_map/all_gather | solution.py:114
  7.9 93.1 %all-gather.15.cloned.1.call-start = ((), (), s32[]{:S(2)}) async-start(), calls=%async_computation.5 | async-start | bytes 8921088 | tf_op jit(solution)/shard_map/all_gather | solution.py:113
  8.7 128.4 %all-gather.21.cloned.1.call-start = ((), (), s32[]{:S(2)}) async-start(), calls=%async_computation.8 | async-start | bytes 3649536 | tf_op jit(solution)/shard_map/all_gather | solution.py:117
  9.4 186.3 %all-gather.19.cloned.1.call-start = ((), (), s32[]{:S(2)}) async-start(), calls=%async_computation.7 | async-start | bytes 3604480 | tf_op jit(solution)/shard_map/all_gather | solution.py:227
  22.5 266.7 %copy-start.99 = (f32[1408]{0:T(1024)}, f32[1408]{0:T(1024)S(1)}, u32[]{:S(2)}) copy-start(f32[1408]{0:T(1024)S(1)} %get-tuple-element.423) | copy-start | bytes 16900
  109.3 178.2 %reduce-scatter.6.cloned.1.call-start = ((), (), s32[]{:S(2)}) async-start(), calls=%async_computation.9 | async-start | bytes 3604480 | tf_op jit(solution)/shard_map/reduce_scatter | solution.py:245
  231.3 120.4 %all-gather.25.cloned.1.call-start = ((), (), s32[]{:S(2)}) async-start(), calls=%async_computation.11 | async-start | bytes 2433024 | tf_op jit(solution)/shard_map/all_gather | solution.py:120
  233.0 156.0 %all-gather.23.cloned.1.call-start = ((), (), s32[]{:S(2)}) async-start(), calls=%async_computation.10 | async-start | bytes 3604480 | tf_op jit(solution)/shard_map/all_gather | solution.py:254
  290.5 171.2 %reduce-scatter.8.cloned.1.call-start = ((), (), s32[]{:S(2)}) async-start(), calls=%async_computation.12 | async-start | bytes 3604480 | tf_op jit(solution)/shard_map/reduce_scatter | solution.py:266
  406.7 95.4 %all-gather.29.cloned.1.call-start = ((), (), s32[]{:S(2)}) async-start(), calls=%async_computation.14 | async-start | bytes 4866048 | tf_op jit(solution)/shard_map/all_gather | solution.py:122
  407.5 153.3 %all-gather.27.cloned.1.call-start = ((), (), s32[]{:S(2)}) async-start(), calls=%async_computation.13 | async-start | bytes 3604480 | tf_op jit(solution)/shard_map/all_gather | solution.py:275
  465.3 154.9 %all-gather.33.cloned.1.call-start = ((), (), s32[]{:S(2)}) async-start(), calls=%async_computation.17 | async-start | bytes 3604480 | tf_op jit(solution)/shard_map/all_gather | solution.py:229
  466.1 194.4 %all-gather.31.cloned.1.call-start = ((), (), s32[]{:S(2)}) async-start(), calls=%async_computation.15 | async-start | bytes 4866048 | tf_op jit(solution)/shard_map/all_gather | solution.py:123
  466.7 272.7 %reduce-scatter.12.cloned.1.call-start = ((), (), s32[]{:S(2)}) async-start(), calls=%async_computation.18 | async-start | bytes 3604480 | tf_op jit(solution)/shard_map/reduce_scatter | solution.py:320
  476.3 208.2 %copy-start.160 = (f32[1536]{0:T(1024)}, f32[1536]{0:T(1024)S(1)}, u32[]{:S(2)}) copy-start(f32[1536]{0:T(1024)S(1)} %dynamic_slice.73) | copy-start | bytes 18436
  684.4 113.1 %reduce-scatter.10.cloned.1.call-start = ((), (), s32[]{:S(2)}) async-start(), calls=%async_computation.16 | async-start | bytes 3604480 | tf_op jit(solution)/shard_map/reduce_scatter | solution.py:280
  694.7 166.0 %all-gather.35.cloned.1.call-start = ((), (), s32[]{:S(2)}) async-start(), calls=%async_computation.19 | async-start | bytes 3604480 | tf_op jit(solution)/shard_map/all_gather | solution.py:328
  802.6 168.9 %reduce-scatter.14.cloned.1.call-start = ((), (), s32[]{:S(2)}) async-start(), calls=%async_computation.20 | async-start | bytes 4730880 | tf_op jit(solution)/shard_map/reduce_scatter | solution.py:361
  884.9 160.6 %copy-start.66 = (bf16[320,1,352]{2,0,1:T(8,128)(2,1)}, bf16[320,1,352]{2,0,1:T(8,128)(2,1)S(1)}, u32[]{:S(2)}) copy-start(bf16[320,1,352]{2,0,1:T(8,128)(2,1)S(1)} %copy.156) | copy-start | bytes 675844
  887.4 158.2 %copy-start.67 = (bf16[320,1,352]{2,0,1:T(8,128)(2,1)}, bf16[320,1,352]{2,0,1:T(8,128)(2,1)S(1)}, u32[]{:S(2)}) copy-start(bf16[320,1,352]{2,0,1:T(8,128)(2,1)S(1)} %copy.155) | copy-start | bytes 675844
  900.6 173.7 %all-gather.37.cloned.1.call-start = ((), (), s32[]{:S(2)}) async-start(), calls=%async_computation.21 | async-start | bytes 3604480 | tf_op jit(solution)/shard_map/all_gather | solution.py:371
  978.7 316.6 %all-reduce.16.cloned.1.call-start = ((), (), s32[]{:S(2)}) async-start(), calls=%async_computation.22 | async-start | bytes 5773312
  1183.1 620.5 %all-reduce.18.cloned.1.call-start = ((), (), s32[]{:S(2)}) async-start(), calls=%async_computation.23 | async-start | bytes 57118720
  1458.0 456.3 %all-reduce.20.cloned.1.call-start = ((), (), s32[]{:S(2)}) async-start(), calls=%async_computation.24 | async-start | bytes 2973696 | tf_op jit(solution)/shard_map/psum | solution.py:445
  (170 other events, 2307.4 us)
Sparse Core Ops, SparseCore 0:
  9.9 36.7 all-gather.16
  48.6 52.4 all-gather.14
  103.0 34.0 all-gather.20
  139.1 56.5 all-gather.18
  231.4 56.0 reduce-scatter.5
  289.8 33.0 all-gather.24
  325.0 63.9 all-gather.22
  406.9 54.7 reduce-scatter.7
  463.5 38.5 all-gather.28
  504.1 56.5 all-gather.26
  562.3 57.8 all-gather.32
  622.0 38.5 all-gather.30
  684.6 54.7 reduce-scatter.11
  741.5 56.0 reduce-scatter.9
  802.7 57.8 all-gather.34
  900.7 70.8 reduce-scatter.13
  978.9 57.8 all-gather.36
  1183.2 112.0 all-reduce.15
  1458.1 345.4 all-reduce.17
  1840.5 66.0 all-reduce.19
where the time goes:
time: 1940 us; the launch traced here: 1930 us
  waiting for transfers between devices  1080 us (56%)
  local copies, waits for them, and re-layouts  421 us (22%)
  matrix products  196 us (10%)
  blocking collectives  111 us (6%)
  other arithmetic  97.8 us (5%)
    unnamed x22, waiting for transfers between devices  392 us
    unnamed x386, local copies, waits for them, and re-layouts  147 us
    reduce_scatter x1, waiting for transfers between devices, on_device(): lax.psum_scatter(cross_packed.astype(jnp.bfloat16), 'tensor', scatter_dim...  70.7 us
    slice x8, local copies, waits for them, and re-layouts, sum_grads(): segment = summed[offset:offset + length]  64.3 us
    all_gather x1, waiting for transfers between devices, on_device(): lax.all_gather(attn_low, 'tensor', axis=0, tiled=True)  58.6 us
    all_gather x1, waiting for transfers between devices, on_device(): mlp_full = lax.all_gather(mlp_low, 'tensor', axis=0, tiled=True)  58.6 us
    all_gather x1, waiting for transfers between devices, on_device(): three_full = lax.all_gather(three_low, 'tensor', axis=0, tiled=True)  58 us
    reduce_scatter x1, waiting for transfers between devices, on_device(): lax.psum_scatter(jnp.dot(hidden_low, w_down, preferred_element_type=FLOAT...  55.4 us
  transfers between devices with their start and end apart: 20, of which 17 were waited for; matrix products, arithmetic and copies ran while one was open for 14% of the time, Pallas kernels for 0%

commit v1 on v0

v1 whole, which is shorter than its diff:
```python
import functools
import math

import jax
import jax.numpy as jnp
import numpy as np
from jax import lax
from jax.experimental import pallas as pl
from jax.experimental.pallas import tpu as pltpu
from jax.sharding import PartitionSpec as P

HEADS = 16
HD = 88
LANES = 128
EPSILON = 1e-06
HIGHEST = lax.Precision.HIGHEST
FLOAT = jnp.float32
BFLOAT = jnp.bfloat16
LOG2E = 1.4426950408889634
SCALE = 1.0 / math.sqrt(HD)


def layer_norm(values, norm_gain, norm_bias):
    centred = values - jnp.mean(values, axis=-1, keepdims=True)
    variance = jnp.mean(centred * centred, axis=-1, keepdims=True)
    return centred * lax.rsqrt(variance + EPSILON) * norm_gain + norm_bias


def head_norm(values, norm_gain):
    centred = values - jnp.mean(values, axis=-1, keepdims=True)
    variance = jnp.mean(centred * centred, axis=-1, keepdims=True)
    return centred * lax.rsqrt(variance + EPSILON) * norm_gain


def silu(values):
    return values / (1.0 + jnp.exp(-values))


def gelu(values):
    inner = math.sqrt(2.0 / math.pi) * (values + 0.044715 * values * values * values)
    return 0.5 * values * (1.0 + jnp.tanh(inner))


def dot(left, right, contract=((1,), (0,))):
    return lax.dot_general(left, right, (contract, ((), ())), preferred_element_type=FLOAT)


NT = ((1,), (1,))
TN = ((0,), (0,))


def rot(values, step):
    count = lax.axis_size("tensor")
    return lax.ppermute(values, "tensor", [(i, (i + step) % count) for i in range(count)])


def ring_gather(own):
    blocks = [own]
    for _ in range(lax.axis_size("tensor") - 1):
        blocks.append(rot(blocks[-1], 1))
    return blocks


def ring_scatter(parts):
    running = parts[1].astype(BFLOAT)
    for part in parts[2:]:
        running = (rot(running, 1).astype(FLOAT) + part.astype(FLOAT)).astype(BFLOAT)
    return rot(running, 1).astype(FLOAT) + parts[0].astype(FLOAT)


def exchange(parts):
    count = len(parts)
    return [parts[0]] + [rot(parts[count - r], r) for r in range(1, count)]


def after(values, *earlier):
    return lax.optimization_barrier((values, *earlier))[0]


def small_gather(own):
    have = own[None]
    me = lax.axis_index("dp")
    count = lax.axis_size("dp")
    step = 1
    while step < count:
        other = lax.ppermute(have, "dp", [(i, i ^ step) for i in range(count)])
        upper = (me // step) % 2 == 1
        have = jnp.where(upper, jnp.concatenate([other, have]), jnp.concatenate([have, other]))
        step *= 2
    return have


def tensor_sum(values):
    total = values
    for step in range(1, lax.axis_size("tensor")):
        total = total + rot(values, step)
    return total


def grad_kernel(*refs):
    left_ref, right_ref, out_ref, turned_ref = refs[0], refs[1], refs[-2], refs[-1]

    @pl.when(pl.program_id(0) == 0)
    def _():
        turned_ref[...] = left_ref[...].T

    out_ref[...] = dot(turned_ref[...], right_ref[...]).astype(BFLOAT)


def pack_grad(packed, left, right, lanes, start, tile):
    rows, height = left.shape
    wide = right.shape[1]
    first = start // tile
    in_specs = [
        pl.BlockSpec((rows, height), lambda i: (0, 0)),
        pl.BlockSpec((rows, tile), lambda i: (0, i)),
    ]
    operands = [left, right]
    if packed is not None:
        in_specs.append(pl.BlockSpec(memory_space=pl.ANY))
        operands.append(packed)
    return pl.pallas_call(
        grad_kernel,
        grid=(pl.cdiv(wide, tile),),
        in_specs=in_specs,
        out_specs=pl.BlockSpec((height, tile), lambda i: (0, first + i)),
        out_shape=jax.ShapeDtypeStruct((height, lanes), BFLOAT),
        scratch_shapes=[pltpu.VMEM((height, rows), BFLOAT)],
        input_output_aliases={} if packed is None else {2: 0},
        compiler_params=pltpu.CompilerParams(vmem_limit_bytes=40 * 2**20),
        cost_estimate=pl.CostEstimate(
            flops=2 * rows * height * wide, bytes_accessed=2 * (rows * height + rows * wide + height * wide), transcendentals=0
        ),
    )(*operands)


def padded(values):
    return jnp.concatenate([values, jnp.zeros((values.shape[0], LANES - HD), values.dtype)], axis=1)


def lane_mask(rows):
    lanes = lax.broadcasted_iota(jnp.int32, (rows, LANES), 1)
    return (lanes < HD).astype(FLOAT)


def norm_parts(values, mask):
    mean = jnp.sum(values, axis=-1, keepdims=True) * (1.0 / HD)
    centred = (values - mean) * mask
    variance = jnp.sum(centred * centred, axis=-1, keepdims=True) * (1.0 / HD)
    inverse = lax.rsqrt(variance + EPSILON)
    return centred * inverse, inverse


CHUNK = 128


def attend_forward_kernel(
    heads, block, raw_ref, cos_ref, sin_a_ref, sin_b_ref, gain_ref, o_ref, opad_ref, q_ref, k_ref, v_ref, lse_ref
):
    length = raw_ref.shape[0]
    span = heads * HD
    mask = lane_mask(CHUNK)

    def prepare(index, carry):
        rows = pl.ds(pl.multiple_of(index * CHUNK, CHUNK), CHUNK)
        cosine, sine_a, sine_b = cos_ref[rows, :], sin_a_ref[rows, :], sin_b_ref[rows, :]
        for head in range(heads):
            for part, out_ref in ((0, q_ref), (1, k_ref)):
                start = part * span + head * HD
                values = padded(raw_ref[rows, start : start + HD])
                normed, _ = norm_parts(values, mask)
                turned = normed * gain_ref[part * heads + head, :][None, :]
                turned = (
                    turned * cosine
                    + pltpu.roll(turned, LANES - HD // 4, 1) * sine_a
                    + pltpu.roll(turned, HD // 4, 1) * sine_b
                )
                out_ref[head, rows, :] = turned.astype(BFLOAT)
            start = 2 * span + head * HD
            v_ref[head, rows, :] = padded(raw_ref[rows, start : start + HD]).astype(BFLOAT)
        return carry

    lax.fori_loop(0, length // CHUNK, prepare, 0)
    count = length // block

    def attend(index, carry):
        head = lax.div(index, count)
        rows = pl.ds(pl.multiple_of(lax.rem(index, count) * block, block), block)
        scores = dot(k_ref[head], q_ref[head, rows, :], NT)
        peak = jnp.max(scores, axis=0, keepdims=True)
        powers = jnp.exp2((scores - peak) * (SCALE * LOG2E))
        total = jnp.sum(powers, axis=0, keepdims=True)
        mixed = dot(v_ref[head], powers.astype(BFLOAT), TN) / total
        opad_ref[head, rows, :] = jnp.transpose(mixed).astype(BFLOAT)
        lse_ref[index] = peak * (SCALE * LOG2E) + jnp.log2(total)
        return carry

    lax.fori_loop(0, heads * count, attend, 0)

    def finish(index, carry):
        rows = pl.ds(pl.multiple_of(index * CHUNK, CHUNK), CHUNK)
        o_ref[rows, :] = jnp.concatenate(
            [opad_ref[head, rows, :].astype(FLOAT)[:, :HD] for head in range(heads)], axis=1
        ).astype(BFLOAT)
        return carry

    lax.fori_loop(0, length // CHUNK, finish, 0)


def attend_forward(raw, tables, gains, heads, block):
    length = raw.shape[0]
    head_shape = jax.ShapeDtypeStruct((heads, length, LANES), BFLOAT)
    return pl.pallas_call(
        functools.partial(attend_forward_kernel, heads, block),
        out_shape=(
            jax.ShapeDtypeStruct((length, heads * HD), BFLOAT),
            head_shape,
            head_shape,
            head_shape,
            head_shape,
            jax.ShapeDtypeStruct((heads * (length // block), 1, block), FLOAT),
        ),
        compiler_params=pltpu.CompilerParams(vmem_limit_bytes=56 * 2**20),
        cost_estimate=pl.CostEstimate(flops=4_000_000_000, bytes_accessed=12_000_000, transcendentals=4_200_000),
    )(raw, *tables, gains)


def attend_backward_kernel(
    heads, block, raw_ref, cos_ref, sin_a_ref, sin_b_ref, gain_ref, opad_ref, q_ref, k_ref, v_ref, lse_ref, do_ref,
    graw_ref, gain_out_ref, sums_ref, dpad_ref, dq_ref, dk_ref, dv_ref,
):
    length = raw_ref.shape[0]
    span = heads * HD
    mask = lane_mask(CHUNK)
    count = length // block

    def prepare(index, carry):
        rows = pl.ds(pl.multiple_of(index * CHUNK, CHUNK), CHUNK)
        values = do_ref[rows, :].astype(FLOAT)
        for head in range(heads):
            dpad_ref[head, rows, :] = padded(values[:, head * HD : (head + 1) * HD]).astype(BFLOAT)
        return carry

    lax.fori_loop(0, length // CHUNK, prepare, 0)

    def attend(index, carry):
        head = lax.div(index, count)
        rows = pl.ds(pl.multiple_of(lax.rem(index, count) * block, block), block)
        queries = q_ref[head, rows, :]
        grad = dpad_ref[head, rows, :]
        scores = dot(k_ref[head], queries, NT)
        probs = jnp.exp2(scores * (SCALE * LOG2E) - lse_ref[index])
        grad_probs = dot(v_ref[head], grad, NT)
        inner = jnp.transpose(grad.astype(FLOAT) * opad_ref[head, rows, :].astype(FLOAT))
        inner = jnp.sum(inner, axis=0, keepdims=True)
        grad_scores = (probs * (grad_probs - inner)).astype(BFLOAT)
        add_v = dot(probs.astype(BFLOAT), grad)
        add_k = dot(grad_scores, queries)
        dq_ref[head, rows, :] = jnp.transpose(dot(k_ref[head], grad_scores, TN))

        @pl.when(lax.rem(index, count) == 0)
        def _():
            dv_ref[head] = add_v
            dk_ref[head] = add_k

        @pl.when(lax.rem(index, count) != 0)
        def _():
            dv_ref[head] += add_v
            dk_ref[head] += add_k

        return carry

    lax.fori_loop(0, heads * count, attend, 0)
    gain_out_ref[...] = jnp.zeros_like(gain_out_ref)
    sums_ref[...] = jnp.zeros_like(sums_ref)

    def finish(index, carry):
        rows = pl.ds(pl.multiple_of(index * CHUNK, CHUNK), CHUNK)
        cosine, sine_a, sine_b = cos_ref[rows, :], sin_a_ref[rows, :], sin_b_ref[rows, :]
        for part, grad_ref in ((0, dq_ref), (1, dk_ref)):
            pieces = []
            for head in range(heads):
                start = part * span + head * HD
                normed, inverse = norm_parts(padded(raw_ref[rows, start : start + HD]), mask)
                grad = grad_ref[head, rows, :] * SCALE
                grad = (
                    grad * cosine
                    + pltpu.roll(grad * sine_a, HD // 4, 1)
                    + pltpu.roll(grad * sine_b, LANES - HD // 4, 1)
                )
                slot = part * heads + head
                gain_out_ref[slot : slot + 1, :] += jnp.sum(grad * normed, axis=0, keepdims=True)
                grad = grad * gain_ref[slot, :][None, :]
                mean = jnp.sum(grad, axis=-1, keepdims=True) * (1.0 / HD)
                slope = jnp.sum(grad * normed, axis=-1, keepdims=True) * (1.0 / HD)
                pieces.append((inverse * (grad - mean - normed * slope))[:, :HD])
            low = jnp.concatenate(pieces, axis=1).astype(BFLOAT)
            graw_ref[rows, part * span : (part + 1) * span] = low
            sums_ref[part : part + 1, :] += jnp.sum(low.astype(FLOAT), axis=0, keepdims=True)
        low = jnp.concatenate([dv_ref[head, rows, :][:, :HD] for head in range(heads)], axis=1).astype(BFLOAT)
        graw_ref[rows, 2 * span :] = low
        sums_ref[2:3, :] += jnp.sum(low.astype(FLOAT), axis=0, keepdims=True)
        return carry

    lax.fori_loop(0, length // CHUNK, finish, 0)


def attend_backward(raw, tables, gains, kept, grad_out, heads, block):
    length = raw.shape[0]
    return pl.pallas_call(
        functools.partial(attend_backward_kernel, heads, block),
        out_shape=(
            jax.ShapeDtypeStruct((length, 3 * heads * HD), BFLOAT),
            jax.ShapeDtypeStruct((2 * heads, LANES), FLOAT),
            jax.ShapeDtypeStruct((8, heads * HD), FLOAT),
        ),
        scratch_shapes=[
            pltpu.VMEM((heads, length, LANES), BFLOAT),
            pltpu.VMEM((heads, length, LANES), FLOAT),
            pltpu.VMEM((heads, length, LANES), FLOAT),
            pltpu.VMEM((heads, length, LANES), FLOAT),
        ],
        compiler_params=pltpu.CompilerParams(vmem_limit_bytes=56 * 2**20),
        cost_estimate=pl.CostEstimate(flops=10_000_000_000, bytes_accessed=16_000_000, transcendentals=4_200_000),
    )(raw, *tables, gains, *kept, grad_out)


def cross_forward(queries, keys, values_in):
    scores = jnp.einsum("qhd,khd->hqk", queries, keys, preferred_element_type=FLOAT) * SCALE
    peak = jnp.max(scores, axis=-1, keepdims=True)
    powers = jnp.exp(scores - peak)
    totals = jnp.sum(powers, axis=-1, keepdims=True)
    weights = (powers / totals).astype(BFLOAT)
    mixed = jnp.einsum("hqk,khd->qhd", weights, values_in, preferred_element_type=FLOAT)
    return mixed.astype(BFLOAT), peak + jnp.log(totals)


def cross_backward(queries, keys, values_in, log_sums, grad):
    scores = jnp.einsum("qhd,khd->hqk", queries, keys, preferred_element_type=FLOAT) * SCALE
    probs = jnp.exp(scores - log_sums)
    grad_probs = jnp.einsum("qhd,khd->hqk", grad, values_in, preferred_element_type=FLOAT)
    inner = jnp.sum(probs * grad_probs, axis=-1, keepdims=True)
    grad_scores = (probs * (grad_probs - inner)).astype(BFLOAT)
    grad_q = jnp.einsum("hqk,khd->qhd", grad_scores, keys, preferred_element_type=FLOAT) * SCALE
    grad_k = jnp.einsum("hqk,qhd->khd", grad_scores, queries, preferred_element_type=FLOAT) * SCALE
    grad_v = jnp.einsum("hqk,qhd->khd", probs.astype(BFLOAT), grad, preferred_element_type=FLOAT)
    return grad_q, grad_k, grad_v


def on_device(
    latent, skip_in, text_tokens, time_embed, t_index, grid_pos, skip_weight, mod_weight, vectors, up_bias,
    qkv_weight, proj_weight, query_weight, text_weight, cross_weight, up_weight, down_weight, out_grad,
):
    split = lax.axis_size("tensor")
    shards = lax.axis_size("dp")
    place = lax.axis_index("tensor")
    me = lax.axis_index("dp")
    own_rows, width = latent.shape
    own_text = text_tokens.shape[0]
    part = mod_weight.shape[0]
    heads = HEADS // split
    span = heads * HD
    hidden = up_weight.shape[1]
    rows_ahead = vectors.shape[0]

    def others(r):
        return lax.rem(place - r + split, split)

    condition = time_embed
    half = width // 2
    frequencies = jnp.exp(-math.log(10000.0) * jnp.arange(half, dtype=FLOAT) / half)
    angles = t_index.astype(FLOAT)[:, None] * frequencies[None, :]
    condition = time_embed + jnp.concatenate([jnp.cos(angles), jnp.sin(angles)], axis=-1)
    silu_low = silu(condition).astype(BFLOAT)
    small = jnp.concatenate([vectors.reshape(-1), up_bias, silu_low.reshape(-1)])
    small_all = small_gather(small)
    cut_one, cut_two = rows_ahead * part, rows_ahead * part + up_bias.shape[0]
    table = (
        small_all[:, :cut_one].reshape(shards, rows_ahead, part).transpose(1, 0, 2).reshape(rows_ahead, width)
    ).astype(FLOAT)
    bias_all = small_all[:, cut_one:cut_two].reshape(-1).astype(FLOAT)
    silu_all = small_all[:, cut_two:]

    packed_one = jnp.concatenate(
        [
            skip_weight[:part],
            skip_weight[part:],
            qkv_weight.reshape(part, 3 * span),
            text_weight.reshape(part, 2 * span),
        ],
        axis=1,
    )
    all_one = lax.all_gather(packed_one, "dp", axis=0, tiled=True)
    w_skip = all_one[:, : 2 * width]
    w_qkv = all_one[:, 2 * width : 2 * width + 3 * span]
    w_text = all_one[:, 2 * width + 3 * span :]

    own_full = jnp.stack([proj_weight.T, query_weight, cross_weight.T])
    full_blocks = ring_gather(own_full)
    packed_two = jnp.concatenate(
        [full_blocks[r][index] for index in range(3) for r in range(split)], axis=1
    )
    all_two = lax.all_gather(packed_two, "dp", axis=0, tiled=True)
    w_proj_t, w_query, w_cross_t = (all_two[:, i * width : (i + 1) * width] for i in range(3))

    packed_three = jnp.concatenate([up_weight, down_weight.T], axis=1)
    all_three = lax.all_gather(packed_three, "dp", axis=0, tiled=True)
    w_up, w_down_t = all_three[:, :hidden], all_three[:, hidden:]

    text_blocks = ring_gather(text_tokens)
    cot_blocks = ring_gather(out_grad)
    text_full = jnp.concatenate(text_blocks, axis=0)
    cot_full = jnp.concatenate(cot_blocks, axis=0)

    def head_slice(index):
        return lax.dynamic_slice_in_dim(table[index], place * span, span, 0)

    def relative(index):
        return jnp.concatenate(
            [lax.dynamic_slice_in_dim(table[index], others(r) * span, span, 0) for r in range(split)]
        )

    def spread(values):
        return lax.dynamic_update_slice_in_dim(jnp.zeros((width,), FLOAT), values.reshape(-1), place * span, 0)

    def absolute(values):
        result = jnp.zeros((width,), FLOAT)
        for r in range(split):
            result = lax.dynamic_update_slice_in_dim(
                result, values.reshape(-1)[r * span : (r + 1) * span], others(r) * span, 0
            )
        return result

    def padded_gains(index):
        return jnp.pad(head_slice(index).reshape(heads, HD), ((0, 0), (0, LANES - HD)))

    quarter = HD // 4
    lane = np.arange(LANES)
    rate = np.where(lane < HD, 10000.0 ** (-(lane % quarter).astype(np.float64) / quarter), 0.0).astype(np.float32)
    by_row = (lane < HD // 2)[None, :]
    first = ((lane % (HD // 2)) < quarter) & (lane < HD)
    second = ((lane % (HD // 2)) >= quarter) & (lane < HD)
    grid_rel = jnp.concatenate(
        [lax.dynamic_slice_in_dim(grid_pos, others(r) * own_rows, own_rows, 1) for r in range(split)], axis=1
    ).astype(FLOAT)
    turn = jnp.where(by_row, grid_rel[0][:, None], grid_rel[1][:, None]) * rate[None, :]
    cosine, sine = jnp.cos(turn), jnp.sin(turn)
    tables = (
        cosine * (lane < HD).astype(np.float32)[None, :],
        -sine * first.astype(np.float32)[None, :],
        sine * second.astype(np.float32)[None, :],
    )

    silu_mine = lax.dynamic_slice_in_dim(silu_all, me * part, part, 1)
    shift_terms = dot(silu_mine, mod_weight)
    shift = jnp.sum(lax.all_to_all(shift_terms, "dp", 0, 0, tiled=True), axis=0, keepdims=True) + table[5]

    joined = jnp.concatenate([latent.astype(FLOAT), skip_in.astype(FLOAT)], axis=-1)
    joined_gain = jnp.concatenate([table[0], table[1]])
    joined_bias = jnp.concatenate([table[2], table[3]])
    normed_low = layer_norm(joined, joined_gain, joined_bias).astype(BFLOAT)
    normed_perm = normed_low.reshape(own_rows, shards, 2, part).transpose(0, 2, 1, 3).reshape(own_rows, 2 * width)
    stream_one = (
        dot(normed_perm[:, :width], w_skip[:, :width]) + dot(normed_perm[:, width:], w_skip[:, width:]) + table[4]
    )
    attn_low = (layer_norm(stream_one, table[6], table[7]) + shift).astype(BFLOAT)
    attn_low = after(attn_low, text_blocks[-1], cot_blocks[-1], full_blocks[-1])
    attn_blocks = ring_gather(attn_low)
    qkv_bias = jnp.concatenate([head_slice(8), head_slice(9), head_slice(10)])
    raw = jnp.concatenate([dot(block, w_qkv) + qkv_bias for block in attn_blocks], axis=0)
    gains = jnp.concatenate([padded_gains(12), padded_gains(13)], axis=0)
    length = raw.shape[0]
    block = min(512, length)
    mixed, *kept = attend_forward(raw, tables, gains, heads, block)

    def blocks_of(values, rows):
        return [values[r * rows : (r + 1) * rows] for r in range(split)]

    mixed_own = jnp.concatenate(exchange(blocks_of(mixed, own_rows)), axis=1)

    text_raw = dot(text_full, w_text) + jnp.concatenate([head_slice(17), head_slice(18)])
    text_length = text_raw.shape[0]
    gain_21 = head_slice(21).reshape(heads, HD)
    raw_key = text_raw[:, :span].reshape(text_length, heads, HD)
    text_low = jnp.concatenate(
        [head_norm(raw_key, gain_21).reshape(text_length, span), text_raw[:, span:]], axis=1
    ).astype(BFLOAT)
    text_rel = ring_gather(after(text_low, attn_blocks[-1]))
    text_keys = jnp.concatenate([item[:, :span] for item in text_rel], axis=1).reshape(text_length, HEADS, HD)
    text_values = jnp.concatenate([item[:, span:] for item in text_rel], axis=1).reshape(text_length, HEADS, HD)

    stream_two = stream_one + dot(mixed_own, w_proj_t, NT) + table[11]
    cross_low = layer_norm(stream_two, table[14], table[15]).astype(BFLOAT)
    cross_raw = (dot(cross_low, w_query) + relative(16)).reshape(own_rows, HEADS, HD)
    gain_20 = relative(20).reshape(HEADS, HD)
    cross_queries = head_norm(cross_raw, gain_20).astype(BFLOAT)
    cross_mixed, cross_logs = cross_forward(cross_queries, text_keys, text_values)
    cross_mixed = cross_mixed.reshape(own_rows, width)
    stream_three = stream_two + dot(cross_mixed, w_cross_t, NT) + table[19]
    mlp_low = layer_norm(stream_three, table[22], table[23]).astype(BFLOAT)
    mlp_blocks = ring_gather(mlp_low)
    hidden_bias = lax.dynamic_slice_in_dim(bias_all, place * hidden, hidden, 0)

    hidden_lows, pre_lows, out_parts, back_parts = [], [], [], []
    for r in range(split):
        hidden_pre = dot(mlp_blocks[r], w_up) + hidden_bias
        activated, pull = jax.vjp(gelu, hidden_pre)
        hidden_lows.append(activated.astype(BFLOAT))
        pre_lows.append(pull(dot(cot_blocks[r], w_down_t))[0].astype(BFLOAT))
        back_parts.append(dot(pre_lows[r], w_up, NT))
        out_parts.append(dot(hidden_lows[r], w_down_t, NT))
    grad_mlp_in = ring_scatter(back_parts)

    rows_grad = {}
    mlp_full = jnp.concatenate(mlp_blocks, axis=0)
    pre_full = jnp.concatenate(pre_lows, axis=0)
    hidden_full = jnp.concatenate(hidden_lows, axis=0)
    grad_bias = jnp.sum(pre_full, axis=0, dtype=FLOAT)
    grads_one = pack_grad(None, mlp_full, pre_full, 2 * hidden, 0, 512)
    grads_one = pack_grad(grads_one, cot_full, hidden_full, 2 * hidden, hidden, 512)
    summed_one = lax.psum_scatter(grads_one, "dp", scatter_dimension=0, tiled=True).astype(FLOAT)

    cot_here = out_grad.astype(FLOAT)
    rows_grad[24] = jnp.sum(cot_here, axis=0)
    into_three, rows_grad[22], rows_grad[23] = jax.vjp(layer_norm, stream_three, table[22], table[23])[1](grad_mlp_in)
    grad_three = cot_here + into_three
    three_low = grad_three.astype(BFLOAT)
    rows_grad[19] = jnp.sum(grad_three, axis=0)
    grad_cross_mixed = dot(three_low, w_cross_t).astype(BFLOAT).reshape(own_rows, HEADS, HD)
    grad_cq, grad_ck, grad_cv = cross_backward(cross_queries, text_keys, text_values, cross_logs, grad_cross_mixed)
    into_cq, gain_cq = jax.vjp(head_norm, cross_raw, gain_20)[1](grad_cq)
    rows_grad[20] = absolute(gain_cq)
    cq_low = into_cq.reshape(own_rows, width).astype(BFLOAT)
    rows_grad[16] = absolute(jnp.sum(cq_low, axis=0, dtype=FLOAT))
    grad_cross_in = dot(cq_low, w_query, NT)
    into_two, rows_grad[14], rows_grad[15] = jax.vjp(layer_norm, stream_two, table[14], table[15])[1](grad_cross_in)
    grad_two = grad_three + into_two
    two_low = grad_two.astype(BFLOAT)
    rows_grad[11] = jnp.sum(grad_two, axis=0)
    grad_mixed = dot(two_low, w_proj_t).astype(BFLOAT)
    grad_mixed_blocks = exchange([grad_mixed[:, r * span : (r + 1) * span] for r in range(split)])
    out_parts[1] = after(out_parts[1].astype(BFLOAT), grad_mixed_blocks[-1])
    block_out = (stream_three + ring_scatter(out_parts) + table[24]).astype(BFLOAT)

    grad_ck = grad_ck.reshape(text_length, width)
    grad_cv = grad_cv.reshape(text_length, width)
    text_terms = [
        jnp.concatenate([grad_ck[:, r * span : (r + 1) * span], grad_cv[:, r * span : (r + 1) * span]], axis=1)
        for r in range(split)
    ]
    text_terms[1] = after(text_terms[1].astype(BFLOAT), grad_mixed_blocks[-1])
    text_sum = ring_scatter(text_terms)
    into_ck, gain_ck = jax.vjp(head_norm, raw_key, gain_21)[1](text_sum[:, :span].reshape(text_length, heads, HD))
    rows_grad[21] = spread(gain_ck)
    ckv_low = jnp.concatenate([into_ck.reshape(text_length, span), text_sum[:, span:]], axis=1).astype(BFLOAT)
    ckv_sums = jnp.sum(ckv_low, axis=0, dtype=FLOAT)
    rows_grad[17], rows_grad[18] = spread(ckv_sums[:span]), spread(ckv_sums[span:])
    text_grad = ring_scatter(blocks_of(dot(ckv_low, w_text, NT), own_text))

    lanes_two = 3 * width + pl.cdiv(2 * span, LANES) * LANES
    grads_two = pack_grad(None, two_low, mixed_own, lanes_two, 0, width)
    grads_two = pack_grad(grads_two, cross_low, cq_low, lanes_two, width, width)
    grads_two = pack_grad(grads_two, three_low, cross_mixed, lanes_two, 2 * width, width)
    grads_two = pack_grad(grads_two, text_full, ckv_low, lanes_two, 3 * width, LANES)
    summed_two = lax.psum_scatter(grads_two, "dp", scatter_dimension=0, tiled=True)
    full_sum = ring_scatter(
        [
            jnp.concatenate(
                [summed_two[:, i * width + r * span : i * width + (r + 1) * span] for i in range(3)], axis=1
            )
            for r in range(split)
        ]
    )

    grad_raw, gain_grads, raw_sums = attend_backward(
        raw, tables, gains, kept, jnp.concatenate(grad_mixed_blocks, axis=0), heads, block
    )
    rows_grad[12] = spread(gain_grads[:heads, :HD])
    rows_grad[13] = spread(gain_grads[heads:, :HD])
    rows_grad[8], rows_grad[9], rows_grad[10] = spread(raw_sums[0]), spread(raw_sums[1]), spread(raw_sums[2])
    raw_blocks = blocks_of(grad_raw, own_rows)
    attn_parts = [dot(item, w_qkv, NT) for item in raw_blocks]
    shift_part = sum(jnp.sum(item, axis=0) for item in attn_parts)
    rows_grad[5] = shift_part
    grad_attn_in = ring_scatter(attn_parts)
    shift_grads = small_gather(tensor_sum(shift_part))
    mod_grad = lax.dot_general(
        silu_mine.astype(FLOAT), shift_grads, ((TN), ((), ())), precision=HIGHEST, preferred_element_type=FLOAT
    )
    into_silu = lax.dot_general(
        shift_grads, mod_weight.astype(FLOAT), ((NT), ((), ())), precision=HIGHEST, preferred_element_type=FLOAT
    )
    into_silu = lax.all_to_all(into_silu, "dp", 0, 0, tiled=True).reshape(1, width)
    time_full = jax.vjp(silu, condition)[1](into_silu)[0]
    time_grad = lax.dynamic_slice_in_dim(time_full, place * (width // split), width // split, 1)

    into_one, rows_grad[6], rows_grad[7] = jax.vjp(layer_norm, stream_one, table[6], table[7])[1](grad_attn_in)
    grad_one = grad_two + into_one
    rows_grad[4] = jnp.sum(grad_one, axis=0)
    one_low = grad_one.astype(BFLOAT)
    grad_joined = jnp.concatenate([dot(one_low, w_skip[:, :width], NT), dot(one_low, w_skip[:, width:], NT)], axis=1)
    grad_joined = grad_joined.reshape(own_rows, 2, shards, part).transpose(0, 2, 1, 3).reshape(own_rows, 2 * width)
    into_joined, gain_joined, bias_joined = jax.vjp(layer_norm, joined, joined_gain, joined_bias)[1](grad_joined)
    rows_grad[0], rows_grad[1] = gain_joined[:width], gain_joined[width:]
    rows_grad[2], rows_grad[3] = bias_joined[:width], bias_joined[width:]

    bias_spread = lax.dynamic_update_slice_in_dim(jnp.zeros(bias_all.shape, FLOAT), grad_bias, place * hidden, 0)
    bias_part = up_bias.shape[0]
    bias_cols = pl.cdiv(bias_part, part)
    table_grad = jnp.stack([rows_grad[index] for index in range(rows_ahead)], axis=1)
    bias_grad = jnp.pad(bias_spread.reshape(shards, bias_part), ((0, 0), (0, bias_cols * part - bias_part)))
    bias_grad = bias_grad.reshape(shards, bias_cols, part).transpose(0, 2, 1).reshape(width, bias_cols)
    small_grads = jnp.concatenate([table_grad, bias_grad], axis=1).astype(BFLOAT)
    small_grads = jnp.pad(small_grads, ((0, 0), (0, LANES - small_grads.shape[1])))

    qkv_lanes = pl.cdiv(3 * span, LANES) * LANES
    lanes_three = 2 * width + LANES + qkv_lanes
    grads_three = pack_grad(None, jnp.concatenate(attn_blocks, axis=0), grad_raw, lanes_three, 2 * width + LANES, LANES)
    grads_three = pack_grad(grads_three, normed_perm[:, :width], one_low, lanes_three, 0, width)
    grads_three = pack_grad(grads_three, normed_perm[:, width:], one_low, lanes_three, width, width)
    grads_three = lax.dynamic_update_slice(grads_three, small_grads, (0, 2 * width))
    summed_three = lax.psum_scatter(grads_three, "dp", scatter_dimension=0, tiled=True)
    shared = 2 * width + LANES
    chunk = shared // split
    shared_terms = [lax.dynamic_slice_in_dim(summed_three, others(r) * chunk, chunk, 1) for r in range(split)]
    shared_blocks = ring_gather(ring_scatter(shared_terms).astype(BFLOAT))
    shared_sum = jnp.zeros((part, shared), FLOAT)
    for r in range(split):
        shared_sum = lax.dynamic_update_slice_in_dim(shared_sum, shared_blocks[r].astype(FLOAT), others(r) * chunk, 1)
    skip_weight_grad = jnp.concatenate([shared_sum[:, :width], shared_sum[:, width : 2 * width]], axis=0)
    vectors_grad = shared_sum[:, 2 * width : 2 * width + rows_ahead].T
    bias_grad = shared_sum[:, 2 * width + rows_ahead : 2 * width + rows_ahead + bias_cols].T.reshape(-1)[:bias_part]
    qkv_sum = summed_three[:, shared : shared + 3 * span].astype(FLOAT).reshape(part, 3, span)

    text_sum_grad = summed_two[:, 3 * width : 3 * width + 2 * span].astype(FLOAT).reshape(part, 2, span)
    return (
        block_out,
        into_joined[:, :width],
        into_joined[:, width:],
        text_grad,
        time_grad,
        skip_weight_grad,
        mod_grad,
        vectors_grad,
        bias_grad,
        qkv_sum,
        full_sum[:, :span].T,
        full_sum[:, span : 2 * span],
        text_sum_grad,
        full_sum[:, 2 * span :].T,
        summed_one[:, :hidden],
        summed_one[:, hidden:].T,
    )


def solution(mesh):
    tokens = P(("dp", "tensor"), None)
    placed = (
        tokens,
        tokens,
        tokens,
        P("dp", None),
        P("dp"),
        P(None, "dp"),
        P("dp", None),
        P("dp", None),
        P(None, "dp"),
        P("dp"),
        P("dp", None, "tensor"),
        P("tensor", "dp"),
        P("dp", "tensor"),
        P("dp", None, "tensor"),
        P("tensor", "dp"),
        P("dp", "tensor"),
        P("tensor", "dp"),
        tokens,
    )
    return jax.shard_map(
        on_device,
        mesh=mesh,
        in_specs=placed,
        out_specs=(
            tokens,
            tokens,
            tokens,
            tokens,
            P("dp", "tensor"),
            P("dp", None),
            P("dp", None),
            P(None, "dp"),
            P("dp"),
            P("dp", None, "tensor"),
            P("tensor", "dp"),
            P("dp", "tensor"),
            P("dp", None, "tensor"),
            P("tensor", "dp"),
            P("dp", "tensor"),
            P("tensor", "dp"),
        ),
        check_vma=False,
    )
```

time: 1940 us -> 999 us (0.51)
  waiting for transfers between devices: 1080 us -> 307 us
  local copies, waits for them, and re-layouts: 421 us -> 158 us
  starting transfers between devices: 0.99 us -> 144 us
  Pallas kernels: 0 us -> 120 us
  blocking collectives: 111 us -> 0 us
  matrix products: 196 us -> 146 us
    all_gather x12 -> x3, waiting for transfers between devices: 409 us -> 0.04 us  [the longest x1 0.02 us: on_device(): all_two = lax.all_gather(packed_two, 'dp', axis=0, tiled=True)]
    unnamed x22 -> x6, waiting for transfers between devices: 392 us -> 0.1 us
    ppermute x0 -> x57, waiting for transfers between devices: none -> 211 us  [the longest x51 207 us: rot(): lax.ppermute(values, 'tensor', [(i, (i + step) % count) for i in range(co...]
    reduce_scatter x5 -> x3, waiting for transfers between devices: 279 us -> 93.7 us  [the longest x1 74 us: on_device(): lax.psum_scatter(grads_two, 'dp', scatter_dimension=0, tiled=True)]
    ppermute x0 -> x57, starting transfers between devices: none -> 137 us  [the longest x51 135 us: rot(): lax.ppermute(values, 'tensor', [(i, (i + step) % count) for i in range(co...]
    pallas_call x0 -> x11, Pallas kernels: none -> 120 us  [the longest x9 46.5 us: pack_grad(): pl.pallas_call(grad_kernel, grid=(pl.cdiv(wide, tile),), in_specs=in_spec...]
    unnamed x386 -> x375, local copies, waits for them, and re-layouts: 147 us -> 49 us
    all_gather x6 -> x0, blocking collectives: 93.7 us -> none  [the longest x1 29.2 us: on_device(): lax.all_gather(text_tokens, 'tensor', axis=0, tiled=True)]
  transfers between devices with their start and end apart: 20 -> 65, of which waited for: 17 -> 38; matrix products, arithmetic and copies ran while one was open for 14% -> 29% of each run, Pallas kernels for 0% -> 12%
where the time goes in v1:
time: 999 us; the launch traced here: 982 us
  waiting for transfers between devices  307 us (31%)
  local copies, waits for them, and re-layouts  158 us (16%)
  matrix products  146 us (15%)
  starting transfers between devices  144 us (14%)
  Pallas kernels  120 us (12%)
  other arithmetic  88.3 us (9%)
  between operations  18.7 us (2%)
    ppermute x51, waiting for transfers between devices, rot(): lax.ppermute(values, 'tensor', [(i, (i + step) % count) for i in range(co...  207 us
    ppermute x51, starting transfers between devices, rot(): lax.ppermute(values, 'tensor', [(i, (i + step) % count) for i in range(co...  135 us
    dot_general x37, matrix products, dot(): lax.dot_general(left, right, (contract, ((), ())), preferred_element_type...  130 us
    reduce_scatter x1, waiting for transfers between devices, on_device(): lax.psum_scatter(grads_two, 'dp', scatter_dimension=0, tiled=True)  74 us
    unnamed x375, local copies, waits for them, and re-layouts  49 us
    pallas_call x9, Pallas kernels, pack_grad(): pl.pallas_call(grad_kernel, grid=(pl.cdiv(wide, tile),), in_specs=in_spec...  46.5 us
    pallas_call x1, Pallas kernels, attend_backward(): pl.pallas_call(functools.partial(attend_backward_kernel, heads, block), o...  41.7 us
    pallas_call x1, Pallas kernels, attend_forward(): pl.pallas_call(functools.partial(attend_forward_kernel, heads, block), ou...  32.2 us
  transfers between devices with their start and end apart: 65, of which 38 were waited for; matrix products, arithmetic and copies ran while one was open for 29% of the time, Pallas kernels for 12%

profile of v1, /device:TPU:24, one launch (start us, length us, event | category | flops | bytes accessed | tf_op | source)
XLA Modules:
  0.0 982.1 jit_solution(12331278331289845014)
XLA Ops:
  12.9 11.1 %collective-permute-done.9 = bf16[3,176,352]{2,1,0:T(8,128)(2,1)S(1)} collective-permute-done((bf16[3,176,352]{2,1,0:T(8,128)(2,1)S(1)}, bf16[3,176,352]{2,1,0:T(8,128)(2,1)S(1)}, u32[]{:S(2)}, u32[]{:S(2)}) %collective-permute-start.9) | collective-permute-done | bytes 371744 | tf_op jit(solution)/shard_map/ppermute | solution.py:54
  26.1 8.2 collective-permute-done.10
  38.6 7.1 collective-permute-done.11
  101.4 21.9 %collective-permute-done.4 = bf16[80,1408]{1,0:T(8,128)(2,1)S(1)} collective-permute-done((bf16[80,1408]{1,0:T(8,128)(2,1)}, bf16[80,1408]{1,0:T(8,128)(2,1)S(1)}, u32[]{:S(2)}, u32[]{:S(2)}) %collective-permute-start.4) | collective-permute-done | bytes 225312 | tf_op jit(solution)/shard_map/ppermute | solution.py:54
  142.5 6.2 collective-permute-done.8
  174.9 8.6 collective-permute-done.13
  205.3 32.2 %shard_map.342 = (bf16[1024,352]{1,0:T(8,128)(2,1)}, bf16[4,1024,128]{2,1,0:T(8,128)(2,1)}, bf16[4,1024,128]{2,1,0:T(8,128)(2,1)}, bf16[4,1024,128]{2,1,0:T(8,12...) custom-call(f32[1024,1056]{1,0:T(8,128)} %pad_maximum_fusion.raw_ref, ...), custom_call_target="tpu_custom_call" | custom-call | flops 4000000000 | bytes 12000000 | tf_op jit(solution)/shard_map/pallas_call | solution.py:213
  251.0 7.0 collective-permute-done.16
  271.5 9.0 collective-permute-start.19
  280.7 16.1 %collective-permute-done.19 = bf16[320,704]{1,0:T(8,128)(2,1)S(1)} collective-permute-done((bf16[320,704]{1,0:T(8,128)(2,1)}, bf16[320,704]{1,0:T(8,128)(2,1)S(1)}, u32[]{:S(2)}, u32[]{:S(2)}) %collective-permute-start.19) | collective-permute-done | bytes 450592 | tf_op jit(solution)/shard_map/ppermute | solution.py:54
  339.2 10.1 %collective-permute-done.21 = bf16[256,1408]{1,0:T(8,128)(2,1)} collective-permute-done((bf16[256,1408]{1,0:T(8,128)(2,1)}, bf16[256,1408]{1,0:T(8,128)(2,1)}, u32[]{:S(2)}, u32[]{:S(2)}) %collective-permute-start.21) | collective-permute-done | bytes 720928 | tf_op jit(solution)/shard_map/ppermute | solution.py:54
  362.7 7.9 collective-permute-done.23
  403.6 7.3 collective-permute-done.24
  504.0 41.7 %shard_map.343 = (bf16[1024,1056]{1,0:T(8,128)(2,1)}, f32[8,128]{1,0:T(8,128)}, f32[8,352]{1,0:T(8,128)}) custom-call(f32[1024,1056]{1,0:T(8,128)} %pad_maximum_fusion.raw_ref, f32[1024,128]{1,0:T(8,128)} %get-tuple-element.258.cos_ref, f32[1024,128]{1,0:T(8,128)} %get-tuple-element.257.sin_a_ref, f32[1024,128]{1,0:T(8,128)} %get-tuple-element.256.sin_b_ref, ...), custom_call_target="tpu_custom_call" | custom-call | flops 10000000000 | bytes 16000000 | tf_op jit(solution)/shard_map/pallas_call | solution.py:310
  554.5 10.6 %shard_map.344.refs_2_ = bf16[1408,4096]{1,0:T(8,128)(2,1)} custom-call(bf16[1024,1408]{1,0:T(8,128)(2,1)S(1)} %pad_maximum_fusion.4.refs_0_, bf16[1024,1056]{1,0:T(8,128)(2,1)S(1)} %copy-done.12), custom_call_target="tpu_custom_call" | custom-call | flops 3045064704 | bytes 8019968 | tf_op jit(solution)/shard_map/pallas_call | solution.py:122
  565.9 14.2 %collective-permute-done.37 = bf16[320,704]{1,0:T(8,128)(2,1)S(1)} collective-permute-done((bf16[320,704]{1,0:T(8,128)(2,1)S(1)}, bf16[320,704]{1,0:T(8,128)(2,1)S(1)}, u32[]{:S(2)}, u32[]{:S(2)}) %collective-permute-start.37) | collective-permute-done | bytes 450592 | tf_op jit(solution)/shard_map/ppermute | solution.py:54
  597.7 7.0 collective-permute-done.34
  669.6 7.3 shard_map.351.refs_2_
  676.8 7.2 shard_map.352
  724.5 6.2 collective-permute-done.28
  741.6 7.9 collective-permute-done.40
  805.5 19.7 %reduce-scatter.8.cloned.1.call-done = bf16[176,3072]{1,0:T(8,128)(2,1)} async-done(((bf16[1408,3072]{1,0:T(8,128)(2,1)}), bf16[176,3072]{1,0:T(8,128)(2,1)}) %reduce-scatter.8.cloned.1.call-update) | async-done | bytes 1081360 | tf_op jit(solution)/shard_map/reduce_scatter | solution.py:521
  856.3 74.0 %reduce-scatter.6.cloned.1.call-done = bf16[176,4992]{1,0:T(8,128)(2,1)} async-done(((bf16[1408,4992]{1,0:T(8,128)(2,1)}), bf16[176,4992]{1,0:T(8,128)(2,1)}) %reduce-scatter.6.cloned.1.call-update) | async-done | bytes 1757200 | tf_op jit(solution)/shard_map/reduce_scatter | solution.py:565
  939.7 7.2 collective-permute-done.54
  (867 shorter events, 607.9 us)
Async XLA Ops:
  7.2 127.0 %all-gather.4.cloned.1.call-start = ((), (), s32[]{:S(2)}) async-start(), calls=%async_computation.5 | async-start | bytes 14598144 | tf_op jit(solution)/shard_map/all_gather | solution.py:393
  11.7 246.9 %all-gather.6.cloned.1.call-start = ((), (), s32[]{:S(2)}) async-start(), calls=%async_computation.6 | async-start | bytes 13381632 | tf_op jit(solution)/shard_map/all_gather | solution.py:403
  49.5 284.6 %all-gather.8.cloned.1.call-start = ((), (), s32[]{:S(2)}) async-start(), calls=%async_computation.7 | async-start | bytes 9732096 | tf_op jit(solution)/shard_map/all_gather | solution.py:407
  51.6 48.3 %collective-permute-start.3 = (bf16[80,1408]{1,0:T(8,128)(2,1)}, bf16[80,1408]{1,0:T(8,128)(2,1)}, u32[]{:S(2)}, u32[]{:S(2)}) collective-permute-start(bf16[80,1408]{1,0:T(8,128)(2,1)} %param.25), channel_id=1, source_target_pairs={{0,1},{1,2},{2,3},{3,0},{4,5},{5,6},{6,7},{7,4},{8,9},{9,10},{10,1... | collective-permute-start | bytes 675848 | tf_op jit(solution)/shard_map/ppermute | solution.py:54
  55.8 43.7 %collective-permute-start.6 = (bf16[256,1408]{1,0:T(8,128)(2,1)}, bf16[256,1408]{1,0:T(8,128)(2,1)}, u32[]{:S(2)}, u32[]{:S(2)}) collective-permute-start(bf16[256,1408]{1,0:T(8,128)(2,1)} %param.40), channel_id=1, source_target_pairs={{0,1},{1,2},{2,3},{3,0},{4,5},{5,6},{6,7},{7,4},{8,9},{9,10},{10,1... | collective-permute-start | bytes 2162696 | tf_op jit(solution)/shard_map/ppermute | solution.py:54
  82.2 684.9 %reduce-scatter.4.cloned.1.call-start = ((), (), s32[]{:S(2)}) async-start(), calls=%async_computation.8 | async-start | bytes 12976128 | tf_op jit(solution)/shard_map/reduce_scatter | solution.py:622
  99.5 31.1 %collective-permute-start.7 = (bf16[256,1408]{1,0:T(8,128)(2,1)}, bf16[256,1408]{1,0:T(8,128)(2,1)}, u32[]{:S(2)}, u32[]{:S(2)}) collective-permute-start(bf16[256,1408]{1,0:T(8,128)(2,1)} %collective-permute-done.6), channel_id=1, source_target_pairs={{0,1},{1,2},{2,3},{3,0},{4,5},{5,6},{6,7},{7,4},{8,9},{9,10},{10,1... | collective-permute-start | bytes 2162696 | tf_op jit(solution)/shard_map/ppermute | solution.py:54
  99.8 23.5 %collective-permute-start.4 = (bf16[80,1408]{1,0:T(8,128)(2,1)}, bf16[80,1408]{1,0:T(8,128)(2,1)S(1)}, u32[]{:S(2)}, u32[]{:S(2)}) collective-permute-start(bf16[80,1408]{1,0:T(8,128)(2,1)} %collective-permute-done.3), channel_id=1, source_target_pairs={{0,1},{1,2},{2,3},{3,0},{4,5},{5,6},{6,7},{7,4},{8,9},{9,10},{10,1... | collective-permute-start | bytes 675848 | tf_op jit(solution)/shard_map/ppermute | solution.py:54
  244.0 27.5 %collective-permute-start.18 = (bf16[320,704]{1,0:T(8,128)(2,1)}, bf16[320,704]{1,0:T(8,128)(2,1)}, u32[]{:S(2)}, u32[]{:S(2)}) collective-permute-start(bf16[320,704]{1,0:T(8,128)(2,1)} %pad_maximum_fusion.10), channel_id=1, source_target_pairs={{0,1},{1,2},{2,3},{3,0},{4,5},{5,6},{6,7},{7,4},{8,9},{9,10},{10,1... | collective-permute-start | bytes 1351688 | tf_op jit(solution)/shard_map/ppermute | solution.py:54
  271.5 25.3 %collective-permute-start.19 = (bf16[320,704]{1,0:T(8,128)(2,1)}, bf16[320,704]{1,0:T(8,128)(2,1)S(1)}, u32[]{:S(2)}, u32[]{:S(2)}) collective-permute-start(bf16[320,704]{1,0:T(8,128)(2,1)} %collective-permute-done.18), channel_id=1, source_target_pairs={{0,1},{1,2},{2,3},{3,0},{4,5},{5,6},{6,7},{7,4},{8,9},{9,10},{10,1... | collective-permute-start | bytes 1351688 | tf_op jit(solution)/shard_map/ppermute | solution.py:54
  349.4 21.2 %collective-permute-start.23 = (bf16[256,1408]{1,0:T(8,128)(2,1)}, bf16[256,1408]{1,0:T(8,128)(2,1)S(1)}, u32[]{:S(2)}, u32[]{:S(2)}) collective-permute-start(bf16[256,1408]{1,0:T(8,128)(2,1)} %collective-permute-done.21), channel_id=1, source_target_pairs={{0,1},{1,2},{2,3},{3,0},{4,5},{5,6},{6,7},{7,4},{8,9},{9,10},{10,1... | collective-permute-start | bytes 2162696 | tf_op jit(solution)/shard_map/ppermute | solution.py:54
  362.6 23.3 %collective-permute-start.22 = (bf16[256,1408]{1,0:T(8,128)(2,1)S(1)}, bf16[256,1408]{1,0:T(8,128)(2,1)S(1)}, u32[]{:S(2)}, u32[]{:S(2)}) collective-permute-start(bf16[256,1408]{1,0:T(8,128)(2,1)S(1)} %convolution_convert_fusion), channel_id=1, source_target_pairs={{0,1},{1,2},{2,3},{3,0},{4,5},{5,6},{6,7},{7,4},{8,9},{9,10},{10,1... | collective-permute-start | bytes 2162696 | tf_op jit(solution)/shard_map/ppermute | solution.py:54
  370.6 25.3 %collective-permute-start.25 = (bf16[256,1408]{1,0:T(8,128)(2,1)S(1)}, bf16[256,1408]{1,0:T(8,128)(2,1)S(1)}, u32[]{:S(2)}, u32[]{:S(2)}) collective-permute-start(bf16[256,1408]{1,0:T(8,128)(2,1)S(1)} %collective-permute-done.23), channel_id=1, source_target_pairs={{0,1},{1,2},{2,3},{3,0},{4,5},{5,6},{6,7},{7,4},{8,9},{9,10},{10,1... | collective-permute-start | bytes 2162696 | tf_op jit(solution)/shard_map/ppermute | solution.py:54
  387.3 23.6 %collective-permute-start.24 = (bf16[256,1408]{1,0:T(8,128)(2,1)S(1)}, bf16[256,1408]{1,0:T(8,128)(2,1)S(1)}, u32[]{:S(2)}, u32[]{:S(2)}) collective-permute-start(bf16[256,1408]{1,0:T(8,128)(2,1)S(1)} %add_convert_fusion.8), channel_id=1, source_target_pairs={{0,1},{1,2},{2,3},{3,0},{4,5},{5,6},{6,7},{7,4},{8,9},{9,10},{10,1... | collective-permute-start | bytes 2162696 | tf_op jit(solution)/shard_map/ppermute | solution.py:54
  471.4 28.8 %collective-permute-start.27 = (bf16[256,352]{1,0:T(8,128)(2,1)}, bf16[256,352]{1,0:T(8,128)(2,1)}, u32[]{:S(2)}, u32[]{:S(2)}) collective-permute-start(bf16[256,352]{1,0:T(8,128)(2,1)} %get-tuple-element.235), channel_id=1, source_target_pairs={{0,3},{1,0},{2,1},{3,2},{4,7},{5,4},{6,5},{7,6},{8,11},{9,8},{10,9... | collective-permute-start | bytes 540680 | tf_op jit(solution)/shard_map/ppermute | solution.py:54
  471.4 30.4 %collective-permute-start.32 = (bf16[256,352]{1,0:T(8,128)(2,1)}, bf16[256,352]{1,0:T(8,128)(2,1)}, u32[]{:S(2)}, u32[]{:S(2)}) collective-permute-start(bf16[256,352]{1,0:T(8,128)(2,1)} %get-tuple-element.233), channel_id=1, source_target_pairs={{0,2},{1,3},{2,0},{3,1},{4,6},{5,7},{6,4},{7,5},{8,10},{9,11},{10,... | collective-permute-start | bytes 540680 | tf_op jit(solution)/shard_map/ppermute | solution.py:54
  476.3 25.5 %collective-permute-start.31 = (bf16[256,352]{1,0:T(8,128)(2,1)}, bf16[256,352]{1,0:T(8,128)(2,1)}, u32[]{:S(2)}, u32[]{:S(2)}) collective-permute-start(bf16[256,352]{1,0:T(8,128)(2,1)} %get-tuple-element.234), channel_id=1, source_target_pairs={{0,1},{1,2},{2,3},{3,0},{4,5},{5,6},{6,7},{7,4},{8,9},{9,10},{10,1... | collective-permute-start | bytes 540680 | tf_op jit(solution)/shard_map/ppermute | solution.py:54
  500.3 51.8 %collective-permute-start.36 = (bf16[320,704]{1,0:T(8,128)(2,1)S(1)}, bf16[320,704]{1,0:T(8,128)(2,1)S(1)}, u32[]{:S(2)}, u32[]{:S(2)}) collective-permute-start(bf16[320,704]{1,0:T(8,128)(2,1)S(1)} %pad_maximum_fusion.11), channel_id=1, source_target_pairs={{0,1},{1,2},{2,3},{3,0},{4,5},{5,6},{6,7},{7,4},{8,9},{9,10},{10,1... | collective-permute-start | bytes 1351688 | tf_op jit(solution)/shard_map/ppermute | solution.py:54
  550.6 33.6 %collective-permute-start.33 = (bf16[256,1408]{1,0:T(8,128)(2,1)}, bf16[256,1408]{1,0:T(8,128)(2,1)}, u32[]{:S(2)}, u32[]{:S(2)}) collective-permute-start(bf16[256,1408]{1,0:T(8,128)(2,1)} %get-tuple-element.218), channel_id=1, source_target_pairs={{0,1},{1,2},{2,3},{3,0},{4,5},{5,6},{6,7},{7,4},{8,9},{9,10},{10,1... | collective-permute-start | bytes 2162696 | tf_op jit(solution)/shard_map/ppermute | solution.py:54
  552.4 27.7 %collective-permute-start.37 = (bf16[320,704]{1,0:T(8,128)(2,1)S(1)}, bf16[320,704]{1,0:T(8,128)(2,1)S(1)}, u32[]{:S(2)}, u32[]{:S(2)}) collective-permute-start(bf16[320,704]{1,0:T(8,128)(2,1)S(1)} %fusion.98), channel_id=1, source_target_pairs={{0,1},{1,2},{2,3},{3,0},{4,5},{5,6},{6,7},{7,4},{8,9},{9,10},{10,1... | collective-permute-start | bytes 1351688 | tf_op jit(solution)/shard_map/ppermute | solution.py:54
  662.3 163.0 %reduce-scatter.8.cloned.1.call-start = ((), (), s32[]{:S(2)}) async-start(), calls=%async_computation.10 | async-start | bytes 9732096 | tf_op jit(solution)/shard_map/reduce_scatter | solution.py:521
  684.1 246.1 %reduce-scatter.6.cloned.1.call-start = ((), (), s32[]{:S(2)}) async-start(), calls=%async_computation.9 | async-start | bytes 15814656 | tf_op jit(solution)/shard_map/reduce_scatter | solution.py:565
  730.8 23.1 %collective-permute-start.29 = (bf16[256,1408]{1,0:T(8,128)(2,1)S(1)}, bf16[256,1408]{1,0:T(8,128)(2,1)S(1)}, u32[]{:S(2)}, u32[]{:S(2)}) collective-permute-start(bf16[256,1408]{1,0:T(8,128)(2,1)S(1)} %add_convert_fusion.5), channel_id=1, source_target_pairs={{0,1},{1,2},{2,3},{3,0},{4,5},{5,6},{6,7},{7,4},{8,9},{9,10},{10,1... | collective-permute-start | bytes 2162696 | tf_op jit(solution)/shard_map/ppermute | solution.py:54
  790.7 36.0 %collective-permute-start.50 = (bf16[176,736]{1,0:T(8,128)(2,1)S(1)}, bf16[176,736]{1,0:T(8,128)(2,1)S(1)}, u32[]{:S(2)}, u32[]{:S(2)}) collective-permute-start(bf16[176,736]{1,0:T(8,128)(2,1)S(1)} %add_convert_fusion.15), channel_id=1, source_target_pairs={{0,1},{1,2},{2,3},{3,0},{4,5},{5,6},{6,7},{7,4},{8,9},{9,10},{10,1... | collective-permute-start | bytes 777224 | tf_op jit(solution)/shard_map/ppermute | solution.py:54
  (218 other events, 2158.7 us)
Sparse Core Ops, SparseCore 0:
  11.9 76.0 all-gather.3
  89.8 69.4 all-gather.5
  161.2 55.4 all-gather.7
  662.4 86.3 reduce-scatter.3
  752.1 73.1 reduce-scatter.7
  829.3 100.9 reduce-scatter.5

commit v2 on v1

--- a/solution.py
+++ b/solution.py
@@ -66,6 +66,18 @@
     for part in parts[2:]:
         running = (rot(running, 1).astype(FLOAT) + part.astype(FLOAT)).astype(BFLOAT)
     return rot(running, 1).astype(FLOAT) + parts[0].astype(FLOAT)
+
+
+def direct_gather(own):
+    return [own] + [rot(own, r) for r in range(1, lax.axis_size("tensor"))]
+
+
+def direct_scatter(parts):
+    count = len(parts)
+    total = parts[0].astype(FLOAT)
+    for r in range(1, count):
+        total = total + rot(parts[r], count - r).astype(FLOAT)
+    return total
 
 
 def exchange(parts):
@@ -221,7 +233,7 @@
             jax.ShapeDtypeStruct((heads * (length // block), 1, block), FLOAT),
         ),
         compiler_params=pltpu.CompilerParams(vmem_limit_bytes=56 * 2**20),
-        cost_estimate=pl.CostEstimate(flops=4_000_000_000, bytes_accessed=12_000_000, transcendentals=4_200_000),
+        cost_estimate=pl.CostEstimate(flops=36_000_000_000, bytes_accessed=12_000_000, transcendentals=4_200_000),
     )(raw, *tables, gains)
 
 
@@ -321,30 +333,204 @@
             pltpu.VMEM((heads, length, LANES), FLOAT),
         ],
         compiler_params=pltpu.CompilerParams(vmem_limit_bytes=56 * 2**20),
-        cost_estimate=pl.CostEstimate(flops=10_000_000_000, bytes_accessed=16_000_000, transcendentals=4_200_000),
+        cost_estimate=pl.CostEstimate(flops=46_000_000_000, bytes_accessed=16_000_000, transcendentals=4_200_000),
     )(raw, *tables, gains, *kept, grad_out)
 
 
-def cross_forward(queries, keys, values_in):
-    scores = jnp.einsum("qhd,khd->hqk", queries, keys, preferred_element_type=FLOAT) * SCALE
-    peak = jnp.max(scores, axis=-1, keepdims=True)
-    powers = jnp.exp(scores - peak)
-    totals = jnp.sum(powers, axis=-1, keepdims=True)
-    weights = (powers / totals).astype(BFLOAT)
-    mixed = jnp.einsum("hqk,khd->qhd", weights, values_in, preferred_element_type=FLOAT)
-    return mixed.astype(BFLOAT), peak + jnp.log(totals)
-
-
-def cross_backward(queries, keys, values_in, log_sums, grad):
-    scores = jnp.einsum("qhd,khd->hqk", queries, keys, preferred_element_type=FLOAT) * SCALE
-    probs = jnp.exp(scores - log_sums)
-    grad_probs = jnp.einsum("qhd,khd->hqk", grad, values_in, preferred_element_type=FLOAT)
-    inner = jnp.sum(probs * grad_probs, axis=-1, keepdims=True)
-    grad_scores = (probs * (grad_probs - inner)).astype(BFLOAT)
-    grad_q = jnp.einsum("hqk,khd->qhd", grad_scores, keys, preferred_element_type=FLOAT) * SCALE
-    grad_k = jnp.einsum("hqk,qhd->khd", grad_scores, queries, preferred_element_type=FLOAT) * SCALE
-    grad_v = jnp.einsum("hqk,qhd->khd", probs.astype(BFLOAT), grad, preferred_element_type=FLOAT)
-    return grad_q, grad_k, grad_v
+def norm_rows(values):
+    count = values.shape[-1]
+    mean = jnp.sum(values, axis=-1, keepdims=True) * (1.0 / count)
+    centred = values - mean
+    inverse = lax.rsqrt(jnp.sum(centred * centred, axis=-1, keepdims=True) * (1.0 / count) + EPSILON)
+    return centred * inverse, inverse
+
+
+def norm_rows_back(values, gain, grad):
+    normed, inverse = norm_rows(values)
+    count = values.shape[-1]
+    gain_grad = jnp.sum(grad * normed, axis=0, keepdims=True)
+    bias_grad = jnp.sum(grad, axis=0, keepdims=True)
+    grad = grad * gain
+    mean = jnp.sum(grad, axis=-1, keepdims=True) * (1.0 / count)
+    slope = jnp.sum(grad * normed, axis=-1, keepdims=True) * (1.0 / count)
+    return inverse * (grad - mean - normed * slope), gain_grad, bias_grad
+
+
+def head_means(values, group):
+    high = values.astype(BFLOAT)
+    rest = (values - high.astype(FLOAT)).astype(BFLOAT)
+    return (dot(high, group) + dot(rest, group)) * (1.0 / HD)
+
+
+def norm_heads(values, group):
+    centred = values - head_means(values, group)
+    inverse = lax.rsqrt(head_means(centred * centred, group) + EPSILON)
+    return centred * inverse, inverse
+
+
+def head_masks(heads, span):
+    lanes = lax.broadcasted_iota(jnp.int32, (1, span), 1)
+    return [((lanes >= HD * head) & (lanes < HD * (head + 1))).astype(BFLOAT) for head in range(heads)]
+
+
+def load_weights(weights_ref, kept_ref, sems):
+    width = kept_ref.shape[-1]
+    return [
+        pltpu.make_async_copy(weights_ref.at[:, i * width : (i + 1) * width], kept_ref.at[i], sems.at[i])
+        for i in range(3)
+    ]
+
+
+def middle_forward_kernel(
+    heads, mixed_ref, one_ref, table_ref, text_ref, group_ref, weights_ref,
+    two_ref, raw_ref, three_ref, cross_ref, query_ref, cross_mixed_ref, mlp_ref, kept_ref, sems,
+):
+    span = heads * HD
+    loads = load_weights(weights_ref, kept_ref, sems)
+    for load in loads:
+        load.start()
+    row = lambda index: table_ref[index : index + 1, :]
+    loads[0].wait()
+    two = one_ref[...] + dot(mixed_ref[...], kept_ref[0], NT) + row(0)
+    two_ref[...] = two
+    cross = (norm_rows(two)[0] * row(1) + row(2)).astype(BFLOAT)
+    cross_ref[...] = cross
+    loads[1].wait()
+    raw_ref[...] = dot(cross, kept_ref[1]) + row(3)
+    group = group_ref[...]
+    masks = head_masks(heads, span)
+    pieces, mixes = [], []
+    for r in range(text_ref.shape[0]):
+        part = slice(r * span, (r + 1) * span)
+        normed, _ = norm_heads(raw_ref[:, part], group)
+        queries = (normed * table_ref[4:5, part]).astype(BFLOAT)
+        pieces.append(queries)
+        keys, values = text_ref[r, :, :span], text_ref[r, :, span:]
+        mix = None
+        for head in range(heads):
+            scores = dot(queries * masks[head], keys, NT)
+            peak = jnp.max(scores, axis=-1, keepdims=True)
+            powers = jnp.exp2((scores - peak) * (SCALE * LOG2E))
+            weights = (powers / jnp.sum(powers, axis=-1, keepdims=True)).astype(BFLOAT)
+            term = dot(weights, values * masks[head])
+            mix = term if mix is None else mix + term
+        mixes.append(mix.astype(BFLOAT))
+    query_ref[...] = jnp.concatenate(pieces, axis=1)
+    cross_mixed_ref[...] = jnp.concatenate(mixes, axis=1)
+    loads[2].wait()
+    three = two_ref[...] + dot(cross_mixed_ref[...], kept_ref[2], NT) + row(5)
+    three_ref[...] = three
+    mlp_ref[...] = (norm_rows(three)[0] * row(6) + row(7)).astype(BFLOAT)
+
+
+def middle_forward(mixed, one, table, text, group, weights, heads):
+    rows, width = one.shape
+    wide = jax.ShapeDtypeStruct((rows, width), FLOAT)
+    low = jax.ShapeDtypeStruct((rows, width), BFLOAT)
+    vmem = pl.BlockSpec(memory_space=pltpu.VMEM)
+    return pl.pallas_call(
+        functools.partial(middle_forward_kernel, heads),
+        in_specs=[vmem] * 5 + [pl.BlockSpec(memory_space=pl.ANY)],
+        out_shape=(wide, wide, wide, low, low, low, low),
+        out_specs=(vmem,) * 7,
+        scratch_shapes=[pltpu.VMEM((3, width, width), BFLOAT), pltpu.SemaphoreType.DMA((3,))],
+        compiler_params=pltpu.CompilerParams(vmem_limit_bytes=56 * 2**20),
+        cost_estimate=pl.CostEstimate(flops=26_000_000_000, bytes_accessed=24_000_000, transcendentals=1_300_000),
+    )(mixed, one, table, text, group, weights)
+
+
+def middle_backward_kernel(
+    heads, grad_ref, cot_ref, three_ref, two_ref, raw_ref, query_ref, table_ref, text_ref, group_ref, weights_ref,
+    three_low_ref, raw_low_ref, two_low_ref, grad_two_ref, mixed_ref, text_grad_ref, rows_ref, kept_ref, grad_three_ref,
+    sems,
+):
+    span = heads * HD
+    loads = load_weights(weights_ref, kept_ref, sems)
+    for load in reversed(loads):
+        load.start()
+    row = lambda index: table_ref[index : index + 1, :]
+    into, gain_grad, bias_grad = norm_rows_back(three_ref[...], row(6), grad_ref[...])
+    rows_ref[0:1, :], rows_ref[1:2, :] = gain_grad, bias_grad
+    grad_three = cot_ref[...].astype(FLOAT) + into
+    grad_three_ref[...] = grad_three
+    rows_ref[2:3, :] = jnp.sum(grad_three, axis=0, keepdims=True)
+    three_low = grad_three.astype(BFLOAT)
+    three_low_ref[...] = three_low
+    loads[2].wait()
+    mixed_ref[...] = dot(three_low, kept_ref[2]).astype(BFLOAT)
+    group = group_ref[...]
+    masks = head_masks(heads, span)
+    pieces = []
+    for r in range(text_ref.shape[0]):
+        part = slice(r * span, (r + 1) * span)
+        keys, values = text_ref[r, :, :span], text_ref[r, :, span:]
+        queries, mixed = query_ref[:, part], mixed_ref[:, part]
+        grad_q = grad_k = grad_v = None
+        for head in range(heads):
+            some, grad = queries * masks[head], mixed * masks[head]
+            scores = dot(keys, some, NT)
+            peak = jnp.max(scores, axis=0, keepdims=True)
+            powers = jnp.exp2((scores - peak) * (SCALE * LOG2E))
+            probs = powers / jnp.sum(powers, axis=0, keepdims=True)
+            grad_probs = dot(values, grad, NT)
+            inner = jnp.sum(probs * grad_probs, axis=0, keepdims=True)
+            grad_scores = (probs * (grad_probs - inner)).astype(BFLOAT)
+            add_q = dot(grad_scores, keys * masks[head], TN)
+            add_k = dot(grad_scores, some)
+            add_v = dot(probs.astype(BFLOAT), grad)
+            if head == 0:
+                grad_q, grad_k, grad_v = add_q, add_k, add_v
+            else:
+                grad_q, grad_k, grad_v = grad_q + add_q, grad_k + add_k, grad_v + add_v
+        text_grad_ref[r, :, :span] = (grad_k * SCALE).astype(BFLOAT)
+        text_grad_ref[r, :, span:] = grad_v.astype(BFLOAT)
+        normed, inverse = norm_heads(raw_ref[:, part], group)
+        grad_q = grad_q * SCALE
+        rows_ref[7:8, part] = jnp.sum(grad_q * normed, axis=0, keepdims=True)
+        grad_q = grad_q * table_ref[4:5, part]
+        low = (
+            inverse * (grad_q - head_means(grad_q, group) - normed * head_means(grad_q * normed, group))
+        ).astype(BFLOAT)
+        pieces.append(low)
+    raw_low_ref[...] = jnp.concatenate(pieces, axis=1)
+    rows_ref[6:7, :] = jnp.sum(raw_low_ref[...].astype(FLOAT), axis=0, keepdims=True)
+    loads[1].wait()
+    into, gain_grad, bias_grad = norm_rows_back(two_ref[...], row(1), dot(raw_low_ref[...], kept_ref[1], NT))
+    rows_ref[3:4, :], rows_ref[4:5, :] = gain_grad, bias_grad
+    grad_two = grad_three_ref[...] + into
+    grad_two_ref[...] = grad_two
+    rows_ref[5:6, :] = jnp.sum(grad_two, axis=0, keepdims=True)
+    two_low = grad_two.astype(BFLOAT)
+    two_low_ref[...] = two_low
+    loads[0].wait()
+    mixed_ref[...] = dot(two_low, kept_ref[0]).astype(BFLOAT)
+
+
+def middle_backward(grad, cot, three, two, raw, queries, table, text, group, weights, heads):
+    rows, width = three.shape
+    low = jax.ShapeDtypeStruct((rows, width), BFLOAT)
+    vmem = pl.BlockSpec(memory_space=pltpu.VMEM)
+    return pl.pallas_call(
+        functools.partial(middle_backward_kernel, heads),
+        in_specs=[vmem] * 9 + [pl.BlockSpec(memory_space=pl.ANY)],
+        out_shape=(
+            low,
+            low,
+            low,
+            jax.ShapeDtypeStruct((rows, width), FLOAT),
+            low,
+            jax.ShapeDtypeStruct(text.shape, BFLOAT),
+            jax.ShapeDtypeStruct((8, width), FLOAT),
+        ),
+        out_specs=(vmem,) * 7,
+        scratch_shapes=[
+            pltpu.VMEM((3, width, width), BFLOAT),
+            pltpu.VMEM((rows, width), FLOAT),
+            pltpu.SemaphoreType.DMA((3,)),
+        ],
+        compiler_params=pltpu.CompilerParams(vmem_limit_bytes=56 * 2**20),
+        cost_estimate=pl.CostEstimate(flops=33_000_000_000, bytes_accessed=28_000_000, transcendentals=1_300_000),
+    )(grad, cot, three, two, raw, queries, table, text, group, weights)
 
 
 def on_device(
@@ -396,21 +582,18 @@
     w_text = all_one[:, 2 * width + 3 * span :]
 
     own_full = jnp.stack([proj_weight.T, query_weight, cross_weight.T])
-    full_blocks = ring_gather(own_full)
+    full_blocks, text_blocks = [own_full], [text_tokens]
+    for _ in range(split - 1):
+        both = lax.optimization_barrier((full_blocks[-1], text_blocks[-1]))
+        full_blocks.append(rot(both[0], 1))
+        text_blocks.append(rot(both[1], 1))
     packed_two = jnp.concatenate(
         [full_blocks[r][index] for index in range(3) for r in range(split)], axis=1
     )
-    all_two = lax.all_gather(packed_two, "dp", axis=0, tiled=True)
-    w_proj_t, w_query, w_cross_t = (all_two[:, i * width : (i + 1) * width] for i in range(3))
-
-    packed_three = jnp.concatenate([up_weight, down_weight.T], axis=1)
-    all_three = lax.all_gather(packed_three, "dp", axis=0, tiled=True)
-    w_up, w_down_t = all_three[:, :hidden], all_three[:, hidden:]
-
-    text_blocks = ring_gather(text_tokens)
-    cot_blocks = ring_gather(out_grad)
+
+    cot_blocks = [out_grad, rot(after(out_grad, full_blocks[-1], text_blocks[-1]), 1)]
+    cot_blocks.append(rot(cot_blocks[1], 1))
     text_full = jnp.concatenate(text_blocks, axis=0)
-    cot_full = jnp.concatenate(cot_blocks, axis=0)
 
     def head_slice(index):
         return lax.dynamic_slice_in_dim(table[index], place * span, span, 0)
@@ -460,12 +643,17 @@
     joined_bias = jnp.concatenate([table[2], table[3]])
     normed_low = layer_norm(joined, joined_gain, joined_bias).astype(BFLOAT)
     normed_perm = normed_low.reshape(own_rows, shards, 2, part).transpose(0, 2, 1, 3).reshape(own_rows, 2 * width)
+    packed_two = after(packed_two, normed_perm, shift, *tables, cot_blocks[1])
+    all_two = lax.all_gather(packed_two, "dp", axis=0, tiled=True)
+    packed_three = jnp.concatenate([up_weight, down_weight.T], axis=1)
+    all_three = lax.all_gather(packed_three, "dp", axis=0, tiled=True)
+    w_up, w_down_t = all_three[:, :hidden], all_three[:, hidden:]
+
     stream_one = (
         dot(normed_perm[:, :width], w_skip[:, :width]) + dot(normed_perm[:, width:], w_skip[:, width:]) + table[4]
     )
     attn_low = (layer_norm(stream_one, table[6], table[7]) + shift).astype(BFLOAT)
-    attn_low = after(attn_low, text_blocks[-1], cot_blocks[-1], full_blocks[-1])
-    attn_blocks = ring_gather(attn_low)
+    attn_blocks = ring_gather(after(attn_low, cot_blocks[2]))
     qkv_bias = jnp.concatenate([head_slice(8), head_slice(9), head_slice(10)])
     raw = jnp.concatenate([dot(block, w_qkv) + qkv_bias for block in attn_blocks], axis=0)
     gains = jnp.concatenate([padded_gains(12), padded_gains(13)], axis=0)
@@ -475,8 +663,6 @@
 
     def blocks_of(values, rows):
         return [values[r * rows : (r + 1) * rows] for r in range(split)]
-
-    mixed_own = jnp.concatenate(exchange(blocks_of(mixed, own_rows)), axis=1)
 
     text_raw = dot(text_full, w_text) + jnp.concatenate([head_slice(17), head_slice(18)])
     text_length = text_raw.shape[0]
@@ -485,20 +671,21 @@
     text_low = jnp.concatenate(
         [head_norm(raw_key, gain_21).reshape(text_length, span), text_raw[:, span:]], axis=1
     ).astype(BFLOAT)
-    text_rel = ring_gather(after(text_low, attn_blocks[-1]))
-    text_keys = jnp.concatenate([item[:, :span] for item in text_rel], axis=1).reshape(text_length, HEADS, HD)
-    text_values = jnp.concatenate([item[:, span:] for item in text_rel], axis=1).reshape(text_length, HEADS, HD)
-
-    stream_two = stream_one + dot(mixed_own, w_proj_t, NT) + table[11]
-    cross_low = layer_norm(stream_two, table[14], table[15]).astype(BFLOAT)
-    cross_raw = (dot(cross_low, w_query) + relative(16)).reshape(own_rows, HEADS, HD)
-    gain_20 = relative(20).reshape(HEADS, HD)
-    cross_queries = head_norm(cross_raw, gain_20).astype(BFLOAT)
-    cross_mixed, cross_logs = cross_forward(cross_queries, text_keys, text_values)
-    cross_mixed = cross_mixed.reshape(own_rows, width)
-    stream_three = stream_two + dot(cross_mixed, w_cross_t, NT) + table[19]
-    mlp_low = layer_norm(stream_three, table[22], table[23]).astype(BFLOAT)
-    mlp_blocks = ring_gather(mlp_low)
+    text_rel = jnp.stack(direct_gather(after(text_low, attn_blocks[-1])))
+    mixed_own = jnp.concatenate(exchange(blocks_of(after(mixed, text_rel), own_rows)), axis=1)
+    cot_blocks[-1], mixed_own = lax.optimization_barrier((cot_blocks[-1], mixed_own))
+    while len(cot_blocks) < split:
+        cot_blocks.append(rot(cot_blocks[-1], 1))
+    cot_full = jnp.concatenate(cot_blocks, axis=0)
+    lane_head = np.arange(span) // HD
+    group = jnp.asarray((lane_head[:, None] == lane_head[None, :]).astype(np.float32), BFLOAT)
+    middle_table = jnp.stack(
+        [table[11], table[14], table[15], relative(16), relative(20), table[19], table[22], table[23]]
+    )
+    stream_two, cross_raw, stream_three, cross_low, cross_queries, cross_mixed, mlp_low = middle_forward(
+        mixed_own, stream_one, middle_table, text_rel, group, all_two, heads
+    )
+    mlp_blocks = ring_gather(after(mlp_low, cot_blocks[-1]))
     hidden_bias = lax.dynamic_slice_in_dim(bias_all, place * hidden, hidden, 0)
 
     hidden_lows, pre_lows, out_parts, back_parts = [], [], [], []
@@ -518,63 +705,38 @@
     grad_bias = jnp.sum(pre_full, axis=0, dtype=FLOAT)
     grads_one = pack_grad(None, mlp_full, pre_full, 2 * hidden, 0, 512)
     grads_one = pack_grad(grads_one, cot_full, hidden_full, 2 * hidden, hidden, 512)
+    grads_one, grad_mlp_in = lax.optimization_barrier((grads_one, grad_mlp_in))
     summed_one = lax.psum_scatter(grads_one, "dp", scatter_dimension=0, tiled=True).astype(FLOAT)
 
     cot_here = out_grad.astype(FLOAT)
     rows_grad[24] = jnp.sum(cot_here, axis=0)
-    into_three, rows_grad[22], rows_grad[23] = jax.vjp(layer_norm, stream_three, table[22], table[23])[1](grad_mlp_in)
-    grad_three = cot_here + into_three
-    three_low = grad_three.astype(BFLOAT)
-    rows_grad[19] = jnp.sum(grad_three, axis=0)
-    grad_cross_mixed = dot(three_low, w_cross_t).astype(BFLOAT).reshape(own_rows, HEADS, HD)
-    grad_cq, grad_ck, grad_cv = cross_backward(cross_queries, text_keys, text_values, cross_logs, grad_cross_mixed)
-    into_cq, gain_cq = jax.vjp(head_norm, cross_raw, gain_20)[1](grad_cq)
-    rows_grad[20] = absolute(gain_cq)
-    cq_low = into_cq.reshape(own_rows, width).astype(BFLOAT)
-    rows_grad[16] = absolute(jnp.sum(cq_low, axis=0, dtype=FLOAT))
-    grad_cross_in = dot(cq_low, w_query, NT)
-    into_two, rows_grad[14], rows_grad[15] = jax.vjp(layer_norm, stream_two, table[14], table[15])[1](grad_cross_in)
-    grad_two = grad_three + into_two
-    two_low = grad_two.astype(BFLOAT)
-    rows_grad[11] = jnp.sum(grad_two, axis=0)
-    grad_mixed = dot(two_low, w_proj_t).astype(BFLOAT)
+    three_low, cq_low, two_low, grad_two, grad_mixed, text_terms, middle_rows = middle_backward(
+        grad_mlp_in, out_grad, stream_three, stream_two, cross_raw, cross_queries, middle_table, text_rel, group,
+        all_two, heads,
+    )
+    for index, number in enumerate((22, 23, 19, 14, 15, 11)):
+        rows_grad[number] = middle_rows[index]
+    rows_grad[16], rows_grad[20] = absolute(middle_rows[6]), absolute(middle_rows[7])
     grad_mixed_blocks = exchange([grad_mixed[:, r * span : (r + 1) * span] for r in range(split)])
-    out_parts[1] = after(out_parts[1].astype(BFLOAT), grad_mixed_blocks[-1])
-    block_out = (stream_three + ring_scatter(out_parts) + table[24]).astype(BFLOAT)
-
-    grad_ck = grad_ck.reshape(text_length, width)
-    grad_cv = grad_cv.reshape(text_length, width)
-    text_terms = [
-        jnp.concatenate([grad_ck[:, r * span : (r + 1) * span], grad_cv[:, r * span : (r + 1) * span]], axis=1)
-        for r in range(split)
-    ]
-    text_terms[1] = after(text_terms[1].astype(BFLOAT), grad_mixed_blocks[-1])
-    text_sum = ring_scatter(text_terms)
+    lanes_two = 3 * width
+    grads_two = pack_grad(None, two_low, mixed_own, lanes_two, 0, width)
+    grads_two = pack_grad(grads_two, cross_low, cq_low, lanes_two, width, width)
+    grads_two = pack_grad(grads_two, three_low, cross_mixed, lanes_two, 2 * width, width)
+    grads_two, *grad_mixed_blocks = lax.optimization_barrier((grads_two, *grad_mixed_blocks))
+    summed_two = lax.psum_scatter(grads_two, "dp", scatter_dimension=0, tiled=True)
+    text_terms = after(text_terms, grad_mixed_blocks[-1])
+    text_sum = direct_scatter([text_terms[r] for r in range(split)])
+    grad_raw, gain_grads, raw_sums = attend_backward(
+        raw, tables, gains, kept, jnp.concatenate(grad_mixed_blocks, axis=0), heads, block
+    )
+    text_sum, grad_raw, summed_one = lax.optimization_barrier((text_sum, grad_raw, summed_one))
     into_ck, gain_ck = jax.vjp(head_norm, raw_key, gain_21)[1](text_sum[:, :span].reshape(text_length, heads, HD))
     rows_grad[21] = spread(gain_ck)
     ckv_low = jnp.concatenate([into_ck.reshape(text_length, span), text_sum[:, span:]], axis=1).astype(BFLOAT)
+    text_back = dot(ckv_low, w_text, NT)
     ckv_sums = jnp.sum(ckv_low, axis=0, dtype=FLOAT)
     rows_grad[17], rows_grad[18] = spread(ckv_sums[:span]), spread(ckv_sums[span:])
-    text_grad = ring_scatter(blocks_of(dot(ckv_low, w_text, NT), own_text))
-
-    lanes_two = 3 * width + pl.cdiv(2 * span, LANES) * LANES
-    grads_two = pack_grad(None, two_low, mixed_own, lanes_two, 0, width)
-    grads_two = pack_grad(grads_two, cross_low, cq_low, lanes_two, width, width)
-    grads_two = pack_grad(grads_two, three_low, cross_mixed, lanes_two, 2 * width, width)
-    grads_two = pack_grad(grads_two, text_full, ckv_low, lanes_two, 3 * width, LANES)
-    summed_two = lax.psum_scatter(grads_two, "dp", scatter_dimension=0, tiled=True)
-    full_sum = ring_scatter(
-        [
-            jnp.concatenate(
-                [summed_two[:, i * width + r * span : i * width + (r + 1) * span] for i in range(3)], axis=1
-            )
-            for r in range(split)
-        ]
-    )
-
-    grad_raw, gain_grads, raw_sums = attend_backward(
-        raw, tables, gains, kept, jnp.concatenate(grad_mixed_blocks, axis=0), heads, block
-    )
+
     rows_grad[12] = spread(gain_grads[:heads, :HD])
     rows_grad[13] = spread(gain_grads[heads:, :HD])
     rows_grad[8], rows_grad[9], rows_grad[10] = spread(raw_sums[0]), spread(raw_sums[1]), spread(raw_sums[2])
@@ -582,22 +744,23 @@
     attn_parts = [dot(item, w_qkv, NT) for item in raw_blocks]
     shift_part = sum(jnp.sum(item, axis=0) for item in attn_parts)
     rows_grad[5] = shift_part
+    qkv_lanes = pl.cdiv(3 * span, LANES) * LANES
+    text_lanes = pl.cdiv(2 * span, LANES) * LANES
+    grads_qkv = pack_grad(
+        None, jnp.concatenate(attn_blocks, axis=0), grad_raw, qkv_lanes + text_lanes, 0, LANES
+    )
+    grads_qkv = pack_grad(grads_qkv, text_full, ckv_low, qkv_lanes + text_lanes, qkv_lanes, LANES)
+    summed_qkv = lax.psum_scatter(grads_qkv, "dp", scatter_dimension=0, tiled=True)
+    attn_parts[3 % split] = after(attn_parts[3 % split], grads_qkv)
     grad_attn_in = ring_scatter(attn_parts)
-    shift_grads = small_gather(tensor_sum(shift_part))
-    mod_grad = lax.dot_general(
-        silu_mine.astype(FLOAT), shift_grads, ((TN), ((), ())), precision=HIGHEST, preferred_element_type=FLOAT
-    )
-    into_silu = lax.dot_general(
-        shift_grads, mod_weight.astype(FLOAT), ((NT), ((), ())), precision=HIGHEST, preferred_element_type=FLOAT
-    )
-    into_silu = lax.all_to_all(into_silu, "dp", 0, 0, tiled=True).reshape(1, width)
-    time_full = jax.vjp(silu, condition)[1](into_silu)[0]
-    time_grad = lax.dynamic_slice_in_dim(time_full, place * (width // split), width // split, 1)
+    out_parts[1] = after(out_parts[1].astype(BFLOAT), grad_attn_in)
+    block_out = (stream_three + ring_scatter(out_parts) + table[24]).astype(BFLOAT)
+    text_grad = ring_scatter(blocks_of(after(text_back, grad_attn_in), own_text))
 
     into_one, rows_grad[6], rows_grad[7] = jax.vjp(layer_norm, stream_one, table[6], table[7])[1](grad_attn_in)
     grad_one = grad_two + into_one
     rows_grad[4] = jnp.sum(grad_one, axis=0)
-    one_low = grad_one.astype(BFLOAT)
+    one_low, summed_two = lax.optimization_barrier((grad_one.astype(BFLOAT), summed_two))
     grad_joined = jnp.concatenate([dot(one_low, w_skip[:, :width], NT), dot(one_low, w_skip[:, width:], NT)], axis=1)
     grad_joined = grad_joined.reshape(own_rows, 2, shards, part).transpose(0, 2, 1, 3).reshape(own_rows, 2 * width)
     into_joined, gain_joined, bias_joined = jax.vjp(layer_norm, joined, joined_gain, joined_bias)[1](grad_joined)
@@ -613,26 +776,45 @@
     small_grads = jnp.concatenate([table_grad, bias_grad], axis=1).astype(BFLOAT)
     small_grads = jnp.pad(small_grads, ((0, 0), (0, LANES - small_grads.shape[1])))
 
-    qkv_lanes = pl.cdiv(3 * span, LANES) * LANES
-    lanes_three = 2 * width + LANES + qkv_lanes
-    grads_three = pack_grad(None, jnp.concatenate(attn_blocks, axis=0), grad_raw, lanes_three, 2 * width + LANES, LANES)
-    grads_three = pack_grad(grads_three, normed_perm[:, :width], one_low, lanes_three, 0, width)
-    grads_three = pack_grad(grads_three, normed_perm[:, width:], one_low, lanes_three, width, width)
+    shared = 2 * width + LANES
+    grads_three = pack_grad(None, normed_perm[:, :width], one_low, shared, 0, width)
+    grads_three = pack_grad(grads_three, normed_perm[:, width:], one_low, shared, width, width)
     grads_three = lax.dynamic_update_slice(grads_three, small_grads, (0, 2 * width))
+    shift_part = after(shift_part, grads_three)
     summed_three = lax.psum_scatter(grads_three, "dp", scatter_dimension=0, tiled=True)
-    shared = 2 * width + LANES
+    full_sum = ring_scatter(
+        [
+            jnp.concatenate(
+                [summed_two[:, i * width + r * span : i * width + (r + 1) * span] for i in range(3)], axis=1
+            )
+            for r in range(split)
+        ]
+    )
+
+    summed_three = after(summed_three, full_sum, block_out, text_grad)
     chunk = shared // split
     shared_terms = [lax.dynamic_slice_in_dim(summed_three, others(r) * chunk, chunk, 1) for r in range(split)]
-    shared_blocks = ring_gather(ring_scatter(shared_terms).astype(BFLOAT))
+    shared_blocks = direct_gather(direct_scatter(shared_terms).astype(BFLOAT))
     shared_sum = jnp.zeros((part, shared), FLOAT)
     for r in range(split):
         shared_sum = lax.dynamic_update_slice_in_dim(shared_sum, shared_blocks[r].astype(FLOAT), others(r) * chunk, 1)
     skip_weight_grad = jnp.concatenate([shared_sum[:, :width], shared_sum[:, width : 2 * width]], axis=0)
     vectors_grad = shared_sum[:, 2 * width : 2 * width + rows_ahead].T
     bias_grad = shared_sum[:, 2 * width + rows_ahead : 2 * width + rows_ahead + bias_cols].T.reshape(-1)[:bias_part]
-    qkv_sum = summed_three[:, shared : shared + 3 * span].astype(FLOAT).reshape(part, 3, span)
-
-    text_sum_grad = summed_two[:, 3 * width : 3 * width + 2 * span].astype(FLOAT).reshape(part, 2, span)
+    qkv_sum = summed_qkv[:, : 3 * span].astype(FLOAT).reshape(part, 3, span)
+    text_sum_grad = summed_qkv[:, qkv_lanes : qkv_lanes + 2 * span].astype(FLOAT).reshape(part, 2, span)
+
+    shift_grads = small_gather(tensor_sum(shift_part))
+    mod_grad = lax.dot_general(
+        silu_mine.astype(FLOAT), shift_grads, ((TN), ((), ())), precision=HIGHEST, preferred_element_type=FLOAT
+    )
+    into_silu = lax.dot_general(
+        shift_grads, mod_weight.astype(FLOAT), ((NT), ((), ())), precision=HIGHEST, preferred_element_type=FLOAT
+    )
+    into_silu = lax.all_to_all(into_silu, "dp", 0, 0, tiled=True).reshape(1, width)
+    time_full = jax.vjp(silu, condition)[1](into_silu)[0]
+    time_grad = lax.dynamic_slice_in_dim(time_full, place * (width // split), width // split, 1)
+
     return (
         block_out,
         into_joined[:, :width],

time: 999 us -> 775 us (0.78)
  waiting for transfers between devices: 307 us -> 180 us
  matrix products: 146 us -> 98.6 us
  Pallas kernels: 120 us -> 167 us
  local copies, waits for them, and re-layouts: 158 us -> 111 us
  other arithmetic: 88.3 us -> 66.6 us
  starting transfers between devices: 144 us -> 124 us
    reduce_scatter x1, waiting for transfers between devices: 74 us -> 0.02 us  [on_device(): lax.psum_scatter(grads_two, 'dp', scatter_dimension=0, tiled=True)]
    pallas_call x0 -> x2, Pallas kernels: none -> 53 us  [the longest x1 29.5 us: middle_backward(): pl.pallas_call(functools.partial(middle_backward_kernel, heads), in_specs...]
    ppermute x51, waiting for transfers between devices: 207 us -> 162 us  [rot(): lax.ppermute(values, 'tensor', [(i, (i + step) % count) for i in range(co...]
    dot_general x37 -> x31, matrix products: 130 us -> 95.7 us  [dot(): lax.dot_general(left, right, (contract, ((), ())), preferred_element_type...]
    ppermute x51, starting transfers between devices: 135 us -> 107 us  [rot(): lax.ppermute(values, 'tensor', [(i, (i + step) % count) for i in range(co...]
    reduce_scatter x1, waiting for transfers between devices: 19.7 us -> 0.02 us  [on_device(): lax.psum_scatter(grads_one, 'dp', scatter_dimension=0, tiled=True)]
    unnamed x375 -> x337, local copies, waits for them, and re-layouts: 49 us -> 31.6 us
    dot_general x6 -> x0, matrix products: 13.3 us -> none  [the longest x1 4.49 us: cross_backward(): jnp.einsum('qhd,khd->hqk', grad, values_in, preferred_element_type=FLOAT)]
  transfers between devices with their start and end apart: 65 -> 66, of which waited for: 38 -> 28; matrix products, arithmetic and copies ran while one was open for 29% -> 29% of each run, Pallas kernels for 12% -> 21%
where the time goes in v2:
time: 775 us; the launch traced here: 765 us
  waiting for transfers between devices  180 us (23%)
  Pallas kernels  167 us (22%)
  starting transfers between devices  124 us (16%)
  local copies, waits for them, and re-layouts  111 us (14%)
  matrix products  98.6 us (13%)
  other arithmetic  66.6 us (9%)
  between operations  18.1 us (2%)
    ppermute x51, waiting for transfers between devices, rot(): lax.ppermute(values, 'tensor', [(i, (i + step) % count) for i in range(co...  162 us
    ppermute x51, starting transfers between devices, rot(): lax.ppermute(values, 'tensor', [(i, (i + step) % count) for i in range(co...  107 us
    dot_general x31, matrix products, dot(): lax.dot_general(left, right, (contract, ((), ())), preferred_element_type...  95.7 us
    pallas_call x1, Pallas kernels, attend_backward(): pl.pallas_call(functools.partial(attend_backward_kernel, heads, block), o...  41.7 us
    pallas_call x9, Pallas kernels, pack_grad(): pl.pallas_call(grad_kernel, grid=(pl.cdiv(wide, tile),), in_specs=in_spec...  39.2 us
    pallas_call x1, Pallas kernels, attend_forward(): pl.pallas_call(functools.partial(attend_forward_kernel, heads, block), ou...  32.7 us
    unnamed x337, local copies, waits for them, and re-layouts  31.6 us
    pallas_call x1, Pallas kernels, middle_backward(): pl.pallas_call(functools.partial(middle_backward_kernel, heads), in_specs...  29.5 us
  transfers between devices with their start and end apart: 66, of which 28 were waited for; matrix products, arithmetic and copies ran while one was open for 29% of the time, Pallas kernels for 21%

profile of v2, /device:TPU:24, one launch (start us, length us, event | category | flops | bytes accessed | tf_op | source)
XLA Modules:
  0.0 764.8 jit_solution(8520251298112364234)
XLA Ops:
  55.0 9.9 %collective-permute-done.5 = bf16[80,1408]{1,0:T(8,128)(2,1)} collective-permute-done((bf16[80,1408]{1,0:T(8,128)(2,1)}, bf16[80,1408]{1,0:T(8,128)(2,1)}, u32[]{:S(2)}, u32[]{:S(2)}) %collective-permute-start.5) | collective-permute-done | bytes 225312 | tf_op jit(solution)/shard_map/ppermute | solution.py:54
  117.7 7.4 collective-permute-done.11
  133.0 8.7 %collective-permute-done.12 = bf16[256,1408]{1,0:T(8,128)(2,1)S(1)} collective-permute-done((bf16[256,1408]{1,0:T(8,128)(2,1)}, bf16[256,1408]{1,0:T(8,128)(2,1)S(1)}, u32[]{:S(2)}, u32[]{:S(2)}) %collective-permute-start.12) | collective-permute-done | bytes 720928 | tf_op jit(solution)/shard_map/ppermute | solution.py:54
  152.5 6.0 collective-permute-done.13
  169.1 32.7 %shard_map.351 = (bf16[1024,352]{1,0:T(8,128)(2,1)}, bf16[4,1024,128]{2,1,0:T(8,128)(2,1)}, bf16[4,1024,128]{2,1,0:T(8,128)(2,1)}, bf16[4,1024,128]{2,1,0:T(8,12...) custom-call(f32[1024,1056]{1,0:T(8,128)} %pad_maximum_fusion.raw_ref, ...), custom_call_target="tpu_custom_call" | custom-call | flops 35999997952 | bytes 12000000 | tf_op jit(solution)/shard_map/pallas_call | solution.py:225
  211.3 10.6 %collective-permute-done.18 = bf16[256,352]{1,0:T(8,128)(2,1)S(1)} collective-permute-done((bf16[256,352]{1,0:T(8,128)(2,1)S(1)}, bf16[256,352]{1,0:T(8,128)(2,1)S(1)}, u32[]{:S(2)}, u32[]{:S(2)}) %collective-permute-start.18) | collective-permute-done | bytes 180256 | tf_op jit(solution)/shard_map/ppermute | solution.py:54
  223.7 23.5 %shard_map.352 = (f32[256,1408]{1,0:T(8,128)}, f32[256,1408]{1,0:T(8,128)}, f32[256,1408]{1,0:T(8,128)}, bf16[256,1408]{1,0:T(8,128)(2,1)}, bf16[256,1408]{1,0:T...) custom-call(bf16[256,1408]{1,0:T(8,128)(2,1)} %concatenate.183.mixed_ref.refs_1_, ...), custom_call_target="tpu_custom_call" | custom-call | flops 25999998976 | bytes 24000000 | tf_op jit(solution)/shard_map/pallas_call | solution.py:431
  275.9 9.3 %collective-permute-done.22 = bf16[256,1408]{1,0:T(8,128)(2,1)S(1)} collective-permute-done((bf16[256,1408]{1,0:T(8,128)(2,1)S(1)}, bf16[256,1408]{1,0:T(8,128)(2,1)S(1)}, u32[]{:S(2)}, u32[]{:S(2)}) %collective-permute-start.22) | collective-permute-done | bytes 720928 | tf_op jit(solution)/shard_map/ppermute | solution.py:54
  295.5 5.2 collective-permute-done.24
  306.4 9.7 %collective-permute-done.23 = bf16[256,1408]{1,0:T(8,128)(2,1)S(1)} collective-permute-done((bf16[256,1408]{1,0:T(8,128)(2,1)S(1)}, bf16[256,1408]{1,0:T(8,128)(2,1)S(1)}, u32[]{:S(2)}, u32[]{:S(2)}) %collective-permute-start.23) | collective-permute-done | bytes 720928 | tf_op jit(solution)/shard_map/ppermute | solution.py:54
  322.9 5.9 collective-permute-done.25
  338.9 7.3 shard_map.353.refs_2_
  346.5 7.4 shard_map.354
  355.4 29.5 %shard_map.355 = (bf16[256,1408]{1,0:T(8,128)(2,1)}, bf16[256,1408]{1,0:T(8,128)(2,1)}, bf16[256,1408]{1,0:T(8,128)(2,1)}, f32[256,1408]{1,0:T(8,128)}, bf16[256...) custom-call(f32[256,1408]{1,0:T(8,128)} %convert_add_fusion.1.grad_ref, ...), custom_call_target="tpu_custom_call" | custom-call | flops 32999999488 | bytes 28000000 | tf_op jit(solution)/shard_map/pallas_call | solution.py:513
  418.4 41.7 %shard_map.359 = (bf16[1024,1056]{1,0:T(8,128)(2,1)}, f32[8,128]{1,0:T(8,128)}, f32[8,352]{1,0:T(8,128)}) custom-call(f32[1024,1056]{1,0:T(8,128)} %pad_maximum_fusion.raw_ref, f32[1024,128]{1,0:T(8,128)} %get-tuple-element.330.cos_ref, f32[1024,128]{1,0:T(8,128)} %get-tuple-element.329.sin_a_ref, f32[1024,128]{1,0:T(8,128)} %get-tuple-element.328.sin_b_ref, ...), custom_call_target="tpu_custom_call" | custom-call | flops 46000001024 | bytes 16000000 | tf_op jit(solution)/shard_map/pallas_call | solution.py:322
  481.6 7.4 collective-permute-done.33
  496.0 10.0 %shard_map.360.refs_2_ = bf16[1408,1920]{1,0:T(8,128)(2,1)S(1)} custom-call(bf16[1024,1408]{1,0:T(8,128)(2,1)S(1)} %copy-done.3, bf16[1024,1056]{1,0:T(8,128)(2,1)S(1)} %copy-done.12), custom_call_target="tpu_custom_call" | custom-call | flops 3045064704 | bytes 8019968 | tf_op jit(solution)/shard_map/pallas_call | solution.py:134
  525.6 8.8 %collective-permute-done.35 = bf16[256,1408]{1,0:T(8,128)(2,1)} collective-permute-done((bf16[256,1408]{1,0:T(8,128)(2,1)}, bf16[256,1408]{1,0:T(8,128)(2,1)}, u32[]{:S(2)}, u32[]{:S(2)}) %collective-permute-start.35) | collective-permute-done | bytes 720928 | tf_op jit(solution)/shard_map/ppermute | solution.py:54
  591.0 8.7 %collective-permute-done.36 = bf16[256,1408]{1,0:T(8,128)(2,1)} collective-permute-done((bf16[256,1408]{1,0:T(8,128)(2,1)}, bf16[256,1408]{1,0:T(8,128)(2,1)}, u32[]{:S(2)}, u32[]{:S(2)}) %collective-permute-start.36) | collective-permute-done | bytes 720928 | tf_op jit(solution)/shard_map/ppermute | solution.py:54
  611.9 12.4 %collective-permute-done.37 = bf16[256,1408]{1,0:T(8,128)(2,1)S(1)} collective-permute-done((bf16[256,1408]{1,0:T(8,128)(2,1)S(1)}, bf16[256,1408]{1,0:T(8,128)(2,1)S(1)}, u32[]{:S(2)}, u32[]{:S(2)}) %collective-permute-start.37) | collective-permute-done | bytes 720928 | tf_op jit(solution)/shard_map/ppermute | solution.py:54
  631.1 7.1 collective-permute-done.38
  697.2 9.9 %reduce-scatter.11.cloned.1.call-done = bf16[176,1920]{1,0:T(8,128)(2,1)} async-done(((bf16[1408,1920]{1,0:T(8,128)(2,1)}), bf16[176,1920]{1,0:T(8,128)(2,1)}) %reduce-scatter.11.cloned.1.call-update) | async-done | bytes 675856 | tf_op jit(solution)/shard_map/reduce_scatter | solution.py:753
  709.7 5.6 collective-permute-done.52
  731.5 15.8 %collective-permute-done.55 = bf16[176,736]{1,0:T(8,128)(2,1)} collective-permute-done((bf16[176,736]{1,0:T(8,128)(2,1)}, bf16[176,736]{1,0:T(8,128)(2,1)}, u32[]{:S(2)}, u32[]{:S(2)}) %collective-permute-start.55) | collective-permute-done | bytes 259104 | tf_op jit(solution)/shard_map/ppermute | solution.py:54
  (761 shorter events, 446.2 us)
Async XLA Ops:
  7.2 89.6 %all-gather.4.cloned.1.call-start = ((), (), s32[]{:S(2)}) async-start(), calls=%async_computation.6 | async-start | bytes 14598144 | tf_op jit(solution)/shard_map/all_gather | solution.py:579
  46.1 177.5 %all-gather.6.cloned.1.call-start = ((), (), s32[]{:S(2)}) async-start(), calls=%async_computation.7 | async-start | bytes 13381632 | tf_op jit(solution)/shard_map/all_gather | solution.py:647
  81.2 168.1 %all-gather.8.cloned.1.call-start = ((), (), s32[]{:S(2)}) async-start(), calls=%async_computation.8 | async-start | bytes 9732096 | tf_op jit(solution)/shard_map/all_gather | solution.py:649
  83.5 377.9 %reduce-scatter.5.cloned.1.call-start = ((), (), s32[]{:S(2)}) async-start(), calls=%async_computation.9 | async-start | bytes 9732096 | tf_op jit(solution)/shard_map/reduce_scatter | solution.py:709
  158.5 43.3 %collective-permute-start.14 = (bf16[320,704]{1,0:T(8,128)(2,1)S(1)}, bf16[320,704]{1,0:T(8,128)(2,1)S(1)}, u32[]{:S(2)}, u32[]{:S(2)}) collective-permute-start(bf16[320,704]{1,0:T(8,128)(2,1)S(1)} %pad_maximum_fusion.11), channel_id=1, source_target_pairs={{0,1},{1,2},{2,3},{3,0},{4,5},{5,6},{6,7},{7,4},{8,9},{9,10},{10,1... | collective-permute-start | bytes 1351688 | tf_op jit(solution)/shard_map/ppermute | solution.py:54
  162.9 38.9 %collective-permute-start.15 = (bf16[320,704]{1,0:T(8,128)(2,1)S(1)}, bf16[320,704]{1,0:T(8,128)(2,1)S(1)}, u32[]{:S(2)}, u32[]{:S(2)}) collective-permute-start(bf16[320,704]{1,0:T(8,128)(2,1)S(1)} %pad_maximum_fusion.11), channel_id=1, source_target_pairs={{0,2},{1,3},{2,0},{3,1},{4,6},{5,7},{6,4},{7,5},{8,10},{9,11},{10,... | collective-permute-start | bytes 1351688 | tf_op jit(solution)/shard_map/ppermute | solution.py:54
  162.9 38.9 %collective-permute-start.16 = (bf16[320,704]{1,0:T(8,128)(2,1)S(1)}, bf16[320,704]{1,0:T(8,128)(2,1)S(1)}, u32[]{:S(2)}, u32[]{:S(2)}) collective-permute-start(bf16[320,704]{1,0:T(8,128)(2,1)S(1)} %pad_maximum_fusion.11), channel_id=1, source_target_pairs={{0,3},{1,0},{2,1},{3,2},{4,7},{5,4},{6,5},{7,6},{8,11},{9,8},{10,9... | collective-permute-start | bytes 1351688 | tf_op jit(solution)/shard_map/ppermute | solution.py:54
  223.2 23.9 %collective-permute-start.20 = (bf16[256,1408]{1,0:T(8,128)(2,1)}, bf16[256,1408]{1,0:T(8,128)(2,1)S(1)}, u32[]{:S(2)}, u32[]{:S(2)}) collective-permute-start(bf16[256,1408]{1,0:T(8,128)(2,1)} %collective-permute-done.7), channel_id=1, source_target_pairs={{0,1},{1,2},{2,3},{3,0},{4,5},{5,6},{6,7},{7,4},{8,9},{9,10},{10,1... | collective-permute-start | bytes 2162696 | tf_op jit(solution)/shard_map/ppermute | solution.py:54
  264.4 20.8 %collective-permute-start.22 = (bf16[256,1408]{1,0:T(8,128)(2,1)S(1)}, bf16[256,1408]{1,0:T(8,128)(2,1)S(1)}, u32[]{:S(2)}, u32[]{:S(2)}) collective-permute-start(bf16[256,1408]{1,0:T(8,128)(2,1)S(1)} %collective-permute-done.21), channel_id=1, source_target_pairs={{0,1},{1,2},{2,3},{3,0},{4,5},{5,6},{6,7},{7,4},{8,9},{9,10},{10,1... | collective-permute-start | bytes 2162696 | tf_op jit(solution)/shard_map/ppermute | solution.py:54
  275.8 24.8 %collective-permute-start.24 = (bf16[256,1408]{1,0:T(8,128)(2,1)S(1)}, bf16[256,1408]{1,0:T(8,128)(2,1)S(1)}, u32[]{:S(2)}, u32[]{:S(2)}) collective-permute-start(bf16[256,1408]{1,0:T(8,128)(2,1)S(1)} %convolution_convert_fusion), channel_id=1, source_target_pairs={{0,1},{1,2},{2,3},{3,0},{4,5},{5,6},{6,7},{7,4},{8,9},{9,10},{10,1... | collective-permute-start | bytes 2162696 | tf_op jit(solution)/shard_map/ppermute | solution.py:54
  287.0 29.1 %collective-permute-start.23 = (bf16[256,1408]{1,0:T(8,128)(2,1)S(1)}, bf16[256,1408]{1,0:T(8,128)(2,1)S(1)}, u32[]{:S(2)}, u32[]{:S(2)}) collective-permute-start(bf16[256,1408]{1,0:T(8,128)(2,1)S(1)} %collective-permute-done.22), channel_id=1, source_target_pairs={{0,1},{1,2},{2,3},{3,0},{4,5},{5,6},{6,7},{7,4},{8,9},{9,10},{10,1... | collective-permute-start | bytes 2162696 | tf_op jit(solution)/shard_map/ppermute | solution.py:54
  302.1 26.7 %collective-permute-start.25 = (bf16[256,1408]{1,0:T(8,128)(2,1)S(1)}, bf16[256,1408]{1,0:T(8,128)(2,1)S(1)}, u32[]{:S(2)}, u32[]{:S(2)}) collective-permute-start(bf16[256,1408]{1,0:T(8,128)(2,1)S(1)} %add_convert_fusion.7), channel_id=1, source_target_pairs={{0,1},{1,2},{2,3},{3,0},{4,5},{5,6},{6,7},{7,4},{8,9},{9,10},{10,1... | collective-permute-start | bytes 2162696 | tf_op jit(solution)/shard_map/ppermute | solution.py:54
  329.8 24.0 %collective-permute-start.26 = (bf16[256,1408]{1,0:T(8,128)(2,1)}, bf16[256,1408]{1,0:T(8,128)(2,1)S(1)}, u32[]{:S(2)}, u32[]{:S(2)}) collective-permute-start(bf16[256,1408]{1,0:T(8,128)(2,1)} %add_convert_fusion.6), channel_id=1, source_target_pairs={{0,1},{1,2},{2,3},{3,0},{4,5},{5,6},{6,7},{7,4},{8,9},{9,10},{10,1... | collective-permute-start | bytes 2162696 | tf_op jit(solution)/shard_map/ppermute | solution.py:54
  355.1 184.9 %reduce-scatter.7.cloned.1.call-start = ((), (), s32[]{:S(2)}) async-start(), calls=%async_computation.10 | async-start | bytes 13381632 | tf_op jit(solution)/shard_map/reduce_scatter | solution.py:726
  404.0 287.0 %reduce-scatter.9.cloned.1.call-start = ((), (), s32[]{:S(2)}) async-start(), calls=%async_computation.11 | async-start | bytes 9326592 | tf_op jit(solution)/shard_map/reduce_scatter | solution.py:784
  412.6 47.6 %collective-permute-start.30 = (bf16[320,704]{1,0:T(8,128)(2,1)S(1)}, bf16[320,704]{1,0:T(8,128)(2,1)S(1)}, u32[]{:S(2)}, u32[]{:S(2)}) collective-permute-start(bf16[320,704]{1,0:T(8,128)(2,1)S(1)} %get-tuple-element.262), channel_id=1, source_target_pairs={{0,3},{1,0},{2,1},{3,2},{4,7},{5,4},{6,5},{7,6},{8,11},{9,8},{10,9... | collective-permute-start | bytes 1351688 | tf_op jit(solution)/shard_map/ppermute | solution.py:54
  412.6 47.5 %collective-permute-start.31 = (bf16[320,704]{1,0:T(8,128)(2,1)S(1)}, bf16[320,704]{1,0:T(8,128)(2,1)S(1)}, u32[]{:S(2)}, u32[]{:S(2)}) collective-permute-start(bf16[320,704]{1,0:T(8,128)(2,1)S(1)} %get-tuple-element.264), channel_id=1, source_target_pairs={{0,2},{1,3},{2,0},{3,1},{4,6},{5,7},{6,4},{7,5},{8,10},{9,11},{10,... | collective-permute-start | bytes 1351688 | tf_op jit(solution)/shard_map/ppermute | solution.py:54
  414.6 45.5 %collective-permute-start.32 = (bf16[320,704]{1,0:T(8,128)(2,1)S(1)}, bf16[320,704]{1,0:T(8,128)(2,1)S(1)}, u32[]{:S(2)}, u32[]{:S(2)}) collective-permute-start(bf16[320,704]{1,0:T(8,128)(2,1)S(1)} %get-tuple-element.263), channel_id=1, source_target_pairs={{0,1},{1,2},{2,3},{3,0},{4,5},{5,6},{6,7},{7,4},{8,9},{9,10},{10,1... | collective-permute-start | bytes 1351688 | tf_op jit(solution)/shard_map/ppermute | solution.py:54
  493.8 22.2 %collective-permute-start.34 = (bf16[256,1408]{1,0:T(8,128)(2,1)}, bf16[256,1408]{1,0:T(8,128)(2,1)}, u32[]{:S(2)}, u32[]{:S(2)}) collective-permute-start(bf16[256,1408]{1,0:T(8,128)(2,1)} %get-tuple-element.283), channel_id=1, source_target_pairs={{0,1},{1,2},{2,3},{3,0},{4,5},{5,6},{6,7},{7,4},{8,9},{9,10},{10,1... | collective-permute-start | bytes 2162696 | tf_op jit(solution)/shard_map/ppermute | solution.py:54
  568.4 138.8 %reduce-scatter.11.cloned.1.call-start = ((), (), s32[]{:S(2)}) async-start(), calls=%async_computation.12 | async-start | bytes 6082560 | tf_op jit(solution)/shard_map/reduce_scatter | solution.py:753
  587.1 24.3 %collective-permute-start.40 = (bf16[80,1408]{1,0:T(8,128)(2,1)S(1)}, bf16[80,1408]{1,0:T(8,128)(2,1)S(1)}, u32[]{:S(2)}, u32[]{:S(2)}) collective-permute-start(bf16[80,1408]{1,0:T(8,128)(2,1)S(1)} %add_convert_fusion.13), channel_id=1, source_target_pairs={{0,1},{1,2},{2,3},{3,0},{4,5},{5,6},{6,7},{7,4},{8,9},{9,10},{10,1... | collective-permute-start | bytes 675848 | tf_op jit(solution)/shard_map/ppermute | solution.py:54
  693.4 21.9 %collective-permute-start.52 = (bf16[176,736]{1,0:T(8,128)(2,1)}, bf16[176,736]{1,0:T(8,128)(2,1)S(1)}, u32[]{:S(2)}, u32[]{:S(2)}) collective-permute-start(bf16[176,736]{1,0:T(8,128)(2,1)} %get-tuple-element.286), channel_id=1, source_target_pairs={{0,2},{1,3},{2,0},{3,1},{4,6},{5,7},{6,4},{7,5},{8,10},{9,11},{10,... | collective-permute-start | bytes 777224 | tf_op jit(solution)/shard_map/ppermute | solution.py:54
  721.4 25.8 %collective-permute-start.55 = (bf16[176,736]{1,0:T(8,128)(2,1)}, bf16[176,736]{1,0:T(8,128)(2,1)}, u32[]{:S(2)}, u32[]{:S(2)}) collective-permute-start(bf16[176,736]{1,0:T(8,128)(2,1)} %add_convert_fusion.11), channel_id=1, source_target_pairs={{0,2},{1,3},{2,0},{3,1},{4,6},{5,7},{6,4},{7,5},{8,10},{9,11},{10,... | collective-permute-start | bytes 777224 | tf_op jit(solution)/shard_map/ppermute | solution.py:54
  728.3 22.4 %collective-permute-start.56 = (bf16[176,736]{1,0:T(8,128)(2,1)}, bf16[176,736]{1,0:T(8,128)(2,1)}, u32[]{:S(2)}, u32[]{:S(2)}) collective-permute-start(bf16[176,736]{1,0:T(8,128)(2,1)} %add_convert_fusion.11), channel_id=1, source_target_pairs={{0,3},{1,0},{2,1},{3,2},{4,7},{5,4},{6,5},{7,6},{8,11},{9,8},{10,9... | collective-permute-start | bytes 777224 | tf_op jit(solution)/shard_map/ppermute | solution.py:54
  (204 other events, 1935.9 us)
Sparse Core Ops, SparseCore 0:
  11.9 76.0 all-gather.3
  89.9 69.0 all-gather.5
  161.5 55.6 all-gather.7
  355.3 74.2 reduce-scatter.4
  433.3 89.8 reduce-scatter.6
  568.5 76.5 reduce-scatter.8
  649.0 58.1 reduce-scatter.10

commit v3 on v2

v3 whole, which is shorter than its diff:
```python
import functools
import math

import jax
import jax.numpy as jnp
import numpy as np
from jax import lax
from jax.experimental import pallas as pl
from jax.experimental.pallas import tpu as pltpu
from jax.sharding import PartitionSpec as P

HEADS = 16
HD = 88
LANES = 128
EPSILON = 1e-06
HIGHEST = lax.Precision.HIGHEST
FLOAT = jnp.float32
BFLOAT = jnp.bfloat16
LOG2E = 1.4426950408889634
SCALE = 1.0 / math.sqrt(HD)


def layer_norm(values, norm_gain, norm_bias):
    centred = values - jnp.mean(values, axis=-1, keepdims=True)
    variance = jnp.mean(centred * centred, axis=-1, keepdims=True)
    return centred * lax.rsqrt(variance + EPSILON) * norm_gain + norm_bias


def head_norm(values, norm_gain):
    centred = values - jnp.mean(values, axis=-1, keepdims=True)
    variance = jnp.mean(centred * centred, axis=-1, keepdims=True)
    return centred * lax.rsqrt(variance + EPSILON) * norm_gain


def silu(values):
    return values / (1.0 + jnp.exp(-values))


def gelu(values):
    inner = math.sqrt(2.0 / math.pi) * (values + 0.044715 * values * values * values)
    return 0.5 * values * (1.0 + jnp.tanh(inner))


def dot(left, right, contract=((1,), (0,))):
    return lax.dot_general(left, right, (contract, ((), ())), preferred_element_type=FLOAT)


NT = ((1,), (1,))
TN = ((0,), (0,))


def rot(values, step):
    count = lax.axis_size("tensor")
    return lax.ppermute(values, "tensor", [(i, (i + step) % count) for i in range(count)])


def ring_gather(own):
    blocks = [own]
    for _ in range(lax.axis_size("tensor") - 1):
        blocks.append(rot(blocks[-1], 1))
    return blocks


def ring_scatter(parts):
    running = parts[1].astype(BFLOAT)
    for part in parts[2:]:
        running = (rot(running, 1).astype(FLOAT) + part.astype(FLOAT)).astype(BFLOAT)
    return rot(running, 1).astype(FLOAT) + parts[0].astype(FLOAT)


def direct_gather(own):
    return [own] + [rot(own, r) for r in range(1, lax.axis_size("tensor"))]


def direct_scatter(parts):
    count = len(parts)
    total = parts[0].astype(FLOAT)
    for r in range(1, count):
        total = total + rot(parts[r], count - r).astype(FLOAT)
    return total


def exchange(parts):
    count = len(parts)
    return [parts[0]] + [rot(parts[count - r], r) for r in range(1, count)]


def after(values, *earlier):
    return lax.optimization_barrier((values, *earlier))[0]


def small_gather(own):
    have = own[None]
    me = lax.axis_index("dp")
    count = lax.axis_size("dp")
    step = 1
    while step < count:
        other = lax.ppermute(have, "dp", [(i, i ^ step) for i in range(count)])
        upper = (me // step) % 2 == 1
        have = jnp.where(upper, jnp.concatenate([other, have]), jnp.concatenate([have, other]))
        step *= 2
    return have


def tensor_sum(values):
    total = values.astype(FLOAT)
    for step in range(1, lax.axis_size("tensor")):
        total = total + rot(values, step).astype(FLOAT)
    return total


def grad_kernel(lefts, rights, turned, *refs):
    left_refs, right_refs = refs[:lefts], refs[lefts : lefts + rights]
    out_ref, kept_ref = refs[-2], refs[-1]
    rows = left_refs[0].shape[0]

    @pl.when(pl.program_id(0) == 0)
    def _():
        for r in range(lefts):
            kept_ref[:, r * rows : (r + 1) * rows] = left_refs[r][...].T

    total = None
    for r in range(rights):
        span = lefts // rights * rows
        left = kept_ref[:, r * span : (r + 1) * span]
        term = dot(left, right_refs[r][...], NT if turned else ((1,), (0,)))
        total = term if total is None else total + term
    out_ref[...] = total.astype(BFLOAT)


def pack_grad(packed, lefts, rights, lanes, start, tile, turned=False):
    rows, height = lefts[0].shape
    deep = rights[0].shape[1 if turned else 0]
    wide = rights[0].shape[0 if turned else 1]
    first = start // tile
    in_specs = [pl.BlockSpec((rows, height), lambda i: (0, 0))] * len(lefts)
    if turned:
        in_specs += [pl.BlockSpec((tile, deep), lambda i: (i, 0))] * len(rights)
    else:
        in_specs += [pl.BlockSpec((deep, tile), lambda i: (0, i))] * len(rights)
    operands = [*lefts, *rights]
    if packed is not None:
        in_specs.append(pl.BlockSpec(memory_space=pl.ANY))
        operands.append(packed)
    tokens = rows * len(lefts)
    return pl.pallas_call(
        functools.partial(grad_kernel, len(lefts), len(rights), turned),
        grid=(pl.cdiv(wide, tile),),
        in_specs=in_specs,
        out_specs=pl.BlockSpec((height, tile), lambda i: (0, first + i)),
        out_shape=jax.ShapeDtypeStruct((height, lanes), BFLOAT),
        scratch_shapes=[pltpu.VMEM((height, tokens), BFLOAT)],
        input_output_aliases={} if packed is None else {len(operands) - 1: 0},
        compiler_params=pltpu.CompilerParams(vmem_limit_bytes=40 * 2**20),
        cost_estimate=pl.CostEstimate(
            flops=4 * tokens * height * wide,
            bytes_accessed=2 * (tokens * height + tokens * wide + height * wide),
            transcendentals=0,
        ),
    )(*operands)


def flipped(index, bit):
    return index + (1 - 2 * lax.rem(lax.div(index, 2**bit), 2)) * 2**bit


def to_device(source, target, send, recv, where):
    return pltpu.make_async_remote_copy(
        src_ref=source,
        dst_ref=target,
        send_sem=send,
        recv_sem=recv,
        device_id=where,
        device_id_type=pl.DeviceIdType.MESH,
    )


def neighbours(place, split):
    return lax.rem(place + 1, split), lax.rem(place + split - 1, split)


def ring_kernel(split, start, raw_ref, packed_ref, sum_out, shift_out, weights_ref, sent, got, load_sem, sems):
    load = pltpu.make_async_copy(packed_ref.at[:, start : start + weights_ref.shape[1]], weights_ref, load_sem.at[0])
    load.start()
    place = lax.axis_index("tensor")
    right, left = neighbours(place, split)
    barrier = pltpu.get_barrier_semaphore()
    for where in (left, right):
        pl.semaphore_signal(barrier, inc=1, device_id={"tensor": where}, device_id_type=pl.DeviceIdType.MESH)
    rows = sum_out.shape[0]

    def term(r):
        return dot(weights_ref[...], raw_ref[:, r * rows : (r + 1) * rows]).T

    def hop(step):
        return to_device(sent.at[step], got.at[step], sems.at[0, step], sems.at[1, step], {"tensor": right})

    load.wait()
    part = term(1)
    total = jnp.sum(part, axis=0, keepdims=True)
    sent[0] = part.astype(BFLOAT)
    pl.semaphore_wait(barrier, 2)
    hop(0).start()
    for step in range(1, split):
        part = term((step + 1) % split)
        total = total + jnp.sum(part, axis=0, keepdims=True)
        hop(step - 1).wait_recv()
        part = part + got[step - 1].astype(FLOAT)
        if step + 1 < split:
            sent[step] = part.astype(BFLOAT)
            hop(step).start()
        else:
            sum_out[...] = part
    shift_out[...] = jnp.broadcast_to(total, shift_out.shape)
    for step in range(split - 1):
        hop(step).wait_send()


def ring_sum(raw, packed, start, split):
    rows, width = raw.shape[1] // split, packed.shape[0]
    vmem = pl.BlockSpec(memory_space=pltpu.VMEM)
    return pl.pallas_call(
        functools.partial(ring_kernel, split, start),
        in_specs=[vmem, pl.BlockSpec(memory_space=pl.ANY)],
        out_specs=(vmem,) * 2,
        out_shape=(jax.ShapeDtypeStruct((rows, width), FLOAT), jax.ShapeDtypeStruct((8, width), FLOAT)),
        scratch_shapes=[
            pltpu.VMEM((width, raw.shape[0]), BFLOAT),
            pltpu.VMEM((split - 1, rows, width), BFLOAT),
            pltpu.VMEM((split - 1, rows, width), BFLOAT),
            pltpu.SemaphoreType.DMA((1,)),
            pltpu.SemaphoreType.DMA((2, split - 1)),
        ],
        compiler_params=pltpu.CompilerParams(
            vmem_limit_bytes=40 * 2**20, collective_id=1, has_side_effects=True
        ),
        cost_estimate=pl.CostEstimate(flops=60_000_000_000, bytes_accessed=10_000_000, transcendentals=0),
    )(raw, packed)


def skip_kernel(
    grad_ref, two_ref, one_ref, gain_ref, left_ref, packed_ref, out_ref, low_ref, rows_ref
):
    @pl.when(pl.program_id(0) == 0)
    def _():
        into, gain_grad, bias_grad = norm_rows_back(one_ref[...], gain_ref[...], grad_ref[...])
        grad_one = two_ref[...] + into
        low_ref[...] = grad_one.astype(BFLOAT)
        rows_ref[...] = jnp.concatenate(
            [gain_grad, bias_grad, jnp.sum(grad_one, axis=0, keepdims=True), jnp.zeros((5, grad_one.shape[1]), FLOAT)],
            axis=0,
        )

    out_ref[...] = dot(left_ref[...].T, low_ref[...]).astype(BFLOAT)


def skip_grads(packed, grad, two, one, gain, left):
    rows, width = one.shape
    fixed = pl.BlockSpec((rows, width), lambda i: (0, 0))
    return pl.pallas_call(
        skip_kernel,
        grid=(left.shape[1] // width,),
        in_specs=[fixed] * 3
        + [
            pl.BlockSpec((1, width), lambda i: (0, 0)),
            pl.BlockSpec((rows, width), lambda i: (0, i)),
            pl.BlockSpec(memory_space=pl.ANY),
        ],
        out_specs=(
            pl.BlockSpec((width, width), lambda i: (0, i)),
            pl.BlockSpec((rows, width), lambda i: (0, 0)),
            pl.BlockSpec((8, width), lambda i: (0, 0)),
        ),
        out_shape=(
            jax.ShapeDtypeStruct(packed.shape, BFLOAT),
            jax.ShapeDtypeStruct((rows, width), BFLOAT),
            jax.ShapeDtypeStruct((8, width), FLOAT),
        ),
        input_output_aliases={5: 0},
        compiler_params=pltpu.CompilerParams(vmem_limit_bytes=40 * 2**20),
        cost_estimate=pl.CostEstimate(flops=10_000_000_000, bytes_accessed=16_000_000, transcendentals=0),
    )(grad, two, one, gain, left, packed)


def side_kernel(shards, split, hops, *refs):
    low_ref, late_ref, shift_ref, table_ref, latent_ref, skip_ref, base_ref, hop_ref, summed_ref, ckv_ref = refs[:10]
    weights_ref, refs = refs[10], refs[11:]
    out_refs, refs = refs[: hops + 1], refs[hops + 1 :]
    latent_out, skip_out, table_out, full_out, text_out, block_out = refs[:6]
    weights, text_weights, full_refs, text_refs, full_got, text_got, hop_sent, hop_got, table_sent, table_got = refs[6:16]
    load_sem, side_sems, hop_sems, table_sems = refs[16:]
    me, place = lax.axis_index("dp"), lax.axis_index("tensor")
    count = shards.bit_length() - 1
    width = latent_out.shape[1]
    part = width // shards
    right, _ = neighbours(place, split)

    loads = [
        pltpu.make_async_copy(weights_ref.at[:, half * width : (half + 1) * width], weights, load_sem.at[half])
        for half in range(2)
    ]
    text_wide = text_weights.shape[1]
    text_start = weights_ref.shape[1] - text_wide
    loads.append(pltpu.make_async_copy(weights_ref.at[:, text_start:], text_weights, load_sem.at[2]))
    loads[0].start()
    loads[2].start()
    barrier = pltpu.get_barrier_semaphore()
    for bit in range(count):
        pl.semaphore_signal(barrier, inc=1, device_id={"dp": flipped(me, bit)}, device_id_type=pl.DeviceIdType.MESH)
    for step in range(1, split):
        pl.semaphore_signal(
            barrier, inc=1, device_id={"tensor": lax.rem(place + step, split)}, device_id_type=pl.DeviceIdType.MESH
        )

    def side(step, i):
        return to_device(
            (full_refs, text_refs)[i].at[step],
            (full_got, text_got)[i].at[step - 1],
            side_sems.at[i, 0, step - 1],
            side_sems.at[i, 1, step - 1],
            {"tensor": lax.rem(place + split - step, split)},
        )

    def hop(step):
        return to_device(
            hop_sent.at[step], hop_got.at[step], hop_sems.at[0, step], hop_sems.at[1, step], {"tensor": right}
        )

    hop_sent[0] = (hop_ref[...].astype(FLOAT) + out_refs[1][...]).astype(BFLOAT)
    pl.semaphore_wait(barrier, count + split - 1)
    hop(0).start()
    low = low_ref[...]
    grads = []
    for half in range(2):
        loads[half].wait()
        grads.append(dot(low, weights[...], NT))
        if half == 0:
            loads[1].start()
    ordered = [grads[half][:, shard * part : (shard + 1) * part] for shard in range(shards) for half in range(2)]
    grads = [jnp.concatenate(ordered[:shards], axis=1), jnp.concatenate(ordered[shards:], axis=1)]
    values = [latent_ref[...].astype(FLOAT), skip_ref[...].astype(FLOAT)]

    def mean_of(one, two):
        return (jnp.sum(one, axis=-1, keepdims=True) + jnp.sum(two, axis=-1, keepdims=True)) * (0.5 / width)

    mean = mean_of(*values)
    centred = [item - mean for item in values]
    inverse = lax.rsqrt(mean_of(*[item * item for item in centred]) + EPSILON)
    normed = [item * inverse for item in centred]
    gain_rows = [jnp.sum(grads[i] * normed[i], axis=0, keepdims=True) for i in range(2)]
    bias_rows = [jnp.sum(grads[i], axis=0, keepdims=True) for i in range(2)]
    scaled = [grads[i] * table_ref[i : i + 1, :] for i in range(2)]
    mean = mean_of(*scaled)
    slope = mean_of(*[scaled[i] * normed[i] for i in range(2)])
    latent_out[...] = inverse * (scaled[0] - mean - normed[0] * slope)
    skip_out[...] = inverse * (scaled[1] - mean - normed[1] * slope)

    spare = table_out.shape[0] - 8
    table_sent[0] = jnp.concatenate(
        [
            *gain_rows,
            *bias_rows,
            late_ref[2:3, :],
            late_ref[0:2, :],
            shift_ref[0:1, :],
            jnp.zeros((spare, width), FLOAT),
        ],
        axis=0,
    )
    bits = split.bit_length() - 1
    shares = table_sent.shape[0]

    def share(step):
        where = {"tensor": flipped(place, step)} if step < bits else {"dp": flipped(me, step - bits)}
        return to_device(
            table_sent.at[step], table_got.at[step], table_sems.at[0, step], table_sems.at[1, step], where
        )

    def open_hop(step):
        hop(step - 1).wait_recv()
        hop_sent[step] = (hop_got[step - 1].astype(FLOAT) + out_refs[step + 1][...]).astype(BFLOAT)
        hop(step).start()

    def pass_on(step):
        share(step).wait_recv()
        total = table_sent[step] + table_got[step]
        if step + 1 == bits:
            at = lax.broadcasted_iota(jnp.int32, (8 + spare, 1), 0)
            total = jnp.where(at == 8 + me, total[7:8, :], total)
        if step + 1 < shares:
            table_sent[step + 1] = total
            share(step + 1).start()
        else:
            table_out[...] = total
    share(0).start()
    span = full_out.shape[1] // 3
    for r in range(split):
        full_refs[r] = jnp.concatenate(
            [summed_ref[:, k * width + r * span : k * width + (r + 1) * span] for k in range(3)], axis=1
        )
    for step in range(bits):
        pass_on(step)
    for step in range(1, split):
        side(step, 0).start()
    loads[2].wait()
    back = dot(ckv_ref[...], text_weights[...], NT).astype(BFLOAT)
    own_text = text_out.shape[0]
    for r in range(split):
        text_refs[r] = back[r * own_text : (r + 1) * own_text]
    for step in range(1, split):
        side(step, 1).start()
    for step in range(1, hops):
        open_hop(step)
    for step in range(bits, shares):
        pass_on(step)
    for i, (terms, result) in enumerate(((full_refs, full_out), (text_refs, text_out))):
        if i == 1:
            hop(hops - 1).wait_recv()
            last = hop_got[hops - 1].astype(FLOAT) + out_refs[0][...]
            block_out[...] = (base_ref[...] + table_ref[2:3, :] + last).astype(BFLOAT)
        total = terms[0].astype(FLOAT)
        for step in range(1, split):
            side(step, i).wait_recv()
            total = total + (full_got, text_got)[i][step - 1].astype(FLOAT)
        result[...] = total
    for step in range(hops):
        hop(step).wait_send()
    for step in range(shares):
        share(step).wait_send()
    for step in range(1, split):
        for i in range(2):
            side(step, i).wait_send()


def side_sums(low, late, shift, table, latent, skip_in, base, hop, summed, ckv, weights, out, shards, split):
    rows, width = low.shape
    spare = pl.cdiv(shards, 8) * 8
    shares = shards.bit_length() - 1 + split.bit_length() - 1
    vmem = pl.BlockSpec(memory_space=pltpu.VMEM)
    wide = jax.ShapeDtypeStruct((rows, width), FLOAT)
    hops = len(out) - 1
    full, text = (summed.shape[0], summed.shape[1] // split), (ckv.shape[0] // split, width)
    return pl.pallas_call(
        functools.partial(side_kernel, shards, split, hops),
        in_specs=[vmem] * 10 + [pl.BlockSpec(memory_space=pl.ANY)] + [vmem] * len(out),
        out_specs=(vmem,) * 6,
        out_shape=(
            wide,
            wide,
            jax.ShapeDtypeStruct((8 + spare, width), FLOAT),
            jax.ShapeDtypeStruct(full, FLOAT),
            jax.ShapeDtypeStruct(text, FLOAT),
            jax.ShapeDtypeStruct((rows, width), BFLOAT),
        ),
        scratch_shapes=[
            pltpu.VMEM((width, width), BFLOAT),
            pltpu.VMEM((width, ckv.shape[1]), BFLOAT),
            pltpu.VMEM((split, *full), BFLOAT),
            pltpu.VMEM((split, *text), BFLOAT),
            pltpu.VMEM((split - 1, *full), BFLOAT),
            pltpu.VMEM((split - 1, *text), BFLOAT),
            pltpu.VMEM((hops, rows, width), BFLOAT),
            pltpu.VMEM((hops, rows, width), BFLOAT),
            pltpu.VMEM((shares, 8 + spare, width), FLOAT),
            pltpu.VMEM((shares, 8 + spare, width), FLOAT),
            pltpu.SemaphoreType.DMA((3,)),
            pltpu.SemaphoreType.DMA((2, 2, split - 1)),
            pltpu.SemaphoreType.DMA((2, hops)),
            pltpu.SemaphoreType.DMA((2, shares)),
        ],
        compiler_params=pltpu.CompilerParams(
            vmem_limit_bytes=56 * 2**20, collective_id=0, has_side_effects=True
        ),
        cost_estimate=pl.CostEstimate(flops=90_000_000_000, bytes_accessed=30_000_000, transcendentals=0),
    )(low, late, shift, table, latent, skip_in, base, hop, summed, ckv, weights, *out)


def spread_kernel(split, starts, in_ref, skip_out, small_out, piece_sent, piece_got, pieces, whole, sems):
    place = lax.axis_index("tensor")
    part, width = skip_out.shape[0] // 2, skip_out.shape[1]
    wide = piece_sent.shape[2]
    barrier = pltpu.get_barrier_semaphore()
    for step in range(1, split):
        pl.semaphore_signal(
            barrier, inc=1, device_id={"tensor": lax.rem(place + step, split)}, device_id_type=pl.DeviceIdType.MESH
        )
    for i in range(split):
        piece_sent[i] = in_ref[:, starts[i] : starts[i] + wide]
    pl.semaphore_wait(barrier, split - 1)

    def scatter(step):
        where = lax.rem(place + step, split)
        return to_device(
            piece_sent.at[where], piece_got.at[step - 1], sems.at[0, step - 1], sems.at[1, step - 1], {"tensor": where}
        )

    def gather(step):
        return to_device(
            pieces.at[place], pieces.at[place], sems.at[2, step - 1], sems.at[3, step - 1],
            {"tensor": lax.rem(place + step, split)},
        )

    for step in range(1, split):
        scatter(step).start()
    total = piece_sent[place].astype(FLOAT)
    for step in range(1, split):
        scatter(step).wait_recv()
        total = total + piece_got[step - 1].astype(FLOAT)
    pieces[place] = total.astype(BFLOAT)
    for step in range(1, split):
        gather(step).start()
    for step in range(1, split):
        gather(step).wait_recv()
    for i in range(split):
        stop = starts[i + 1] if i + 1 < split else whole.shape[1]
        whole[:, starts[i] : stop] = pieces[i][:, : stop - starts[i]].astype(FLOAT)
    skip_out[:part] = whole[:, :width]
    skip_out[part:] = whole[:, width : 2 * width]
    small_out[...] = whole[:, 2 * width :]
    for step in range(1, split):
        scatter(step).wait_send()
        gather(step).wait_send()


def spread_sum(values, width, split):
    part, lanes = values.shape
    wide = pl.cdiv(lanes // LANES, split) * LANES
    starts = [min(i * wide, lanes - wide) for i in range(split)]
    vmem = pl.BlockSpec(memory_space=pltpu.VMEM)
    return pl.pallas_call(
        functools.partial(spread_kernel, split, starts),
        in_specs=[vmem],
        out_specs=(vmem,) * 2,
        out_shape=(
            jax.ShapeDtypeStruct((2 * part, width), FLOAT),
            jax.ShapeDtypeStruct((part, lanes - 2 * width), FLOAT),
        ),
        scratch_shapes=[
            pltpu.VMEM((split, part, wide), BFLOAT),
            pltpu.VMEM((split - 1, part, wide), BFLOAT),
            pltpu.VMEM((split, part, wide), BFLOAT),
            pltpu.VMEM((part, lanes), FLOAT),
            pltpu.SemaphoreType.DMA((4, split - 1)),
        ],
        compiler_params=pltpu.CompilerParams(
            vmem_limit_bytes=30 * 2**20, collective_id=2, has_side_effects=True
        ),
        cost_estimate=pl.CostEstimate(flops=40_000_000_000, bytes_accessed=4_000_000, transcendentals=0),
    )(values)


def text_kernel(parts, *refs):
    term_refs, (raw_ref, gain_ref, group_ref, low_ref, rows_ref) = refs[:parts], refs[parts:]
    span = gain_ref.shape[1]
    total = term_refs[0][...].astype(FLOAT)
    for ref in term_refs[1:]:
        total = total + ref[...].astype(FLOAT)
    group = group_ref[...]
    normed, inverse = norm_heads(raw_ref[:, :span], group)
    grad = total[:, :span]
    gain_grad = jnp.sum(grad * normed, axis=0, keepdims=True)
    grad = grad * gain_ref[...]
    grad = inverse * (grad - head_means(grad, group) - normed * head_means(grad * normed, group))
    low = jnp.concatenate([grad, total[:, span:]], axis=1).astype(BFLOAT)
    low_ref[...] = low
    zeros = jnp.zeros((1, span), FLOAT)
    rows_ref[...] = jnp.concatenate(
        [
            jnp.sum(low.astype(FLOAT), axis=0, keepdims=True),
            jnp.concatenate([gain_grad, zeros], axis=1),
            jnp.zeros((6, 2 * span), FLOAT),
        ],
        axis=0,
    )


def text_norm_back(terms, raw, gain, group):
    return pl.pallas_call(
        functools.partial(text_kernel, len(terms)),
        out_shape=(
            jax.ShapeDtypeStruct(terms[0].shape, BFLOAT),
            jax.ShapeDtypeStruct((8, terms[0].shape[1]), FLOAT),
        ),
        compiler_params=pltpu.CompilerParams(vmem_limit_bytes=30 * 2**20),
        cost_estimate=pl.CostEstimate(flops=5_000_000_000, bytes_accessed=4_000_000, transcendentals=0),
    )(*terms, raw, gain, group)


QUARTER = 24
DEEP = 4 * QUARTER


def expansion(heads):
    result = np.zeros((3 * heads * HD, 3 * heads * DEEP), np.float32)
    for part in range(3):
        for head in range(heads):
            for channel in range(HD):
                quarter = HD // 4
                place = channel if part == 2 else channel // quarter * QUARTER + channel % quarter
                result[(part * heads + head) * HD + channel, (part * heads + head) * DEEP + place] = 1.0
    return result


def real_rows():
    rows = lax.broadcasted_iota(jnp.int32, (DEEP, 1), 0)
    return (lax.rem(rows, QUARTER) < HD // 4).astype(FLOAT)


def norm_deep(values, mask):
    mean = jnp.sum(values, axis=0, keepdims=True) * (1.0 / HD)
    centred = (values - mean) * mask
    inverse = lax.rsqrt(jnp.sum(centred * centred, axis=0, keepdims=True) * (1.0 / HD) + EPSILON)
    return centred * inverse, inverse


def turn_deep(values, row_cos, row_sin, col_cos, col_sin):
    one, two, three, four = (values[i * QUARTER : (i + 1) * QUARTER] for i in range(4))
    return jnp.concatenate(
        [
            one * row_cos - two * row_sin,
            two * row_cos + one * row_sin,
            three * col_cos - four * col_sin,
            four * col_cos + three * col_sin,
        ],
        axis=0,
    )


def full_tile(values):
    return jnp.concatenate([values, jnp.zeros((LANES - DEEP, values.shape[1]), values.dtype)], axis=0)


def attend_forward_kernel(heads, parts, block, *refs):
    raw_refs, refs = refs[:parts], refs[parts:]
    turn_ref, gain_ref, refs = refs[0], refs[1], refs[2:]
    o_refs, (oturn_ref, qturn_ref, kturn_ref, k_ref, v_ref, lse_ref, vturn_ref) = refs[:parts], refs[parts:]
    rows = raw_refs[0].shape[1]
    length = parts * rows
    mask = real_rows()
    for r in range(parts):
        here = slice(r * rows, (r + 1) * rows)

        def prepare(head, carry):
            tables = [turn_ref[i, :, here] for i in range(4)]
            turned = []
            for part in range(2):
                at = pl.ds((part * heads + head) * DEEP, DEEP)
                normed, _ = norm_deep(raw_refs[r][at, :], mask)
                turned.append(full_tile(turn_deep(normed * gain_ref[at, :], *tables)))
            qturn_ref[head, :, here] = turned[0].astype(BFLOAT)
            kturn_ref[head, :, here] = turned[1].astype(BFLOAT)
            k_ref[head, here, :] = turned[1].T.astype(BFLOAT)
            values = full_tile(raw_refs[r][pl.ds((2 * heads + head) * DEEP, DEEP), :])
            vturn_ref[head, :, here] = values.astype(BFLOAT)
            v_ref[head, here, :] = values.T.astype(BFLOAT)
            return carry

        lax.fori_loop(0, heads, prepare, 0)
    for head in range(heads):
        for index in range(length // block):
            here = slice(index * block, (index + 1) * block)
            scores = dot(k_ref[head], qturn_ref[head, :, here])
            peak = jnp.max(scores, axis=0, keepdims=True)
            powers = jnp.exp2((scores - peak) * (SCALE * LOG2E))
            total = jnp.sum(powers, axis=0, keepdims=True)
            mixed = dot(vturn_ref[head], powers.astype(BFLOAT)) / total
            oturn_ref[head, :, here] = mixed.astype(BFLOAT)
            lse_ref[head, :, here] = peak * (SCALE * LOG2E) + jnp.log2(total)
    for r in range(parts):
        here = slice(r * rows, (r + 1) * rows)
        o_refs[r][...] = jnp.concatenate(
            [oturn_ref[head, :, here].astype(FLOAT).T[:, :HD] for head in range(heads)], axis=1
        ).astype(BFLOAT)


def attend_forward(raws, turns, gains, heads, block):
    rows = raws[0].shape[1]
    length = rows * len(raws)
    tall = jax.ShapeDtypeStruct((heads, LANES, length), BFLOAT)
    long = jax.ShapeDtypeStruct((heads, length, LANES), BFLOAT)
    return pl.pallas_call(
        functools.partial(attend_forward_kernel, heads, len(raws), block),
        out_shape=(
            *[jax.ShapeDtypeStruct((rows, heads * HD), BFLOAT) for _ in raws],
            tall,
            tall,
            tall,
            long,
            long,
            jax.ShapeDtypeStruct((heads, 1, length), FLOAT),
        ),
        scratch_shapes=[pltpu.VMEM((heads, LANES, length), BFLOAT)],
        compiler_params=pltpu.CompilerParams(vmem_limit_bytes=56 * 2**20),
        cost_estimate=pl.CostEstimate(flops=20_000_000_000, bytes_accessed=12_000_000, transcendentals=4_200_000),
    )(*raws, turns, gains)


def attend_backward_kernel(heads, parts, block, *refs):
    raw_refs, refs = refs[:parts], refs[parts:]
    turn_ref, gain_ref, oturn_ref, qturn_ref, kturn_ref, k_ref, v_ref, lse_ref = refs[:8]
    do_refs = refs[8 : 8 + parts]
    graw_ref, gain_out_ref, sums_ref, dturn_ref, dq_ref, dk_ref, dv_ref = refs[8 + parts :]
    rows = raw_refs[0].shape[1]
    length = parts * rows
    count = length // block
    mask = real_rows()
    for r in range(parts):
        here = slice(r * rows, (r + 1) * rows)
        values = do_refs[r][...].astype(FLOAT)
        for head in range(heads):
            wide = jnp.concatenate(
                [values[:, head * HD : (head + 1) * HD], jnp.zeros((rows, LANES - HD), FLOAT)], axis=1
            )
            dturn_ref[head, :, here] = wide.T.astype(BFLOAT)

    def attend(head, carry):
        for index in range(count):
            here = slice(index * block, (index + 1) * block)
            queries, grad = qturn_ref[head, :, here], dturn_ref[head, :, here]
            probs = jnp.exp2(dot(k_ref[head], queries) * (SCALE * LOG2E) - lse_ref[head, :, here])
            inner = jnp.sum(grad.astype(FLOAT) * oturn_ref[head, :, here].astype(FLOAT), axis=0, keepdims=True)
            grad_scores = (probs * (dot(v_ref[head], grad) - inner)).astype(BFLOAT)
            add_v = dot(grad, probs.astype(BFLOAT), NT)
            add_k = dot(queries, grad_scores, NT)
            dq_ref[head, :, here] = dot(kturn_ref[head], grad_scores)
            if index == 0:
                dv_ref[head] = add_v
                dk_ref[head] = add_k
            else:
                dv_ref[head] += add_v
                dk_ref[head] += add_k
        return carry

    lax.fori_loop(0, heads, attend, 0)
    gain_out_ref[...] = jnp.zeros_like(gain_out_ref)
    sums_ref[...] = jnp.zeros_like(sums_ref)

    def narrow(values):
        return sum(values[:, i * LANES : (i + 1) * LANES] for i in range(values.shape[1] // LANES))

    for r in range(parts):
        here = slice(r * rows, (r + 1) * rows)

        def finish(head, carry):
            row_cos, row_sin, col_cos, col_sin = (turn_ref[i, :, here] for i in range(4))
            for part, grad_ref in ((0, dq_ref), (1, dk_ref)):
                at = pl.ds((part * heads + head) * DEEP, DEEP)
                normed, inverse = norm_deep(raw_refs[r][at, :], mask)
                grad = turn_deep(grad_ref[head, :DEEP, here] * SCALE, row_cos, -row_sin, col_cos, -col_sin)
                gain_out_ref[at, :] += narrow(grad * normed)
                grad = grad * gain_ref[at, :]
                mean = jnp.sum(grad, axis=0, keepdims=True) * (1.0 / HD)
                slope = jnp.sum(grad * normed, axis=0, keepdims=True) * (1.0 / HD)
                low = ((inverse * (grad - mean - normed * slope)) * mask).astype(BFLOAT)
                graw_ref[at, here] = low
                sums_ref[at, :] += narrow(low.astype(FLOAT))
            at = pl.ds((2 * heads + head) * DEEP, DEEP)
            low = dv_ref[head, :DEEP, here].astype(BFLOAT)
            graw_ref[at, here] = low
            sums_ref[at, :] += narrow(low.astype(FLOAT))
            return carry

        lax.fori_loop(0, heads, finish, 0)


def attend_backward(raws, turns, gains, kept, grad_out, heads, block):
    length = raws[0].shape[1] * len(raws)
    return pl.pallas_call(
        functools.partial(attend_backward_kernel, heads, len(raws), block),
        out_shape=(
            jax.ShapeDtypeStruct((3 * heads * DEEP, length), BFLOAT),
            jax.ShapeDtypeStruct((2 * heads * DEEP, LANES), FLOAT),
            jax.ShapeDtypeStruct((3 * heads * DEEP, LANES), FLOAT),
        ),
        scratch_shapes=[
            pltpu.VMEM((heads, LANES, length), BFLOAT),
            pltpu.VMEM((heads, LANES, length), FLOAT),
            pltpu.VMEM((heads, LANES, length), FLOAT),
            pltpu.VMEM((heads, LANES, length), FLOAT),
        ],
        compiler_params=pltpu.CompilerParams(vmem_limit_bytes=56 * 2**20),
        cost_estimate=pl.CostEstimate(flops=28_000_000_000, bytes_accessed=16_000_000, transcendentals=4_200_000),
    )(*raws, turns, gains, *kept, *grad_out)


def norm_rows(values):
    count = values.shape[-1]
    mean = jnp.sum(values, axis=-1, keepdims=True) * (1.0 / count)
    centred = values - mean
    inverse = lax.rsqrt(jnp.sum(centred * centred, axis=-1, keepdims=True) * (1.0 / count) + EPSILON)
    return centred * inverse, inverse


def norm_rows_back(values, gain, grad):
    normed, inverse = norm_rows(values)
    count = values.shape[-1]
    gain_grad = jnp.sum(grad * normed, axis=0, keepdims=True)
    bias_grad = jnp.sum(grad, axis=0, keepdims=True)
    grad = grad * gain
    mean = jnp.sum(grad, axis=-1, keepdims=True) * (1.0 / count)
    slope = jnp.sum(grad * normed, axis=-1, keepdims=True) * (1.0 / count)
    return inverse * (grad - mean - normed * slope), gain_grad, bias_grad


def head_means(values, group):
    high = values.astype(BFLOAT)
    rest = (values - high.astype(FLOAT)).astype(BFLOAT)
    return (dot(high, group) + dot(rest, group)) * (1.0 / HD)


def norm_heads(values, group):
    centred = values - head_means(values, group)
    inverse = lax.rsqrt(head_means(centred * centred, group) + EPSILON)
    return centred * inverse, inverse


def head_masks(heads, span):
    lanes = lax.broadcasted_iota(jnp.int32, (1, span), 1)
    return [((lanes >= HD * head) & (lanes < HD * (head + 1))).astype(BFLOAT) for head in range(heads)]


def load_weights(weights_ref, kept_ref, sems):
    width = kept_ref.shape[-1]
    return [
        pltpu.make_async_copy(weights_ref.at[:, i * width : (i + 1) * width], kept_ref.at[i], sems.at[i])
        for i in range(3)
    ]


def middle_forward_kernel(
    heads, parts, *refs,
):
    mixed_refs, text_refs, refs = refs[:parts], refs[parts : 2 * parts], refs[2 * parts :]
    one_ref, table_ref, group_ref, weights_ref, two_ref, raw_ref, three_ref, mixed_ref, cross_ref = refs[:9]
    query_ref, cross_mixed_ref, mlp_ref, kept_ref, sems = refs[9:]
    span = heads * HD
    mixed_ref[...] = jnp.concatenate([ref[...] for ref in mixed_refs], axis=1)
    loads = load_weights(weights_ref, kept_ref, sems)
    for load in loads:
        load.start()
    row = lambda index: table_ref[index : index + 1, :]
    loads[0].wait()
    two = one_ref[...] + dot(mixed_ref[...], kept_ref[0], NT) + row(0)
    two_ref[...] = two
    cross = (norm_rows(two)[0] * row(1) + row(2)).astype(BFLOAT)
    cross_ref[...] = cross
    loads[1].wait()
    raw_ref[...] = dot(cross, kept_ref[1]) + row(3)
    group = group_ref[...]
    masks = head_masks(heads, span)
    pieces, mixes = [], []
    for r in range(parts):
        part = slice(r * span, (r + 1) * span)
        normed, _ = norm_heads(raw_ref[:, part], group)
        queries = (normed * table_ref[4:5, part]).astype(BFLOAT)
        pieces.append(queries)
        keys, values = text_refs[r][:, :span], text_refs[r][:, span:]
        mix = None
        for head in range(heads):
            scores = dot(queries * masks[head], keys, NT)
            peak = jnp.max(scores, axis=-1, keepdims=True)
            powers = jnp.exp2((scores - peak) * (SCALE * LOG2E))
            weights = (powers / jnp.sum(powers, axis=-1, keepdims=True)).astype(BFLOAT)
            term = dot(weights, values * masks[head])
            mix = term if mix is None else mix + term
        mixes.append(mix.astype(BFLOAT))
    query_ref[...] = jnp.concatenate(pieces, axis=1)
    cross_mixed_ref[...] = jnp.concatenate(mixes, axis=1)
    loads[2].wait()
    three = two_ref[...] + dot(cross_mixed_ref[...], kept_ref[2], NT) + row(5)
    three_ref[...] = three
    mlp_ref[...] = (norm_rows(three)[0] * row(6) + row(7)).astype(BFLOAT)


def middle_forward(mixed, one, table, text, group, weights, heads):
    rows, width = one.shape
    wide = jax.ShapeDtypeStruct((rows, width), FLOAT)
    low = jax.ShapeDtypeStruct((rows, width), BFLOAT)
    vmem = pl.BlockSpec(memory_space=pltpu.VMEM)
    return pl.pallas_call(
        functools.partial(middle_forward_kernel, heads, len(mixed)),
        in_specs=[vmem] * (2 * len(mixed) + 3) + [pl.BlockSpec(memory_space=pl.ANY)],
        out_shape=(wide, wide, wide, low, low, low, low, low),
        out_specs=(vmem,) * 8,
        scratch_shapes=[pltpu.VMEM((3, width, width), BFLOAT), pltpu.SemaphoreType.DMA((3,))],
        compiler_params=pltpu.CompilerParams(vmem_limit_bytes=56 * 2**20),
        cost_estimate=pl.CostEstimate(flops=26_000_000_000, bytes_accessed=24_000_000, transcendentals=1_300_000),
    )(*mixed, *text, one, table, group, weights)


def middle_backward_kernel(
    heads, parts, *refs,
):
    text_refs, refs = refs[:parts], refs[parts:]
    grad_ref, cot_ref, three_ref, two_ref, raw_ref, query_ref, table_ref, group_ref, weights_ref = refs[:9]
    three_low_ref, raw_low_ref, two_low_ref, grad_two_ref, rows_ref, refs = *refs[9:14], refs[14:]
    mixed_refs, text_grad_refs = refs[:parts], refs[parts : 2 * parts]
    kept_ref, grad_three_ref, mixed_ref, sems = refs[2 * parts :]
    span = heads * HD
    loads = load_weights(weights_ref, kept_ref, sems)
    for load in reversed(loads):
        load.start()
    row = lambda index: table_ref[index : index + 1, :]
    into, gain_grad, bias_grad = norm_rows_back(three_ref[...], row(6), grad_ref[...])
    rows_ref[0:1, :], rows_ref[1:2, :] = gain_grad, bias_grad
    grad_three = cot_ref[...].astype(FLOAT) + into
    grad_three_ref[...] = grad_three
    rows_ref[2:3, :] = jnp.sum(grad_three, axis=0, keepdims=True)
    three_low = grad_three.astype(BFLOAT)
    three_low_ref[...] = three_low
    loads[2].wait()
    mixed_ref[...] = dot(three_low, kept_ref[2]).astype(BFLOAT)
    group = group_ref[...]
    masks = head_masks(heads, span)
    pieces = []
    for r in range(parts):
        part = slice(r * span, (r + 1) * span)
        keys, values = text_refs[r][:, :span], text_refs[r][:, span:]
        queries, mixed = query_ref[:, part], mixed_ref[:, part]
        grad_q = grad_k = grad_v = None
        for head in range(heads):
            some, grad = queries * masks[head], mixed * masks[head]
            scores = dot(keys, some, NT)
            peak = jnp.max(scores, axis=0, keepdims=True)
            powers = jnp.exp2((scores - peak) * (SCALE * LOG2E))
            probs = powers / jnp.sum(powers, axis=0, keepdims=True)
            grad_probs = dot(values, grad, NT)
            inner = jnp.sum(probs * grad_probs, axis=0, keepdims=True)
            grad_scores = (probs * (grad_probs - inner)).astype(BFLOAT)
            add_q = dot(grad_scores, keys * masks[head], TN)
            add_k = dot(grad_scores, some)
            add_v = dot(probs.astype(BFLOAT), grad)
            if head == 0:
                grad_q, grad_k, grad_v = add_q, add_k, add_v
            else:
                grad_q, grad_k, grad_v = grad_q + add_q, grad_k + add_k, grad_v + add_v
        text_grad_refs[r][:, :span] = (grad_k * SCALE).astype(BFLOAT)
        text_grad_refs[r][:, span:] = grad_v.astype(BFLOAT)
        normed, inverse = norm_heads(raw_ref[:, part], group)
        grad_q = grad_q * SCALE
        rows_ref[7:8, part] = jnp.sum(grad_q * normed, axis=0, keepdims=True)
        grad_q = grad_q * table_ref[4:5, part]
        low = (
            inverse * (grad_q - head_means(grad_q, group) - normed * head_means(grad_q * normed, group))
        ).astype(BFLOAT)
        pieces.append(low)
    raw_low_ref[...] = jnp.concatenate(pieces, axis=1)
    rows_ref[6:7, :] = jnp.sum(raw_low_ref[...].astype(FLOAT), axis=0, keepdims=True)
    loads[1].wait()
    into, gain_grad, bias_grad = norm_rows_back(two_ref[...], row(1), dot(raw_low_ref[...], kept_ref[1], NT))
    rows_ref[3:4, :], rows_ref[4:5, :] = gain_grad, bias_grad
    grad_two = grad_three_ref[...] + into
    grad_two_ref[...] = grad_two
    rows_ref[5:6, :] = jnp.sum(grad_two, axis=0, keepdims=True)
    two_low = grad_two.astype(BFLOAT)
    two_low_ref[...] = two_low
    loads[0].wait()
    mixed = dot(two_low, kept_ref[0])
    for r in range(parts):
        mixed_refs[r][...] = mixed[:, r * span : (r + 1) * span].astype(BFLOAT)


def middle_backward(grad, cot, three, two, raw, queries, table, text, group, weights, heads):
    rows, width = three.shape
    low = jax.ShapeDtypeStruct((rows, width), BFLOAT)
    vmem = pl.BlockSpec(memory_space=pltpu.VMEM)
    return pl.pallas_call(
        functools.partial(middle_backward_kernel, heads, len(text)),
        in_specs=[vmem] * (8 + len(text)) + [pl.BlockSpec(memory_space=pl.ANY)],
        out_shape=(
            low,
            low,
            low,
            jax.ShapeDtypeStruct((rows, width), FLOAT),
            jax.ShapeDtypeStruct((8, width), FLOAT),
            *[jax.ShapeDtypeStruct((rows, heads * HD), BFLOAT) for _ in text],
            *[jax.ShapeDtypeStruct(item.shape, BFLOAT) for item in text],
        ),
        out_specs=(vmem,) * (5 + 2 * len(text)),
        scratch_shapes=[
            pltpu.VMEM((3, width, width), BFLOAT),
            pltpu.VMEM((rows, width), FLOAT),
            pltpu.VMEM((rows, width), BFLOAT),
            pltpu.SemaphoreType.DMA((3,)),
        ],
        compiler_params=pltpu.CompilerParams(vmem_limit_bytes=56 * 2**20),
        cost_estimate=pl.CostEstimate(flops=33_000_000_000, bytes_accessed=28_000_000, transcendentals=1_300_000),
    )(*text, grad, cot, three, two, raw, queries, table, group, weights)


def on_device(
    latent, skip_in, text_tokens, time_embed, t_index, grid_pos, skip_weight, mod_weight, vectors, up_bias,
    qkv_weight, proj_weight, query_weight, text_weight, cross_weight, up_weight, down_weight, out_grad,
):
    split = lax.axis_size("tensor")
    shards = lax.axis_size("dp")
    place = lax.axis_index("tensor")
    me = lax.axis_index("dp")
    own_rows, width = latent.shape
    own_text = text_tokens.shape[0]
    part = mod_weight.shape[0]
    heads = HEADS // split
    span = heads * HD
    hidden = up_weight.shape[1]
    rows_ahead = vectors.shape[0]

    def others(r):
        return lax.rem(place - r + split, split)

    condition = time_embed
    half = width // 2
    frequencies = jnp.exp(-math.log(10000.0) * jnp.arange(half, dtype=FLOAT) / half)
    angles = t_index.astype(FLOAT)[:, None] * frequencies[None, :]
    condition = time_embed + jnp.concatenate([jnp.cos(angles), jnp.sin(angles)], axis=-1)
    silu_low = silu(condition).astype(BFLOAT)
    small = jnp.concatenate([vectors.reshape(-1), up_bias, silu_low.reshape(-1)])
    small_all = small_gather(small)
    cut_one, cut_two = rows_ahead * part, rows_ahead * part + up_bias.shape[0]
    table = (
        small_all[:, :cut_one].reshape(shards, rows_ahead, part).transpose(1, 0, 2).reshape(rows_ahead, width)
    ).astype(FLOAT)
    bias_all = small_all[:, cut_one:cut_two].reshape(-1).astype(FLOAT)
    silu_all = small_all[:, cut_two:]

    expand = jnp.asarray(expansion(heads), BFLOAT)
    deep = heads * DEEP
    packed_one = jnp.concatenate(
        [
            skip_weight[:part],
            skip_weight[part:],
            dot(qkv_weight.reshape(part, 3 * span), expand).astype(BFLOAT),
            text_weight.reshape(part, 2 * span),
        ],
        axis=1,
    )
    all_one = lax.all_gather(packed_one, "dp", axis=0, tiled=True)
    w_skip = all_one[:, : 2 * width]
    w_qkv = all_one[:, 2 * width : 2 * width + 3 * deep]
    w_text = all_one[:, 2 * width + 3 * deep :]

    own_full = jnp.stack([proj_weight.T, query_weight, cross_weight.T])
    full_blocks, text_blocks = [own_full], [text_tokens]
    for _ in range(split - 1):
        both = lax.optimization_barrier((full_blocks[-1], text_blocks[-1]))
        full_blocks.append(rot(both[0], 1))
        text_blocks.append(rot(both[1], 1))
    packed_two = jnp.concatenate(
        [full_blocks[r][index] for index in range(3) for r in range(split)], axis=1
    )

    cot_blocks = [out_grad, rot(after(out_grad, all_one, full_blocks[-1], text_blocks[-1]), 1)]
    text_full = jnp.concatenate(text_blocks, axis=0)

    def head_slice(index):
        return lax.dynamic_slice_in_dim(table[index], place * span, span, 0)

    def relative(index):
        return jnp.concatenate(
            [lax.dynamic_slice_in_dim(table[index], others(r) * span, span, 0) for r in range(split)]
        )

    def spread(values):
        return lax.dynamic_update_slice_in_dim(jnp.zeros((width,), FLOAT), values.reshape(-1), place * span, 0)

    def absolute(values):
        result = jnp.zeros((width,), FLOAT)
        for r in range(split):
            result = lax.dynamic_update_slice_in_dim(
                result, values.reshape(-1)[r * span : (r + 1) * span], others(r) * span, 0
            )
        return result

    def deepen(values):
        turned = jnp.pad(values[:2].reshape(2, heads, 4, HD // 4), ((0, 0), (0, 0), (0, 0), (0, QUARTER - HD // 4)))
        plain = jnp.pad(values[2].reshape(heads, HD), ((0, 0), (0, DEEP - HD)))
        return jnp.concatenate([turned.reshape(-1), plain.reshape(-1)])

    def undeepen(values):
        turned = values[: 2 * deep].reshape(2, heads, 4, QUARTER)[..., : HD // 4].reshape(2, span)
        if values.shape[0] == 2 * deep:
            return turned
        return jnp.concatenate([turned, values[2 * deep :].reshape(heads, DEEP)[:, :HD].reshape(1, span)])

    quarter = HD // 4
    rate = np.zeros((QUARTER, 1), np.float32)
    rate[:quarter, 0] = 10000.0 ** (-np.arange(quarter, dtype=np.float64) / quarter)
    grid_rel = jnp.concatenate(
        [lax.dynamic_slice_in_dim(grid_pos, others(r) * own_rows, own_rows, 1) for r in range(split)], axis=1
    ).astype(FLOAT)
    turn = grid_rel[:, None, :] * rate[None]
    turns = jnp.stack([jnp.cos(turn[0]), jnp.sin(turn[0]), jnp.cos(turn[1]), jnp.sin(turn[1])])

    silu_mine = lax.dynamic_slice_in_dim(silu_all, me * part, part, 1)
    shift_terms = dot(silu_mine, mod_weight)
    shift = jnp.sum(lax.all_to_all(shift_terms, "dp", 0, 0, tiled=True), axis=0, keepdims=True) + table[5]

    joined = jnp.concatenate([latent.astype(FLOAT), skip_in.astype(FLOAT)], axis=-1)
    joined_gain = jnp.concatenate([table[0], table[1]])
    joined_bias = jnp.concatenate([table[2], table[3]])
    normed_low = layer_norm(joined, joined_gain, joined_bias).astype(BFLOAT)
    normed_perm = normed_low.reshape(own_rows, shards, 2, part).transpose(0, 2, 1, 3).reshape(own_rows, 2 * width)
    packed_two = after(packed_two, normed_perm, shift, turns)
    all_two = lax.all_gather(packed_two, "dp", axis=0, tiled=True)
    packed_three = jnp.concatenate([up_weight, down_weight.T], axis=1)
    all_three = lax.all_gather(packed_three, "dp", axis=0, tiled=True)
    w_up, w_down_t = all_three[:, :hidden], all_three[:, hidden:]

    stream_one = (
        dot(normed_perm[:, :width], w_skip[:, :width]) + dot(normed_perm[:, width:], w_skip[:, width:]) + table[4]
    )
    attn_low = (layer_norm(stream_one, table[6], table[7]) + shift).astype(BFLOAT)
    attn_blocks = ring_gather(after(attn_low, cot_blocks[1]))
    qkv_bias = deepen(jnp.stack([head_slice(8), head_slice(9), head_slice(10)]))[:, None]
    raws = [dot(w_qkv, block, ((0,), (1,))) + qkv_bias for block in attn_blocks]
    zero_slice = jnp.zeros((span,), FLOAT)
    gains = deepen(jnp.stack([head_slice(12), head_slice(13), zero_slice]))[: 2 * deep, None]
    length = own_rows * split
    block = min(512, length)
    kept = attend_forward(raws, turns, gains, heads, block)
    mixed, kept = kept[:split], kept[split:]

    def blocks_of(values, rows):
        return [values[r * rows : (r + 1) * rows] for r in range(split)]

    text_raw = dot(text_full, w_text) + jnp.concatenate([head_slice(17), head_slice(18)])
    text_length = text_raw.shape[0]
    gain_21 = head_slice(21).reshape(heads, HD)
    raw_key = text_raw[:, :span].reshape(text_length, heads, HD)
    text_low = jnp.concatenate(
        [head_norm(raw_key, gain_21).reshape(text_length, span), text_raw[:, span:]], axis=1
    ).astype(BFLOAT)
    text_rel = direct_gather(after(text_low, attn_blocks[-1]))
    *mixed, text_rel[-1] = lax.optimization_barrier((*mixed, text_rel[-1]))
    mixed = exchange(mixed)
    cot_blocks[-1], mixed[-1] = lax.optimization_barrier((cot_blocks[-1], mixed[-1]))
    cot_blocks.append(rot(cot_blocks[-1], 1))
    lane_head = np.arange(span) // HD
    group = jnp.asarray((lane_head[:, None] == lane_head[None, :]).astype(np.float32), BFLOAT)
    middle_table = jnp.stack(
        [table[11], table[14], table[15], relative(16), relative(20), table[19], table[22], table[23]]
    )
    stream_two, cross_raw, stream_three, mixed_own, cross_low, cross_queries, cross_mixed, mlp_low = middle_forward(
        mixed, stream_one, middle_table, text_rel, group, all_two, heads
    )
    mlp_low, cot_blocks[-1] = lax.optimization_barrier((mlp_low, cot_blocks[-1]))
    while len(cot_blocks) < split:
        cot_blocks.append(rot(cot_blocks[-1], 1))
    mlp_blocks = ring_gather(mlp_low)
    hidden_bias = lax.dynamic_slice_in_dim(bias_all, place * hidden, hidden, 0)

    hidden_lows, pre_lows, out_parts, back_parts = [], [], [], []
    for r in range(split):
        hidden_pre = dot(mlp_blocks[r], w_up) + hidden_bias
        activated, pull = jax.vjp(gelu, hidden_pre)
        hidden_lows.append(activated.astype(BFLOAT))
        pre_lows.append(pull(dot(cot_blocks[r], w_down_t))[0].astype(BFLOAT))
        back_parts.append(dot(pre_lows[r], w_up, NT))
        out_parts.append(dot(hidden_lows[r], w_down_t, NT))
    grad_mlp_in = ring_scatter(back_parts)

    rows_grad = {}
    grad_bias = sum(jnp.sum(item, axis=0, dtype=FLOAT) for item in pre_lows)
    grads_one = pack_grad(None, mlp_blocks, pre_lows, 2 * hidden, 0, 512)
    grads_one = pack_grad(grads_one, cot_blocks, hidden_lows, 2 * hidden, hidden, 512)
    grads_one, grad_mlp_in, *out_parts = lax.optimization_barrier((grads_one, grad_mlp_in, *out_parts))
    out_hop = rot(out_parts[1].astype(BFLOAT), 1)
    summed_one = lax.psum_scatter(grads_one, "dp", scatter_dimension=0, tiled=True).astype(FLOAT)
    cot_here = out_grad.astype(FLOAT)
    rows_grad[24] = jnp.sum(cot_here, axis=0)
    three_low, cq_low, two_low, grad_two, middle_rows, *pieces = middle_backward(
        grad_mlp_in, out_grad, stream_three, stream_two, cross_raw, cross_queries, middle_table, text_rel, group,
        all_two, heads,
    )
    grad_mixed, text_terms = pieces[:split], pieces[split:]
    for index, number in enumerate((22, 23, 19, 14, 15, 11)):
        rows_grad[number] = middle_rows[index]
    rows_grad[16], rows_grad[20] = absolute(middle_rows[6]), absolute(middle_rows[7])
    out_hop, *grad_mixed = lax.optimization_barrier((out_hop, *grad_mixed))
    grad_mixed = exchange(grad_mixed)
    lanes_two = 3 * width
    grads_two = pack_grad(None, [two_low], [mixed_own], lanes_two, 0, width)
    grads_two = pack_grad(grads_two, [cross_low], [cq_low], lanes_two, width, width)
    grads_two = pack_grad(grads_two, [three_low], [cross_mixed], lanes_two, 2 * width, width)
    grads_two, *grad_mixed = lax.optimization_barrier((grads_two, *grad_mixed))
    summed_two = lax.psum_scatter(grads_two, "dp", scatter_dimension=0, tiled=True)
    text_terms[1:] = lax.optimization_barrier((*text_terms[1:], grad_mixed[-1]))[:-1]
    text_got = [rot(text_terms[r], split - r) for r in range(1, split)]
    grad_raw, gain_grads, raw_sums = attend_backward(
        raws, turns, gains, kept, grad_mixed, heads, block
    )
    grad_raw, summed_one = lax.optimization_barrier((grad_raw, summed_one))
    text_got[0], grad_raw = lax.optimization_barrier((text_got[0], grad_raw))
    ckv_low, text_rows = text_norm_back([text_terms[0], *text_got], text_raw, head_slice(21)[None], group)
    rows_grad[21] = spread(text_rows[1, :span])
    rows_grad[17], rows_grad[18] = spread(text_rows[0, :span]), spread(text_rows[0, span:])

    gain_grads = undeepen(jnp.sum(gain_grads, axis=1))
    raw_sums = undeepen(jnp.sum(raw_sums, axis=1))
    rows_grad[12], rows_grad[13] = spread(gain_grads[0]), spread(gain_grads[1])
    rows_grad[8], rows_grad[9], rows_grad[10] = spread(raw_sums[0]), spread(raw_sums[1]), spread(raw_sums[2])
    qkv_lanes = 3 * deep
    text_lanes = pl.cdiv(2 * span, LANES) * LANES
    shared = 2 * width + LANES
    qkv_start = pl.cdiv(shared, deep) * deep
    text_start = qkv_start + qkv_lanes
    lanes_three = text_start + text_lanes
    bias_part = up_bias.shape[0]
    bias_cols = pl.cdiv(bias_part, part)
    bias_spread = lax.dynamic_update_slice_in_dim(jnp.zeros(bias_all.shape, FLOAT), grad_bias, place * hidden, 0)
    zero_row = jnp.zeros((width,), FLOAT)
    table_grad = jnp.stack([rows_grad.get(index, zero_row) for index in range(rows_ahead)], axis=1)
    bias_grad = jnp.pad(bias_spread.reshape(shards, bias_part), ((0, 0), (0, bias_cols * part - bias_part)))
    bias_grad = bias_grad.reshape(shards, bias_cols, part).transpose(0, 2, 1).reshape(width, bias_cols)
    small_grads = jnp.concatenate([table_grad, bias_grad], axis=1).astype(BFLOAT)
    small_grads = jnp.pad(small_grads, ((0, 0), (0, qkv_start - 2 * width - small_grads.shape[1])))

    grads_three = pack_grad(None, attn_blocks, [grad_raw], lanes_three, qkv_start, deep, turned=True)
    grads_three = pack_grad(grads_three, [text_full], [ckv_low], lanes_three, text_start, LANES)
    grads_three = lax.dynamic_update_slice(grads_three, small_grads, (0, 2 * width))
    out_hop = rot(after((out_hop.astype(FLOAT) + out_parts[2]).astype(BFLOAT), ckv_low), 1)
    grad_raw, grads_three, out_hop = lax.optimization_barrier((grad_raw, grads_three, out_hop))
    grad_attn_in, shift_part = ring_sum(grad_raw, all_one, 2 * width, split)
    grads_three, one_low, late_rows = skip_grads(
        grads_three, grad_attn_in, grad_two, stream_one, table[6:7], normed_perm
    )
    grads_three, summed_two, one_low = lax.optimization_barrier((grads_three, summed_two, one_low))
    summed_three = lax.psum_scatter(grads_three, "dp", scatter_dimension=0, tiled=True)
    latent_grad, skip_grad, late, full_sum, text_grad, block_out = side_sums(
        one_low, late_rows, shift_part, jnp.concatenate([table[:2], table[24:25]]), latent, skip_in, stream_three,
        out_hop, summed_two, ckv_low, all_one, [out_parts[0], *out_parts[3:]], shards, split,
    )
    shift_grads = late[8 : 8 + shards]
    late = lax.dynamic_slice_in_dim(late[:8], me * part, part, 1)
    mod_grad = lax.dot_general(
        silu_mine.astype(FLOAT), shift_grads, ((TN), ((), ())), precision=HIGHEST, preferred_element_type=FLOAT
    )
    into_silu = lax.dot_general(
        shift_grads, mod_weight.astype(FLOAT), ((NT), ((), ())), precision=HIGHEST, preferred_element_type=FLOAT
    )
    into_silu = lax.all_to_all(into_silu, "dp", 0, 0, tiled=True).reshape(1, width)
    time_full = jax.vjp(silu, condition)[1](into_silu)[0]
    time_grad = lax.dynamic_slice_in_dim(time_full, place * (width // split), width // split, 1)

    summed_three = after(summed_three, mod_grad, time_grad, full_sum, text_grad, summed_one)
    qkv_part = summed_three[:, qkv_start:text_start]
    text_part = summed_three[:, text_start : text_start + 2 * span]
    skip_weight_grad, small_sum = spread_sum(summed_three[:, :shared], width, split)
    vectors_grad = jnp.concatenate([late[:5], late[7:8], late[5:7], small_sum[:, 8:rows_ahead].T])
    bias_grad = small_sum[:, rows_ahead : rows_ahead + bias_cols].T.reshape(-1)[:bias_part]
    qkv_sum = dot(qkv_part, expand, NT).reshape(part, 3, span)
    text_sum_grad = text_part.astype(FLOAT).reshape(part, 2, span)

    return (
        block_out,
        latent_grad,
        skip_grad,
        text_grad,
        time_grad,
        skip_weight_grad,
        mod_grad,
        vectors_grad,
        bias_grad,
        qkv_sum,
        full_sum[:, :span].T,
        full_sum[:, span : 2 * span],
        text_sum_grad,
        full_sum[:, 2 * span :].T,
        summed_one[:, :hidden],
        summed_one[:, hidden:].T,
    )


def solution(mesh):
    tokens = P(("dp", "tensor"), None)
    placed = (
        tokens,
        tokens,
        tokens,
        P("dp", None),
        P("dp"),
        P(None, "dp"),
        P("dp", None),
        P("dp", None),
        P(None, "dp"),
        P("dp"),
        P("dp", None, "tensor"),
        P("tensor", "dp"),
        P("dp", "tensor"),
        P("dp", None, "tensor"),
        P("tensor", "dp"),
        P("dp", "tensor"),
        P("tensor", "dp"),
        tokens,
    )
    return jax.shard_map(
        on_device,
        mesh=mesh,
        in_specs=placed,
        out_specs=(
            tokens,
            tokens,
            tokens,
            tokens,
            P("dp", "tensor"),
            P("dp", None),
            P("dp", None),
            P(None, "dp"),
            P("dp"),
            P("dp", None, "tensor"),
            P("tensor", "dp"),
            P("dp", "tensor"),
            P("dp", None, "tensor"),
            P("tensor", "dp"),
            P("dp", "tensor"),
            P("tensor", "dp"),
        ),
        check_vma=False,
    )
```

time: 775 us -> 763 us (0.985)
  Pallas kernels: 167 us -> 325 us
  waiting for transfers between devices: 180 us -> 94.9 us
  other arithmetic: 66.6 us -> 36.8 us
  local copies, waits for them, and re-layouts: 111 us -> 82.8 us
  matrix products: 98.6 us -> 75 us
    pallas_call x13 -> x16, Pallas kernels: 167 us -> 325 us  [the longest x1 84 us: side_sums(): pl.pallas_call(functools.partial(side_kernel, shards, split, hops), in_sp...]
    ppermute x51 -> x32, waiting for transfers between devices: 162 us -> 87.2 us  [rot(): lax.ppermute(values, 'tensor', [(i, (i + step) % count) for i in range(co...]
    dot_general x31 -> x26, matrix products: 95.7 us -> 71.1 us  [dot(): lax.dot_general(left, right, (contract, ((), ())), preferred_element_type...]
    concatenate x10 -> x4, other arithmetic: 16.6 us -> 2.56 us  [the longest x1 1.29 us: on_device(): jnp.concatenate([skip_weight[:part], skip_weight[part:], dot(qkv_weight.r...]
    concatenate x8 -> x0, local copies, waits for them, and re-layouts: 11.7 us -> none  [the longest x4 4.55 us: on_device(): jnp.concatenate([summed_two[:, i * width + r * span:i * width + (r + 1) *...]
    reduce_scatter x1 -> x0, waiting for transfers between devices: 9.92 us -> none  [on_device(): lax.psum_scatter(grads_qkv, 'dp', scatter_dimension=0, tiled=True)]
    convert_element_type x4 -> x0, local copies, waits for them, and re-layouts: 8.03 us -> none  [on_device(): shared_blocks[r].astype(FLOAT)]
    ppermute x51 -> x32, starting transfers between devices: 107 us -> 111 us  [rot(): lax.ppermute(values, 'tensor', [(i, (i + step) % count) for i in range(co...]
  transfers between devices with their start and end apart: 66 -> 43, of which waited for: 28 -> 18; matrix products, arithmetic and copies ran while one was open for 29% -> 19% of each run, Pallas kernels for 21% -> 36%
where the time goes in v3:
time: 763 us; the launch traced here: 752 us
  Pallas kernels  325 us (43%)
  starting transfers between devices  121 us (16%)
  waiting for transfers between devices  94.9 us (12%)
  local copies, waits for them, and re-layouts  82.8 us (11%)
  matrix products  75 us (10%)
  other arithmetic  36.8 us (5%)
  between operations  16.8 us (2%)
    ppermute x32, starting transfers between devices, rot(): lax.ppermute(values, 'tensor', [(i, (i + step) % count) for i in range(co...  111 us
    ppermute x32, waiting for transfers between devices, rot(): lax.ppermute(values, 'tensor', [(i, (i + step) % count) for i in range(co...  87.2 us
    pallas_call x1, Pallas kernels, side_sums(): pl.pallas_call(functools.partial(side_kernel, shards, split, hops), in_sp...  84 us
    dot_general x26, matrix products, dot(): lax.dot_general(left, right, (contract, ((), ())), preferred_element_type...  71.1 us
    pallas_call x1, Pallas kernels, spread_sum(): pl.pallas_call(functools.partial(spread_kernel, split, starts), in_specs=...  53 us
    pallas_call x1, Pallas kernels, ring_sum(): pl.pallas_call(functools.partial(ring_kernel, split, start), in_specs=[vm...  52.6 us
    unnamed x172, local copies, waits for them, and re-layouts  34.7 us
    pallas_call x7, Pallas kernels, pack_grad(): pl.pallas_call(functools.partial(grad_kernel, len(lefts), len(rights), tu...  34.3 us
  transfers between devices with their start and end apart: 43, of which 18 were waited for; matrix products, arithmetic and copies ran while one was open for 19% of the time, Pallas kernels for 36%

profile of v3, /device:TPU:24, one launch (start us, length us, event | category | flops | bytes accessed | tf_op | source)
XLA Modules:
  0.0 752.5 jit_solution(9396881012190621722)
XLA Ops:
  59.8 8.1 %collective-permute-done.3 = bf16[3,176,352]{2,1,0:T(8,128)(2,1)} collective-permute-done((bf16[3,176,352]{2,1,0:T(8,128)(2,1)}, bf16[3,176,352]{2,1,0:T(8,128)(2,1)}, u32[]{:S(2)}, u32[]{:S(2)}) %collective-permute-start.3) | collective-permute-done | bytes 371744 | tf_op jit(solution)/shard_map/ppermute | solution.py:54
  73.4 6.5 collective-permute-done.8
  127.1 8.7 %collective-permute-done.10.refs_1_ = bf16[256,1408]{1,0:T(8,128)(2,1)} collective-permute-done((bf16[256,1408]{1,0:T(8,128)(2,1)}, bf16[256,1408]{1,0:T(8,128)(2,1)}, u32[]{:S(2)}, u32[]{:S(2)}) %collective-permute-start.10) | collective-permute-done | bytes 720928 | tf_op jit(solution)/shard_map/ppermute | solution.py:54
  145.3 7.1 collective-permute-done.11.refs_2_
  164.9 7.4 collective-permute-done.12.refs_3_
  172.4 4.9 collective-permute-start.14
  181.5 15.6 %shard_map.324 = (bf16[256,352]{1,0:T(8,128)(2,1)}, bf16[256,352]{1,0:T(8,128)(2,1)}, bf16[256,352]{1,0:T(8,128)(2,1)}, bf16[256,352]{1,0:T(8,128)(2,1)}, bf16[4...) custom-call(f32[1152,256]{1,0:T(8,128)} %convolution_add_fusion.3.re, ...), custom_call_target="tpu_custom_call" | custom-call | flops 20000000000 | bytes 12000000 | tf_op jit(solution)/shard_map/pallas_call | solution.py:681
  197.2 19.2 %collective-permute-start.16 = (bf16[256,352]{1,0:T(8,128)(2,1)}, bf16[256,352]{1,0:T(8,128)(2,1)S(1)}, u32[]{:S(2)}, u32[]{:S(2)}) collective-permute-start(bf16[256,352]{1,0:T(8,128)(2,1)} %get-tuple-element.129), channel_id=1, source_target_pairs={{0,3},{1,0},{2,1},{3,2},{4,7},{5,4},{6,5},{7,6},{8,11},{9,8},{10,9... | collective-permute-start | bytes 540680 | tf_op jit(solution)/shard_map/ppermute | solution.py:54
  228.4 24.0 %shard_map.325 = (f32[256,1408]{1,0:T(8,128)}, f32[256,1408]{1,0:T(8,128)}, f32[256,1408]{1,0:T(8,128)}, bf16[256,1408]{1,0:T(8,128)(2,1)}, bf16[256,1408]{1,0:T...) custom-call(bf16[256,352]{1,0:T(8,128)(2,1)} %get-tuple-element.131.refs_0_, ...), custom_call_target="tpu_custom_call" | custom-call | flops 25999998976 | bytes 24000000 | tf_op jit(solution)/shard_map/pallas_call | solution.py:880
  252.4 17.5 %collective-permute-start.20 = (bf16[256,1408]{1,0:T(8,128)(2,1)S(1)}, bf16[256,1408]{1,0:T(8,128)(2,1)}, u32[]{:S(2)}, u32[]{:S(2)}) collective-permute-start(bf16[256,1408]{1,0:T(8,128)(2,1)S(1)} %collective-permute-done.19.refs_2_), channel_id=1, source_target_pairs={{0,1},{1,2},{2,3},{3,0},{4,5},{5,6},{6,7},{7,4},{8,9},{9,10},{10,1... | collective-permute-start | bytes 2162696 | tf_op jit(solution)/shard_map/ppermute | solution.py:54
  283.9 13.3 %collective-permute-done.21.refs_1_ = bf16[256,1408]{1,0:T(8,128)(2,1)} collective-permute-done((bf16[256,1408]{1,0:T(8,128)(2,1)}, bf16[256,1408]{1,0:T(8,128)(2,1)}, u32[]{:S(2)}, u32[]{:S(2)}) %collective-permute-start.21) | collective-permute-done | bytes 720928 | tf_op jit(solution)/shard_map/ppermute | solution.py:54
  311.1 7.3 collective-permute-done.22.refs_2_
  327.0 6.7 collective-permute-done.24
  342.0 7.1 collective-permute-done.23.refs_3_
  364.1 8.4 %shard_map.326.refs_8_ = bf16[1408,3072]{1,0:T(8,128)(2,1)} custom-call(bf16[256,1408]{1,0:T(8,128)(2,1)S(1)} %copy-done.19, bf16[256,1408]{1,0:T(8,128)(2,1)} %collective-permute-done.21.refs_1_, bf16[256,1408]{1,0:T(8,128)(2,1)S(1)} %collective-permute-done.22.refs_2_, bf16[256,1408]{1,0:T(8,128)(2,1)S(1)} %collective-permute-done.23.refs_3_, ...), custom_call_target="tpu_custom_call" | custom-call | flops 8858370048 | bytes 10354688 | tf_op jit(solution)/shard_map/pallas_call | solution.py:146
  375.0 8.6 %shard_map.327 = bf16[1408,3072]{1,0:T(8,128)(2,1)} custom-call(bf16[256,1408]{1,0:T(8,128)(2,1)} %refs_5_.2, bf16[256,1408]{1,0:T(8,128)(2,1)S(1)} %copy-done.18, bf16[256,1408]{1,0:T(8,128)(2,1)S(1)} %collective-permute-done.19.refs_2_, bf16[256,1408]{1,0:T(8,128)(2,1)} %collective-permute-done.20.refs_3_, ...), custom_call_target="tpu_custom_call", output_to_operand_aliasing={{}: (8, {})} | custom-call | flops 8858370048 | bytes 10354688 | tf_op jit(solution)/shard_map/pallas_call | solution.py:146
  387.9 30.2 %shard_map.328 = (bf16[256,1408]{1,0:T(8,128)(2,1)}, bf16[256,1408]{1,0:T(8,128)(2,1)}, bf16[256,1408]{1,0:T(8,128)(2,1)}, f32[256,1408]{1,0:T(8,128)}, f32[8,14...) custom-call(bf16[320,704]{1,0:T(8,128)(2,1)} %pad_maximum_fusion.2.r, ...), custom_call_target="tpu_custom_call" | custom-call | flops 32999999488 | bytes 28000000 | tf_op jit(solution)/shard_map/pallas_call | solution.py:967
  449.7 21.8 %shard_map.332 = (bf16[1152,1024]{1,0:T(8,128)(2,1)}, f32[768,128]{1,0:T(8,128)}, f32[1152,128]{1,0:T(8,128)}) custom-call(f32[1152,256]{1,0:T(8,128)} %convolution_add_fusion.3.refs_0_, f32[1152,256]{1,0:T(8,128)} %convolution_add_fusion.2.refs_1_, f32[1152,256]{1,0:T(8,128)} %convolution_add_fusion.1.refs_2_, f32[1152,256]{1,0:T(8,128)} %convolution_add_fusion.refs_3_, ...), custom_call_target="tpu_custom_call" | custom-call | flops 28000000000 | bytes 16000000 | tf_op jit(solution)/shard_map/pallas_call | solution.py:768
  487.1 5.3 collective-permute-start.34
  496.4 8.4 %shard_map.334.refs_2_ = bf16[1408,4992]{1,0:T(8,128)(2,1)} custom-call(bf16[256,1408]{1,0:T(8,128)(2,1)} %add_convert_fusion.3.refs_0_, bf16[256,1408]{1,0:T(8,128)(2,1)} %collective-permute-done.10.refs_1_, bf16[256,1408]{1,0:T(8,128)(2,1)S(1)} %copy-done.14, bf16[256,1408]{1,0:T(8,128)(2,1)S(1)} %copy-done.16, bf16[1152,1024]{1,0:T(8,128)(2,1)S(1)} %copy-done.23), custom_call_target="tpu_custom_call" | custom-call | flops 6643777536 | bytes 8486912 | tf_op jit(solution)/shard_map/pallas_call | solution.py:146
  510.5 52.6 %shard_map.336 = (f32[256,1408]{1,0:T(8,128)S(1)}, f32[8,1408]{1,0:T(8,128)S(1)}) custom-call(bf16[1152,1024]{1,0:T(8,128)(2,1)S(1)} %copy-done.24, bf16[1408,4672]{1,0:T(8,128)(2,1)} %all-gather.4.cloned.1.call-done.packed_ref.refs_10_), custom_call_target="tpu_custom_call" | custom-call | flops 60000002048 | bytes 10000000 | tf_op jit(solution)/shard_map/pallas_call | solution.py:222
  563.7 6.1 shard_map.337
  574.5 84.0 %shard_map.338 = (f32[256,1408]{1,0:T(8,128)}, f32[256,1408]{1,0:T(8,128)}, f32[16,1408]{1,0:T(8,128)}, f32[176,1056]{1,0:T(8,128)}, f32[80,1408]{1,0:T(8,128)}, /*index=5*/bf16[256,1408]{1,0:T(8,128)(2,1)}) custom-call(bf16[256,1408]{1,0:T(8,128)(2,1)} %copy-done.26, f32[8,1408]{1,0:T(8,128)} %copy-done.28, f32[8,1408]{1,0:T(8,128)} %copy-done.29, ...), custom_call_target="tpu_custom_call" | custom-call | flops 89999998976 | bytes 30000000 | tf_op jit(solution)/shard_map/pallas_call | solution.py:443
  678.5 53.0 %shard_map.339 = (f32[352,1408]{1,0:T(8,128)S(1)}, f32[176,128]{1,0:T(8,128)S(1)}) custom-call(bf16[176,2944]{1,0:T(8,128)(2,1)S(1)} %slice.491.in_ref), custom_call_target="tpu_custom_call" | custom-call | flops 40000000000 | bytes 4000000 | tf_op jit(solution)/shard_map/pallas_call | solution.py:530
  (489 shorter events, 304.0 us)
Async XLA Ops:
  7.2 94.0 %all-gather.4.cloned.1.call-start = ((), (), s32[]{:S(2)}) async-start(), calls=%async_computation.5 | async-start | bytes 15003648 | tf_op jit(solution)/shard_map/all_gather | solution.py:1036
  18.7 32.4 %collective-permute-start = (bf16[80,1408]{1,0:T(8,128)(2,1)}, bf16[80,1408]{1,0:T(8,128)(2,1)}, u32[]{:S(2)}, u32[]{:S(2)}) collective-permute-start(bf16[80,1408]{1,0:T(8,128)(2,1)} %param.23), channel_id=1, source_target_pairs={{0,1},{1,2},{2,3},{3,0},{4,5},{5,6},{6,7},{7,4},{8,9},{9,10},{10,1... | collective-permute-start | bytes 675848 | tf_op jit(solution)/shard_map/ppermute | solution.py:54
  18.7 32.4 %collective-permute-start.1 = (bf16[3,176,352]{2,1,0:T(8,128)(2,1)}, bf16[3,176,352]{2,1,0:T(8,128)(2,1)}, u32[]{:S(2)}, u32[]{:S(2)}) collective-permute-start(bf16[3,176,352]{2,1,0:T(8,128)(2,1)} %pad_maximum_fusion.3), channel_id=1, source_target_pairs={{0,1},{1,2},{2,3},{3,0},{4,5},{5,6},{6,7},{7,4},{8,9},{9,10},{10,1... | collective-permute-start | bytes 1115144 | tf_op jit(solution)/shard_map/ppermute | solution.py:54
  46.6 180.6 %all-gather.6.cloned.1.call-start = ((), (), s32[]{:S(2)}) async-start(), calls=%async_computation.6 | async-start | bytes 13381632 | tf_op jit(solution)/shard_map/all_gather | solution.py:1103
  83.8 186.2 %all-gather.8.cloned.1.call-start = ((), (), s32[]{:S(2)}) async-start(), calls=%async_computation.7 | async-start | bytes 9732096 | tf_op jit(solution)/shard_map/all_gather | solution.py:1105
  85.0 391.8 %reduce-scatter.4.cloned.1.call-start = ((), (), s32[]{:S(2)}) async-start(), calls=%async_computation.8 | async-start | bytes 9732096 | tf_op jit(solution)/shard_map/reduce_scatter | solution.py:1167
  172.3 24.8 %collective-permute-start.15 = (bf16[320,704]{1,0:T(8,128)(2,1)}, bf16[320,704]{1,0:T(8,128)(2,1)S(1)}, u32[]{:S(2)}, u32[]{:S(2)}) collective-permute-start(bf16[320,704]{1,0:T(8,128)(2,1)} %pad_maximum_fusion.2.refs_4_.refs_0_), channel_id=1, source_target_pairs={{0,3},{1,0},{2,1},{3,2},{4,7},{5,4},{6,5},{7,6},{8,11},{9,8},{10,9... | collective-permute-start | bytes 1351688 | tf_op jit(solution)/shard_map/ppermute | solution.py:54
  172.4 54.8 %collective-permute-start.14 = (bf16[320,704]{1,0:T(8,128)(2,1)}, bf16[320,704]{1,0:T(8,128)(2,1)}, u32[]{:S(2)}, u32[]{:S(2)}) collective-permute-start(bf16[320,704]{1,0:T(8,128)(2,1)} %pad_maximum_fusion.2.refs_4_.refs_0_), channel_id=1, source_target_pairs={{0,2},{1,3},{2,0},{3,1},{4,6},{5,7},{6,4},{7,5},{8,10},{9,11},{10,... | collective-permute-start | bytes 1351688 | tf_op jit(solution)/shard_map/ppermute | solution.py:54
  177.3 49.9 %collective-permute-start.13 = (bf16[320,704]{1,0:T(8,128)(2,1)}, bf16[320,704]{1,0:T(8,128)(2,1)}, u32[]{:S(2)}, u32[]{:S(2)}) collective-permute-start(bf16[320,704]{1,0:T(8,128)(2,1)} %pad_maximum_fusion.2.refs_4_.refs_0_), channel_id=1, source_target_pairs={{0,1},{1,2},{2,3},{3,0},{4,5},{5,6},{6,7},{7,4},{8,9},{9,10},{10,1... | collective-permute-start | bytes 1351688 | tf_op jit(solution)/shard_map/ppermute | solution.py:54
  197.2 25.5 %collective-permute-start.16 = (bf16[256,352]{1,0:T(8,128)(2,1)}, bf16[256,352]{1,0:T(8,128)(2,1)S(1)}, u32[]{:S(2)}, u32[]{:S(2)}) collective-permute-start(bf16[256,352]{1,0:T(8,128)(2,1)} %get-tuple-element.129), channel_id=1, source_target_pairs={{0,3},{1,0},{2,1},{3,2},{4,7},{5,4},{6,5},{7,6},{8,11},{9,8},{10,9... | collective-permute-start | bytes 540680 | tf_op jit(solution)/shard_map/ppermute | solution.py:54
  222.7 29.7 %collective-permute-start.19 = (bf16[256,1408]{1,0:T(8,128)(2,1)S(1)}, bf16[256,1408]{1,0:T(8,128)(2,1)S(1)}, u32[]{:S(2)}, u32[]{:S(2)}) collective-permute-start(bf16[256,1408]{1,0:T(8,128)(2,1)S(1)} %copy-done.18), channel_id=1, source_target_pairs={{0,1},{1,2},{2,3},{3,0},{4,5},{5,6},{6,7},{7,4},{8,9},{9,10},{10,1... | collective-permute-start | bytes 2162696 | tf_op jit(solution)/shard_map/ppermute | solution.py:54
  252.4 98.5 %collective-permute-start.20 = (bf16[256,1408]{1,0:T(8,128)(2,1)S(1)}, bf16[256,1408]{1,0:T(8,128)(2,1)}, u32[]{:S(2)}, u32[]{:S(2)}) collective-permute-start(bf16[256,1408]{1,0:T(8,128)(2,1)S(1)} %collective-permute-done.19.refs_2_), channel_id=1, source_target_pairs={{0,1},{1,2},{2,3},{3,0},{4,5},{5,6},{6,7},{7,4},{8,9},{9,10},{10,1... | collective-permute-start | bytes 2162696 | tf_op jit(solution)/shard_map/ppermute | solution.py:54
  269.9 27.3 %collective-permute-start.21 = (bf16[256,1408]{1,0:T(8,128)(2,1)}, bf16[256,1408]{1,0:T(8,128)(2,1)}, u32[]{:S(2)}, u32[]{:S(2)}) collective-permute-start(bf16[256,1408]{1,0:T(8,128)(2,1)} %get-tuple-element.138.refs_0_), channel_id=1, source_target_pairs={{0,1},{1,2},{2,3},{3,0},{4,5},{5,6},{6,7},{7,4},{8,9},{9,10},{10,1... | collective-permute-start | bytes 2162696 | tf_op jit(solution)/shard_map/ppermute | solution.py:54
  308.6 25.1 %collective-permute-start.24 = (bf16[256,1408]{1,0:T(8,128)(2,1)S(1)}, bf16[256,1408]{1,0:T(8,128)(2,1)S(1)}, u32[]{:S(2)}, u32[]{:S(2)}) collective-permute-start(bf16[256,1408]{1,0:T(8,128)(2,1)S(1)} %convolution_convert_fusion), channel_id=1, source_target_pairs={{0,1},{1,2},{2,3},{3,0},{4,5},{5,6},{6,7},{7,4},{8,9},{9,10},{10,1... | collective-permute-start | bytes 2162696 | tf_op jit(solution)/shard_map/ppermute | solution.py:54
  318.3 30.8 %collective-permute-start.23 = (bf16[256,1408]{1,0:T(8,128)(2,1)S(1)}, bf16[256,1408]{1,0:T(8,128)(2,1)S(1)}, u32[]{:S(2)}, u32[]{:S(2)}) collective-permute-start(bf16[256,1408]{1,0:T(8,128)(2,1)S(1)} %collective-permute-done.22.refs_2_), channel_id=1, source_target_pairs={{0,1},{1,2},{2,3},{3,0},{4,5},{5,6},{6,7},{7,4},{8,9},{9,10},{10,1... | collective-permute-start | bytes 2162696 | tf_op jit(solution)/shard_map/ppermute | solution.py:54
  335.1 23.7 %collective-permute-start.25 = (bf16[256,1408]{1,0:T(8,128)(2,1)S(1)}, bf16[256,1408]{1,0:T(8,128)(2,1)S(1)}, u32[]{:S(2)}, u32[]{:S(2)}) collective-permute-start(bf16[256,1408]{1,0:T(8,128)(2,1)S(1)} %add_convert_fusion.2), channel_id=1, source_target_pairs={{0,1},{1,2},{2,3},{3,0},{4,5},{5,6},{6,7},{7,4},{8,9},{9,10},{10,1... | collective-permute-start | bytes 2162696 | tf_op jit(solution)/shard_map/ppermute | solution.py:54
  359.8 23.7 %collective-permute-start.26 = (bf16[256,1408]{1,0:T(8,128)(2,1)}, bf16[256,1408]{1,0:T(8,128)(2,1)}, u32[]{:S(2)}, u32[]{:S(2)}) collective-permute-start(bf16[256,1408]{1,0:T(8,128)(2,1)} %add_convert_fusion.1), channel_id=1, source_target_pairs={{0,1},{1,2},{2,3},{3,0},{4,5},{5,6},{6,7},{7,4},{8,9},{9,10},{10,1... | collective-permute-start | bytes 2162696 | tf_op jit(solution)/shard_map/ppermute | solution.py:54
  386.4 184.9 %reduce-scatter.6.cloned.1.call-start = ((), (), s32[]{:S(2)}) async-start(), calls=%async_computation.9 | async-start | bytes 13381632 | tf_op jit(solution)/shard_map/reduce_scatter | solution.py:1185
  387.5 34.8 %collective-permute-start.27 = (bf16[256,1408]{1,0:T(8,128)(2,1)S(1)}, bf16[256,1408]{1,0:T(8,128)(2,1)S(1)}, u32[]{:S(2)}, u32[]{:S(2)}) collective-permute-start(bf16[256,1408]{1,0:T(8,128)(2,1)S(1)} %copy-done.71), channel_id=1, source_target_pairs={{0,1},{1,2},{2,3},{3,0},{4,5},{5,6},{6,7},{7,4},{8,9},{9,10},{10,1... | collective-permute-start | bytes 2162696 | tf_op jit(solution)/shard_map/ppermute | solution.py:54
  436.8 236.8 %reduce-scatter.8.cloned.1.call-start = ((), (), s32[]{:S(2)}) async-start(), calls=%async_computation.10 | async-start | bytes 15814656 | tf_op jit(solution)/shard_map/reduce_scatter | solution.py:1227
  445.9 34.1 %collective-permute-start.31 = (bf16[320,704]{1,0:T(8,128)(2,1)}, bf16[320,704]{1,0:T(8,128)(2,1)S(1)}, u32[]{:S(2)}, u32[]{:S(2)}) collective-permute-start(bf16[320,704]{1,0:T(8,128)(2,1)} %get-tuple-element.163), channel_id=1, source_target_pairs={{0,3},{1,0},{2,1},{3,2},{4,7},{5,4},{6,5},{7,6},{8,11},{9,8},{10,9... | collective-permute-start | bytes 1351688 | tf_op jit(solution)/shard_map/ppermute | solution.py:54
  445.9 34.9 %collective-permute-start.32 = (bf16[320,704]{1,0:T(8,128)(2,1)}, bf16[320,704]{1,0:T(8,128)(2,1)}, u32[]{:S(2)}, u32[]{:S(2)}) collective-permute-start(bf16[320,704]{1,0:T(8,128)(2,1)} %get-tuple-element.179), channel_id=1, source_target_pairs={{0,2},{1,3},{2,0},{3,1},{4,6},{5,7},{6,4},{7,5},{8,10},{9,11},{10,... | collective-permute-start | bytes 1351688 | tf_op jit(solution)/shard_map/ppermute | solution.py:54
  446.3 34.5 %collective-permute-start.33 = (bf16[320,704]{1,0:T(8,128)(2,1)}, bf16[320,704]{1,0:T(8,128)(2,1)}, u32[]{:S(2)}, u32[]{:S(2)}) collective-permute-start(bf16[320,704]{1,0:T(8,128)(2,1)} %get-tuple-element.180), channel_id=1, source_target_pairs={{0,1},{1,2},{2,3},{3,0},{4,5},{5,6},{6,7},{7,4},{8,9},{9,10},{10,1... | collective-permute-start | bytes 1351688 | tf_op jit(solution)/shard_map/ppermute | solution.py:54
  487.1 23.4 %collective-permute-start.34 = (bf16[256,1408]{1,0:T(8,128)(2,1)}, bf16[256,1408]{1,0:T(8,128)(2,1)}, u32[]{:S(2)}, u32[]{:S(2)}) collective-permute-start(bf16[256,1408]{1,0:T(8,128)(2,1)} %add_convert_fusion), channel_id=1, source_target_pairs={{0,1},{1,2},{2,3},{3,0},{4,5},{5,6},{6,7},{7,4},{8,9},{9,10},{10,1... | collective-permute-start | bytes 2162696 | tf_op jit(solution)/shard_map/ppermute | solution.py:54
  (99 other events, 824.8 us)
Sparse Core Ops, SparseCore 0:
  15.4 77.4 all-gather.3
  94.7 69.2 all-gather.5
  166.5 55.5 all-gather.7
  386.5 73.0 reduce-scatter.3
  463.4 89.7 reduce-scatter.5
  571.5 102.0 reduce-scatter.7

commit v4 on v3

--- a/solution.py
+++ b/solution.py
@@ -179,9 +179,20 @@
     return lax.rem(place + 1, split), lax.rem(place + split - 1, split)
 
 
-def ring_kernel(split, start, raw_ref, packed_ref, sum_out, shift_out, weights_ref, sent, got, load_sem, sems):
-    load = pltpu.make_async_copy(packed_ref.at[:, start : start + weights_ref.shape[1]], weights_ref, load_sem.at[0])
-    load.start()
+def ring_kernel(split, start, places, *refs):
+    raw_ref, left_refs, refs = refs[0], refs[1 : 1 + split], refs[1 + split :]
+    text_ref, ckv_ref, packed_ref, sum_out, shift_out, grads_ref = refs[:6]
+    weights_ref, turned, qkv_grad, text_grad, sent, got, load_sem, sems = refs[6:]
+    loads = [
+        pltpu.make_async_copy(packed_ref.at[:, start : start + weights_ref.shape[1]], weights_ref, load_sem.at[0]),
+        pltpu.make_async_copy(
+            qkv_grad, grads_ref.at[:, places[0] : places[0] + qkv_grad.shape[1]], load_sem.at[1]
+        ),
+        pltpu.make_async_copy(
+            text_grad, grads_ref.at[:, places[1] : places[1] + text_grad.shape[1]], load_sem.at[2]
+        ),
+    ]
+    loads[0].start()
     place = lax.axis_index("tensor")
     right, left = neighbours(place, split)
     barrier = pltpu.get_barrier_semaphore()
@@ -195,7 +206,27 @@
     def hop(step):
         return to_device(sent.at[step], got.at[step], sems.at[0, step], sems.at[1, step], {"tensor": right})
 
-    load.wait()
+    def qkv_lanes(some):
+        lanes = qkv_grad.shape[1] // 3
+        for i in some:
+            part = slice(i * lanes, (i + 1) * lanes)
+            qkv_grad[:, part] = dot(turned[...], raw_ref[part, :], NT).astype(BFLOAT)
+
+    def beside(step):
+        if step == 1:
+            for r in range(split):
+                turned[:, r * rows : (r + 1) * rows] = left_refs[r][...].T
+            qkv_lanes((0,))
+        elif step == 2:
+            qkv_lanes((1, 2))
+            loads[1].start()
+        elif step == 3:
+            wide = ckv_ref.shape[1]
+            text_grad[:, :wide] = dot(text_ref[...].T, ckv_ref[...]).astype(BFLOAT)
+            text_grad[:, wide:] = jnp.zeros((text_grad.shape[0], text_grad.shape[1] - wide), BFLOAT)
+            loads[2].start()
+
+    loads[0].wait()
     part = term(1)
     total = jnp.sum(part, axis=0, keepdims=True)
     sent[0] = part.astype(BFLOAT)
@@ -204,6 +235,7 @@
     for step in range(1, split):
         part = term((step + 1) % split)
         total = total + jnp.sum(part, axis=0, keepdims=True)
+        beside(step)
         hop(step - 1).wait_recv()
         part = part + got[step - 1].astype(FLOAT)
         if step + 1 < split:
@@ -212,30 +244,40 @@
         else:
             sum_out[...] = part
     shift_out[...] = jnp.broadcast_to(total, shift_out.shape)
+    loads[1].wait()
+    loads[2].wait()
     for step in range(split - 1):
         hop(step).wait_send()
 
 
-def ring_sum(raw, packed, start, split):
+def ring_sum(raw, lefts, text, ckv, packed, start, lanes, places, split):
     rows, width = raw.shape[1] // split, packed.shape[0]
     vmem = pl.BlockSpec(memory_space=pltpu.VMEM)
+    anywhere = pl.BlockSpec(memory_space=pl.ANY)
     return pl.pallas_call(
-        functools.partial(ring_kernel, split, start),
-        in_specs=[vmem, pl.BlockSpec(memory_space=pl.ANY)],
-        out_specs=(vmem,) * 2,
-        out_shape=(jax.ShapeDtypeStruct((rows, width), FLOAT), jax.ShapeDtypeStruct((8, width), FLOAT)),
+        functools.partial(ring_kernel, split, start, places),
+        in_specs=[vmem] * (3 + split) + [anywhere],
+        out_specs=(vmem, vmem, anywhere),
+        out_shape=(
+            jax.ShapeDtypeStruct((rows, width), FLOAT),
+            jax.ShapeDtypeStruct((8, width), FLOAT),
+            jax.ShapeDtypeStruct((width, lanes), BFLOAT),
+        ),
         scratch_shapes=[
             pltpu.VMEM((width, raw.shape[0]), BFLOAT),
+            pltpu.VMEM((width, raw.shape[1]), BFLOAT),
+            pltpu.VMEM((width, raw.shape[0]), BFLOAT),
+            pltpu.VMEM((width, lanes - places[1]), BFLOAT),
             pltpu.VMEM((split - 1, rows, width), BFLOAT),
             pltpu.VMEM((split - 1, rows, width), BFLOAT),
-            pltpu.SemaphoreType.DMA((1,)),
+            pltpu.SemaphoreType.DMA((3,)),
             pltpu.SemaphoreType.DMA((2, split - 1)),
         ],
         compiler_params=pltpu.CompilerParams(
-            vmem_limit_bytes=40 * 2**20, collective_id=1, has_side_effects=True
+            vmem_limit_bytes=48 * 2**20, collective_id=1, has_side_effects=True
         ),
         cost_estimate=pl.CostEstimate(flops=60_000_000_000, bytes_accessed=10_000_000, transcendentals=0),
-    )(raw, packed)
+    )(raw, *lefts, text, ckv, packed)
 
 
 def skip_kernel(
@@ -282,9 +324,9 @@
     )(grad, two, one, gain, left, packed)
 
 
-def side_kernel(shards, split, hops, *refs):
+def side_kernel(shards, split, hops, text_start, *refs):
     low_ref, late_ref, shift_ref, table_ref, latent_ref, skip_ref, base_ref, hop_ref, summed_ref, ckv_ref = refs[:10]
-    weights_ref, refs = refs[10], refs[11:]
+    weights_ref, text_packed_ref, refs = refs[10], refs[11], refs[12:]
     out_refs, refs = refs[: hops + 1], refs[hops + 1 :]
     latent_out, skip_out, table_out, full_out, text_out, block_out = refs[:6]
     weights, text_weights, full_refs, text_refs, full_got, text_got, hop_sent, hop_got, table_sent, table_got = refs[6:16]
@@ -299,9 +341,8 @@
         pltpu.make_async_copy(weights_ref.at[:, half * width : (half + 1) * width], weights, load_sem.at[half])
         for half in range(2)
     ]
-    text_wide = text_weights.shape[1]
-    text_start = weights_ref.shape[1] - text_wide
-    loads.append(pltpu.make_async_copy(weights_ref.at[:, text_start:], text_weights, load_sem.at[2]))
+    text_stop = text_start + text_weights.shape[1]
+    loads.append(pltpu.make_async_copy(text_packed_ref.at[:, text_start:text_stop], text_weights, load_sem.at[2]))
     loads[0].start()
     loads[2].start()
     barrier = pltpu.get_barrier_semaphore()
@@ -403,10 +444,10 @@
     for step in range(1, split):
         side(step, 0).start()
     loads[2].wait()
-    back = dot(ckv_ref[...], text_weights[...], NT).astype(BFLOAT)
+    back = dot(ckv_ref[...], text_weights[:, : ckv_ref.shape[1]], NT).astype(BFLOAT)
     own_text = text_out.shape[0]
     for r in range(split):
-        text_refs[r] = back[r * own_text : (r + 1) * own_text]
+        text_refs[lax.rem(place + split - r, split)] = back[r * own_text : (r + 1) * own_text]
     for step in range(1, split):
         side(step, 1).start()
     for step in range(1, hops):
@@ -432,7 +473,9 @@
             side(step, i).wait_send()
 
 
-def side_sums(low, late, shift, table, latent, skip_in, base, hop, summed, ckv, weights, out, shards, split):
+def side_sums(
+    low, late, shift, table, latent, skip_in, base, hop, summed, ckv, weights, text_packed, text_start, out, shards, split
+):
     rows, width = low.shape
     spare = pl.cdiv(shards, 8) * 8
     shares = shards.bit_length() - 1 + split.bit_length() - 1
@@ -441,8 +484,8 @@
     hops = len(out) - 1
     full, text = (summed.shape[0], summed.shape[1] // split), (ckv.shape[0] // split, width)
     return pl.pallas_call(
-        functools.partial(side_kernel, shards, split, hops),
-        in_specs=[vmem] * 10 + [pl.BlockSpec(memory_space=pl.ANY)] + [vmem] * len(out),
+        functools.partial(side_kernel, shards, split, hops, text_start),
+        in_specs=[vmem] * 10 + [pl.BlockSpec(memory_space=pl.ANY)] * 2 + [vmem] * len(out),
         out_specs=(vmem,) * 6,
         out_shape=(
             wide,
@@ -454,7 +497,7 @@
         ),
         scratch_shapes=[
             pltpu.VMEM((width, width), BFLOAT),
-            pltpu.VMEM((width, ckv.shape[1]), BFLOAT),
+            pltpu.VMEM((width, pl.cdiv(ckv.shape[1], LANES) * LANES), BFLOAT),
             pltpu.VMEM((split, *full), BFLOAT),
             pltpu.VMEM((split, *text), BFLOAT),
             pltpu.VMEM((split - 1, *full), BFLOAT),
@@ -472,7 +515,7 @@
             vmem_limit_bytes=56 * 2**20, collective_id=0, has_side_effects=True
         ),
         cost_estimate=pl.CostEstimate(flops=90_000_000_000, bytes_accessed=30_000_000, transcendentals=0),
-    )(low, late, shift, table, latent, skip_in, base, hop, summed, ckv, weights, *out)
+    )(low, late, shift, table, latent, skip_in, base, hop, summed, ckv, weights, text_packed, *out)
 
 
 def spread_kernel(split, starts, in_ref, skip_out, small_out, piece_sent, piece_got, pieces, whole, sems):
@@ -547,6 +590,40 @@
         ),
         cost_estimate=pl.CostEstimate(flops=40_000_000_000, bytes_accessed=4_000_000, transcendentals=0),
     )(values)
+
+
+def text_forward_kernel(parts, start, text_ref, bias_ref, gain_ref, group_ref, packed_ref, raw_ref, *refs):
+    low_refs, weights_ref, sems = refs[:parts], refs[parts], refs[parts + 1]
+    span = gain_ref.shape[1]
+    wide = 2 * span
+    load = pltpu.make_async_copy(packed_ref.at[:, start : start + parts * wide], weights_ref, sems.at[0])
+    load.start()
+    load.wait()
+    for r in range(parts):
+        raw = dot(text_ref[...], weights_ref[:, r * wide : (r + 1) * wide]) + bias_ref[r : r + 1, :]
+        if r == 0:
+            raw_ref[...] = raw
+        normed, _ = norm_heads(raw[:, :span], group_ref[...])
+        low_refs[r][:, :span] = (normed * gain_ref[r : r + 1, :]).astype(BFLOAT)
+        low_refs[r][:, span:] = raw[:, span:].astype(BFLOAT)
+
+
+def text_forward(text, packed, start, bias, gain, group):
+    parts, wide = bias.shape
+    tokens, width = text.shape
+    vmem = pl.BlockSpec(memory_space=pltpu.VMEM)
+    return pl.pallas_call(
+        functools.partial(text_forward_kernel, parts, start),
+        in_specs=[vmem] * 4 + [pl.BlockSpec(memory_space=pl.ANY)],
+        out_specs=(vmem,) * (1 + parts),
+        out_shape=(
+            jax.ShapeDtypeStruct((tokens, wide), FLOAT),
+            *[jax.ShapeDtypeStruct((tokens, wide), BFLOAT) for _ in range(parts)],
+        ),
+        scratch_shapes=[pltpu.VMEM((width, parts * wide), BFLOAT), pltpu.SemaphoreType.DMA((1,))],
+        compiler_params=pltpu.CompilerParams(vmem_limit_bytes=40 * 2**20),
+        cost_estimate=pl.CostEstimate(flops=12_000_000_000, bytes_accessed=10_000_000, transcendentals=0),
+    )(text, bias, gain, group, packed)
 
 
 def text_kernel(parts, *refs):
@@ -1029,27 +1106,31 @@
             skip_weight[:part],
             skip_weight[part:],
             dot(qkv_weight.reshape(part, 3 * span), expand).astype(BFLOAT),
-            text_weight.reshape(part, 2 * span),
         ],
         axis=1,
     )
     all_one = lax.all_gather(packed_one, "dp", axis=0, tiled=True)
     w_skip = all_one[:, : 2 * width]
     w_qkv = all_one[:, 2 * width : 2 * width + 3 * deep]
-    w_text = all_one[:, 2 * width + 3 * deep :]
-
-    own_full = jnp.stack([proj_weight.T, query_weight, cross_weight.T])
+
+    own_full = jnp.stack([proj_weight.T, query_weight, cross_weight.T, text_weight[:, 0], text_weight[:, 1]])
     full_blocks, text_blocks = [own_full], [text_tokens]
     for _ in range(split - 1):
         both = lax.optimization_barrier((full_blocks[-1], text_blocks[-1]))
         full_blocks.append(rot(both[0], 1))
         text_blocks.append(rot(both[1], 1))
     packed_two = jnp.concatenate(
-        [full_blocks[r][index] for index in range(3) for r in range(split)], axis=1
+        [full_blocks[r][index] for index in range(3) for r in range(split)]
+        + [full_blocks[r][index] for r in range(split) for index in (3, 4)],
+        axis=1,
     )
 
     cot_blocks = [out_grad, rot(after(out_grad, all_one, full_blocks[-1], text_blocks[-1]), 1)]
-    text_full = jnp.concatenate(text_blocks, axis=0)
+
+    text_length = own_text * split
+    text_full = jnp.zeros((text_length, width), BFLOAT)
+    for r in range(split):
+        text_full = lax.dynamic_update_slice_in_dim(text_full, text_blocks[r], others(r) * own_text, 0)
 
     def head_slice(index):
         return lax.dynamic_slice_in_dim(table[index], place * span, span, 0)
@@ -1122,20 +1203,15 @@
     def blocks_of(values, rows):
         return [values[r * rows : (r + 1) * rows] for r in range(split)]
 
-    text_raw = dot(text_full, w_text) + jnp.concatenate([head_slice(17), head_slice(18)])
-    text_length = text_raw.shape[0]
-    gain_21 = head_slice(21).reshape(heads, HD)
-    raw_key = text_raw[:, :span].reshape(text_length, heads, HD)
-    text_low = jnp.concatenate(
-        [head_norm(raw_key, gain_21).reshape(text_length, span), text_raw[:, span:]], axis=1
-    ).astype(BFLOAT)
-    text_rel = direct_gather(after(text_low, attn_blocks[-1]))
-    *mixed, text_rel[-1] = lax.optimization_barrier((*mixed, text_rel[-1]))
-    mixed = exchange(mixed)
-    cot_blocks[-1], mixed[-1] = lax.optimization_barrier((cot_blocks[-1], mixed[-1]))
-    cot_blocks.append(rot(cot_blocks[-1], 1))
     lane_head = np.arange(span) // HD
     group = jnp.asarray((lane_head[:, None] == lane_head[None, :]).astype(np.float32), BFLOAT)
+    text_bias = jnp.stack([relative(17).reshape(split, span), relative(18).reshape(split, span)], axis=1)
+    text_raw, *text_rel = text_forward(
+        text_full, all_two, 3 * width, text_bias.reshape(split, 2 * span), relative(21).reshape(split, span), group
+    )
+    mixed = exchange(mixed)
+    cot_blocks[-1], mixed[-1], text_rel[0] = lax.optimization_barrier((cot_blocks[-1], mixed[-1], text_rel[0]))
+    cot_blocks.append(rot(cot_blocks[-1], 1))
     middle_table = jnp.stack(
         [table[11], table[14], table[15], relative(16), relative(20), table[19], table[22], table[23]]
     )
@@ -1214,12 +1290,10 @@
     small_grads = jnp.concatenate([table_grad, bias_grad], axis=1).astype(BFLOAT)
     small_grads = jnp.pad(small_grads, ((0, 0), (0, qkv_start - 2 * width - small_grads.shape[1])))
 
-    grads_three = pack_grad(None, attn_blocks, [grad_raw], lanes_three, qkv_start, deep, turned=True)
-    grads_three = pack_grad(grads_three, [text_full], [ckv_low], lanes_three, text_start, LANES)
+    grad_attn_in, shift_part, grads_three = ring_sum(
+        grad_raw, attn_blocks, text_full, ckv_low, all_one, 2 * width, lanes_three, (qkv_start, text_start), split
+    )
     grads_three = lax.dynamic_update_slice(grads_three, small_grads, (0, 2 * width))
-    out_hop = rot(after((out_hop.astype(FLOAT) + out_parts[2]).astype(BFLOAT), ckv_low), 1)
-    grad_raw, grads_three, out_hop = lax.optimization_barrier((grad_raw, grads_three, out_hop))
-    grad_attn_in, shift_part = ring_sum(grad_raw, all_one, 2 * width, split)
     grads_three, one_low, late_rows = skip_grads(
         grads_three, grad_attn_in, grad_two, stream_one, table[6:7], normed_perm
     )
@@ -1227,21 +1301,21 @@
     summed_three = lax.psum_scatter(grads_three, "dp", scatter_dimension=0, tiled=True)
     latent_grad, skip_grad, late, full_sum, text_grad, block_out = side_sums(
         one_low, late_rows, shift_part, jnp.concatenate([table[:2], table[24:25]]), latent, skip_in, stream_three,
-        out_hop, summed_two, ckv_low, all_one, [out_parts[0], *out_parts[3:]], shards, split,
+        out_hop, summed_two, ckv_low, all_one, all_two, 3 * width, [out_parts[0], *out_parts[2:]], shards, split,
     )
     shift_grads = late[8 : 8 + shards]
     late = lax.dynamic_slice_in_dim(late[:8], me * part, part, 1)
+    silu_terms = lax.dot_general(
+        shift_grads, mod_weight.astype(FLOAT), ((NT), ((), ())), precision=HIGHEST, preferred_element_type=FLOAT
+    )
+    summed_three = after(summed_three, silu_terms, full_sum, text_grad, summed_one)
     mod_grad = lax.dot_general(
         silu_mine.astype(FLOAT), shift_grads, ((TN), ((), ())), precision=HIGHEST, preferred_element_type=FLOAT
     )
-    into_silu = lax.dot_general(
-        shift_grads, mod_weight.astype(FLOAT), ((NT), ((), ())), precision=HIGHEST, preferred_element_type=FLOAT
-    )
-    into_silu = lax.all_to_all(into_silu, "dp", 0, 0, tiled=True).reshape(1, width)
+    into_silu = lax.all_to_all(silu_terms, "dp", 0, 0, tiled=True).reshape(1, width)
     time_full = jax.vjp(silu, condition)[1](into_silu)[0]
     time_grad = lax.dynamic_slice_in_dim(time_full, place * (width // split), width // split, 1)
 
-    summed_three = after(summed_three, mod_grad, time_grad, full_sum, text_grad, summed_one)
     qkv_part = summed_three[:, qkv_start:text_start]
     text_part = summed_three[:, text_start : text_start + 2 * span]
     skip_weight_grad, small_sum = spread_sum(summed_three[:, :shared], width, split)

time: 763 us -> 751 us (0.984)
  starting transfers between devices: 121 us -> 74 us
  Pallas kernels: 325 us -> 355 us
  waiting for transfers between devices: 94.9 us -> 105 us
  local copies, waits for them, and re-layouts: 82.8 us -> 92.8 us
    ppermute x32 -> x28, starting transfers between devices: 111 us -> 63 us  [rot(): lax.ppermute(values, 'tensor', [(i, (i + step) % count) for i in range(co...]
    pallas_call x2 -> x3, Pallas kernels: 137 us -> 178 us  [the longest x1 106 us: side_sums(): pl.pallas_call(functools.partial(side_kernel, shards, split, hops, text_s...]
    all_gather x1, waiting for transfers between devices: 0.01 us -> 16.7 us  [on_device(): all_three = lax.all_gather(packed_three, 'dp', axis=0, tiled=True)]
    pallas_call x7 -> x5, Pallas kernels: 34.3 us -> 21.3 us  [pack_grad(): pl.pallas_call(functools.partial(grad_kernel, len(lefts), len(rights), tu...]
    dot_general x26 -> x25, matrix products: 71.1 us -> 64.7 us  [dot(): lax.dot_general(left, right, (contract, ((), ())), preferred_element_type...]
    ppermute x32 -> x28, waiting for transfers between devices: 87.2 us -> 81.2 us  [rot(): lax.ppermute(values, 'tensor', [(i, (i + step) % count) for i in range(co...]
    unnamed x172 -> x225, local copies, waits for them, and re-layouts: 34.7 us -> 40.2 us
  transfers between devices with their start and end apart: 43 -> 39, of which waited for: 18 -> 17; matrix products, arithmetic and copies ran while one was open for 19% -> 19% of each run, Pallas kernels for 36% -> 40%
where the time goes in v4:
time: 751 us; the launch traced here: 744 us
  Pallas kernels  355 us (47%)
  waiting for transfers between devices  105 us (14%)
  local copies, waits for them, and re-layouts  92.8 us (12%)
  starting transfers between devices  74 us (10%)
  matrix products  68.5 us (9%)
  other arithmetic  32 us (4%)
  between operations  17 us (2%)
    pallas_call x1, Pallas kernels, side_sums(): pl.pallas_call(functools.partial(side_kernel, shards, split, hops, text_s...  106 us
    ppermute x28, waiting for transfers between devices, rot(): lax.ppermute(values, 'tensor', [(i, (i + step) % count) for i in range(co...  81.2 us
    dot_general x25, matrix products, dot(): lax.dot_general(left, right, (contract, ((), ())), preferred_element_type...  64.7 us
    ppermute x28, starting transfers between devices, rot(): lax.ppermute(values, 'tensor', [(i, (i + step) % count) for i in range(co...  63 us
    pallas_call x1, Pallas kernels, ring_sum(): pl.pallas_call(functools.partial(ring_kernel, split, start, places), in_s...  62.4 us
    pallas_call x1, Pallas kernels, spread_sum(): pl.pallas_call(functools.partial(spread_kernel, split, starts), in_specs=...  54.9 us
    unnamed x225, local copies, waits for them, and re-layouts  40.2 us
    pallas_call x1, Pallas kernels, middle_backward(): pl.pallas_call(functools.partial(middle_backward_kernel, heads, len(text)...  30.2 us
  transfers between devices with their start and end apart: 39, of which 17 were waited for; matrix products, arithmetic and copies ran while one was open for 19% of the time, Pallas kernels for 40%

profile of v4, /device:TPU:24, one launch (start us, length us, event | category | flops | bytes accessed | tf_op | source)
XLA Modules:
  0.0 744.4 jit_solution(13375617779143934079)
XLA Ops:
  60.7 11.4 %collective-permute-done.3 = bf16[80,1408]{1,0:T(8,128)(2,1)} collective-permute-done((bf16[80,1408]{1,0:T(8,128)(2,1)}, bf16[80,1408]{1,0:T(8,128)(2,1)}, u32[]{:S(2)}, u32[]{:S(2)}) %collective-permute-start.3) | collective-permute-done | bytes 225312 | tf_op jit(solution)/shard_map/ppermute | solution.py:54
  78.8 11.0 %collective-permute-done.4 = bf16[5,176,352]{2,1,0:T(8,128)(2,1)S(1)} collective-permute-done((bf16[5,176,352]{2,1,0:T(8,128)(2,1)}, bf16[5,176,352]{2,1,0:T(8,128)(2,1)S(1)}, u32[]{:S(2)}, u32[]{:S(2)}) %collective-permute-start.4) | collective-permute-done | bytes 619552 | tf_op jit(solution)/shard_map/ppermute | solution.py:54
  90.7 5.5 concatenate.149
  138.2 5.8 collective-permute-done.10.refs_2_
  149.3 4.5 convolution_add_fusion.3.refs_0_
  153.8 6.4 collective-permute-done.11.refs_3_
  177.8 14.9 %shard_map.324 = (bf16[256,352]{1,0:T(8,128)(2,1)}, bf16[256,352]{1,0:T(8,128)(2,1)}, bf16[256,352]{1,0:T(8,128)(2,1)}, bf16[256,352]{1,0:T(8,128)(2,1)}, bf16[4...) custom-call(f32[1152,256]{1,0:T(8,128)} %convolution_add_fusion.3.re, ...), custom_call_target="tpu_custom_call" | custom-call | flops 20000000000 | bytes 12000000 | tf_op jit(solution)/shard_map/pallas_call | solution.py:758
  192.8 4.6 collective-permute-start.14
  201.0 9.2 %shard_map.325 = (f32[320,704]{1,0:T(8,128)S(1)}, bf16[320,704]{1,0:T(8,128)(2,1)S(1)}, bf16[320,704]{1,0:T(8,128)(2,1)S(1)}, bf16[320,704]{1,0:T(8,128)(2,1)S(1)}, bf16[320,704]{1,0:T(8,128)(2,1)S(1)}) custom-call(bf16[320,1408]{1,0:T(8,128)(2,1)S(1)} %constant_dynamic-update-slice_fusion.text_ref.refs_5_, f32[4,704]{1,0:T(4,128)S(1)} %reshape.395.bias_ref, ...), custom_call_target="tpu_custom_call" | custom-call | flops 12000000000 | bytes 10000000 | tf_op jit(solution)/shard_map/pallas_call | solution.py:615
  215.6 23.7 %shard_map.326 = (f32[256,1408]{1,0:T(8,128)}, f32[256,1408]{1,0:T(8,128)}, f32[256,1408]{1,0:T(8,128)}, bf16[256,1408]{1,0:T(8,128)(2,1)}, bf16[256,1408]{1,0:T...) custom-call(bf16[256,352]{1,0:T(8,128)(2,1)} %get-tuple-element.128.refs_0_, ...), custom_call_target="tpu_custom_call" | custom-call | flops 25999998976 | bytes 24000000 | tf_op jit(solution)/shard_map/pallas_call | solution.py:957
  242.3 16.7 %all-gather.8.cloned.1.call-done = bf16[1408,3072]{1,0:T(8,128)(2,1)} async-done(((bf16[176,3072]{1,0:T(8,128)(2,1)}), bf16[1408,3072]{1,0:T(8,128)(2,1)}) %all-gather.8.cloned.1.call-update) | async-done | bytes 8650768 | tf_op jit(solution)/shard_map/all_gather | solution.py:1186
  286.3 7.0 collective-permute-done.19.refs_2_
  303.1 5.6 collective-permute-done.21
  317.0 7.1 collective-permute-done.20.refs_3_
  330.0 7.7 %collective-permute-done.22 = bf16[256,1408]{1,0:T(8,128)(2,1)S(1)} collective-permute-done((bf16[256,1408]{1,0:T(8,128)(2,1)S(1)}, bf16[256,1408]{1,0:T(8,128)(2,1)S(1)}, u32[]{:S(2)}, u32[]{:S(2)}) %collective-permute-start.22) | collective-permute-done | bytes 720928 | tf_op jit(solution)/shard_map/ppermute | solution.py:54
  342.9 8.4 %shard_map.327.refs_8_ = bf16[1408,3072]{1,0:T(8,128)(2,1)} custom-call(bf16[256,1408]{1,0:T(8,128)(2,1)S(1)} %copy-done.18, bf16[256,1408]{1,0:T(8,128)(2,1)} %collective-permute-done.18.refs_1_, bf16[256,1408]{1,0:T(8,128)(2,1)S(1)} %collective-permute-done.19.refs_2_, bf16[256,1408]{1,0:T(8,128)(2,1)S(1)} %collective-permute-done.20.refs_3_, ...), custom_call_target="tpu_custom_call" | custom-call | flops 8858370048 | bytes 10354688 | tf_op jit(solution)/shard_map/pallas_call | solution.py:146
  353.8 8.6 %shard_map.328 = bf16[1408,3072]{1,0:T(8,128)(2,1)} custom-call(bf16[256,1408]{1,0:T(8,128)(2,1)} %refs_5_.2, bf16[256,1408]{1,0:T(8,128)(2,1)S(1)} %copy-done.17, bf16[256,1408]{1,0:T(8,128)(2,1)} %collective-permute-done.16.refs_2_, bf16[256,1408]{1,0:T(8,128)(2,1)S(1)} %collective-permute-done.17.refs_3_, ...), custom_call_target="tpu_custom_call", output_to_operand_aliasing={{}: (8, {})} | custom-call | flops 8858370048 | bytes 10354688 | tf_op jit(solution)/shard_map/pallas_call | solution.py:146
  366.5 30.2 %shard_map.329 = (bf16[256,1408]{1,0:T(8,128)(2,1)}, bf16[256,1408]{1,0:T(8,128)(2,1)}, bf16[256,1408]{1,0:T(8,128)(2,1)}, f32[256,1408]{1,0:T(8,128)}, f32[8,14...) custom-call(bf16[320,704]{1,0:T(8,128)(2,1)} %copy-done.28, ...), custom_call_target="tpu_custom_call" | custom-call | flops 32999999488 | bytes 28000000 | tf_op jit(solution)/shard_map/pallas_call | solution.py:1044
  411.4 7.7 %collective-permute-done.26.refs_14_ = bf16[256,352]{1,0:T(8,128)(2,1)S(1)} collective-permute-done((bf16[256,352]{1,0:T(8,128)(2,1)S(1)}, bf16[256,352]{1,0:T(8,128)(2,1)S(1)}, u32[]{:S(2)}, u32[]{:S(2)}) %collective-permute-start.26) | collective-permute-done | bytes 180256 | tf_op jit(solution)/shard_map/ppermute | solution.py:54
  429.6 22.3 %shard_map.333 = (bf16[1152,1024]{1,0:T(8,128)(2,1)}, f32[768,128]{1,0:T(8,128)}, f32[1152,128]{1,0:T(8,128)}) custom-call(f32[1152,256]{1,0:T(8,128)} %convolution_add_fusion.3.refs_0_, f32[1152,256]{1,0:T(8,128)} %convolution_add_fusion.2.refs_1_, f32[1152,256]{1,0:T(8,128)} %convolution_add_fusion.1.refs_2_, f32[1152,256]{1,0:T(8,128)} %convolution_add_fusion.refs_3_, ...), custom_call_target="tpu_custom_call" | custom-call | flops 28000000000 | bytes 16000000 | tf_op jit(solution)/shard_map/pallas_call | solution.py:845
  470.0 62.4 %shard_map.335 = (f32[256,1408]{1,0:T(8,128)S(1)}, f32[8,1408]{1,0:T(8,128)S(1)}, bf16[1408,4992]{1,0:T(8,128)(2,1)}) custom-call(bf16[1152,1024]{1,0:T(8,128)(2,1)} %get-tuple-element.172.refs_0_, bf16[256,1408]{1,0:T(8,128)(2,1)} %add_convert_fusion.2.refs_1_, bf16[256,1408]{1,0:T(8,128)(2,1)S(1)} %copy-done.11, bf16[256,1408]{1,0:T(8,128)(2,1)S(1)} %copy-done.13, ...), custom_call_target="tpu_custom_call" | custom-call | flops 60000002048 | bytes 10000000 | tf_op jit(solution)/shard_map/pallas_call | solution.py:257
  533.5 6.1 shard_map.336
  544.3 106.4 %shard_map.337 = (f32[256,1408]{1,0:T(8,128)}, f32[256,1408]{1,0:T(8,128)}, f32[16,1408]{1,0:T(8,128)}, f32[176,1056]{1,0:T(8,128)}, f32[80,1408]{1,0:T(8,128)}, /*index=5*/bf16[256,1408]{1,0:T(8,128)(2,1)}) custom-call(bf16[256,1408]{1,0:T(8,128)(2,1)} %copy-done.24, f32[8,1408]{1,0:T(8,128)} %copy-done.32, f32[8,1408]{1,0:T(8,128)} %copy-done.33, ...), custom_call_target="tpu_custom_call" | custom-call | flops 89999998976 | bytes 30000000 | tf_op jit(solution)/shard_map/pallas_call | solution.py:486
  668.4 54.9 %shard_map.338 = (f32[352,1408]{1,0:T(8,128)S(1)}, f32[176,128]{1,0:T(8,128)S(1)}) custom-call(bf16[176,2944]{1,0:T(8,128)(2,1)S(1)} %slice.519.in_ref), custom_call_target="tpu_custom_call" | custom-call | flops 40000000000 | bytes 4000000 | tf_op jit(solution)/shard_map/pallas_call | solution.py:573
  (527 shorter events, 279.2 us)
Async XLA Ops:
  7.2 101.8 %all-gather.4.cloned.1.call-start = ((), (), s32[]{:S(2)}) async-start(), calls=%async_computation.5 | async-start | bytes 12570624 | tf_op jit(solution)/shard_map/all_gather | solution.py:1112
  18.9 30.7 %collective-permute-start.1 = (bf16[80,1408]{1,0:T(8,128)(2,1)}, bf16[80,1408]{1,0:T(8,128)(2,1)}, u32[]{:S(2)}, u32[]{:S(2)}) collective-permute-start(bf16[80,1408]{1,0:T(8,128)(2,1)} %param.23), channel_id=1, source_target_pairs={{0,1},{1,2},{2,3},{3,0},{4,5},{5,6},{6,7},{7,4},{8,9},{9,10},{10,1... | collective-permute-start | bytes 675848 | tf_op jit(solution)/shard_map/ppermute | solution.py:54
  18.9 30.7 %collective-permute-start = (bf16[5,176,352]{2,1,0:T(8,128)(2,1)}, bf16[5,176,352]{2,1,0:T(8,128)(2,1)}, u32[]{:S(2)}, u32[]{:S(2)}) collective-permute-start(bf16[5,176,352]{2,1,0:T(8,128)(2,1)} %bitcast_dynamic-update-slice_fusion.2), channel_id=1, source_target_pairs={{0,1},{1,2},{2,3},{3,0},{4,5},{5,6},{6,7},{7,4},{8,9},{9,10},{10,1... | collective-permute-start | bytes 1858568 | tf_op jit(solution)/shard_map/ppermute | solution.py:54
  47.6 153.3 %all-gather.6.cloned.1.call-start = ((), (), s32[]{:S(2)}) async-start(), calls=%async_computation.6 | async-start | bytes 22302720 | tf_op jit(solution)/shard_map/all_gather | solution.py:1184
  49.6 22.6 %collective-permute-start.2 = (bf16[5,176,352]{2,1,0:T(8,128)(2,1)}, bf16[5,176,352]{2,1,0:T(8,128)(2,1)}, u32[]{:S(2)}, u32[]{:S(2)}) collective-permute-start(bf16[5,176,352]{2,1,0:T(8,128)(2,1)} %collective-permute-done), channel_id=1, source_target_pairs={{0,1},{1,2},{2,3},{3,0},{4,5},{5,6},{6,7},{7,4},{8,9},{9,10},{10,1... | collective-permute-start | bytes 1858568 | tf_op jit(solution)/shard_map/ppermute | solution.py:54
  96.2 162.8 %all-gather.8.cloned.1.call-start = ((), (), s32[]{:S(2)}) async-start(), calls=%async_computation.7 | async-start | bytes 9732096 | tf_op jit(solution)/shard_map/all_gather | solution.py:1186
  98.6 358.4 %reduce-scatter.4.cloned.1.call-start = ((), (), s32[]{:S(2)}) async-start(), calls=%async_computation.8 | async-start | bytes 9732096 | tf_op jit(solution)/shard_map/reduce_scatter | solution.py:1243
  192.7 21.5 %collective-permute-start.13 = (bf16[256,352]{1,0:T(8,128)(2,1)}, bf16[256,352]{1,0:T(8,128)(2,1)S(1)}, u32[]{:S(2)}, u32[]{:S(2)}) collective-permute-start(bf16[256,352]{1,0:T(8,128)(2,1)} %get-tuple-element.120), channel_id=1, source_target_pairs={{0,3},{1,0},{2,1},{3,2},{4,7},{5,4},{6,5},{7,6},{8,11},{9,8},{10,9... | collective-permute-start | bytes 540680 | tf_op jit(solution)/shard_map/ppermute | solution.py:54
  192.8 22.0 %collective-permute-start.14 = (bf16[256,352]{1,0:T(8,128)(2,1)}, bf16[256,352]{1,0:T(8,128)(2,1)S(1)}, u32[]{:S(2)}, u32[]{:S(2)}) collective-permute-start(bf16[256,352]{1,0:T(8,128)(2,1)} %get-tuple-element.129), channel_id=1, source_target_pairs={{0,1},{1,2},{2,3},{3,0},{4,5},{5,6},{6,7},{7,4},{8,9},{9,10},{10,1... | collective-permute-start | bytes 540680 | tf_op jit(solution)/shard_map/ppermute | solution.py:54
  214.3 25.0 %collective-permute-start.16 = (bf16[256,1408]{1,0:T(8,128)(2,1)S(1)}, bf16[256,1408]{1,0:T(8,128)(2,1)}, u32[]{:S(2)}, u32[]{:S(2)}) collective-permute-start(bf16[256,1408]{1,0:T(8,128)(2,1)S(1)} %copy-done.17), channel_id=1, source_target_pairs={{0,1},{1,2},{2,3},{3,0},{4,5},{5,6},{6,7},{7,4},{8,9},{9,10},{10,1... | collective-permute-start | bytes 2162696 | tf_op jit(solution)/shard_map/ppermute | solution.py:54
  239.3 86.6 %collective-permute-start.17 = (bf16[256,1408]{1,0:T(8,128)(2,1)}, bf16[256,1408]{1,0:T(8,128)(2,1)S(1)}, u32[]{:S(2)}, u32[]{:S(2)}) collective-permute-start(bf16[256,1408]{1,0:T(8,128)(2,1)} %collective-permute-done.16.refs_2_), channel_id=1, source_target_pairs={{0,1},{1,2},{2,3},{3,0},{4,5},{5,6},{6,7},{7,4},{8,9},{9,10},{10,1... | collective-permute-start | bytes 2162696 | tf_op jit(solution)/shard_map/ppermute | solution.py:54
  240.8 32.3 %collective-permute-start.18 = (bf16[256,1408]{1,0:T(8,128)(2,1)}, bf16[256,1408]{1,0:T(8,128)(2,1)}, u32[]{:S(2)}, u32[]{:S(2)}) collective-permute-start(bf16[256,1408]{1,0:T(8,128)(2,1)} %get-tuple-element.134.refs_0_), channel_id=1, source_target_pairs={{0,1},{1,2},{2,3},{3,0},{4,5},{5,6},{6,7},{7,4},{8,9},{9,10},{10,1... | collective-permute-start | bytes 2162696 | tf_op jit(solution)/shard_map/ppermute | solution.py:54
  273.1 20.2 %collective-permute-start.19 = (bf16[256,1408]{1,0:T(8,128)(2,1)}, bf16[256,1408]{1,0:T(8,128)(2,1)S(1)}, u32[]{:S(2)}, u32[]{:S(2)}) collective-permute-start(bf16[256,1408]{1,0:T(8,128)(2,1)} %collective-permute-done.18.refs_1_), channel_id=1, source_target_pairs={{0,1},{1,2},{2,3},{3,0},{4,5},{5,6},{6,7},{7,4},{8,9},{9,10},{10,1... | collective-permute-start | bytes 2162696 | tf_op jit(solution)/shard_map/ppermute | solution.py:54
  283.5 25.1 %collective-permute-start.21 = (bf16[256,1408]{1,0:T(8,128)(2,1)S(1)}, bf16[256,1408]{1,0:T(8,128)(2,1)S(1)}, u32[]{:S(2)}, u32[]{:S(2)}) collective-permute-start(bf16[256,1408]{1,0:T(8,128)(2,1)S(1)} %convolution_convert_fusion), channel_id=1, source_target_pairs={{0,1},{1,2},{2,3},{3,0},{4,5},{5,6},{6,7},{7,4},{8,9},{9,10},{10,1... | collective-permute-start | bytes 2162696 | tf_op jit(solution)/shard_map/ppermute | solution.py:54
  293.3 30.8 %collective-permute-start.20 = (bf16[256,1408]{1,0:T(8,128)(2,1)S(1)}, bf16[256,1408]{1,0:T(8,128)(2,1)S(1)}, u32[]{:S(2)}, u32[]{:S(2)}) collective-permute-start(bf16[256,1408]{1,0:T(8,128)(2,1)S(1)} %collective-permute-done.19.refs_2_), channel_id=1, source_target_pairs={{0,1},{1,2},{2,3},{3,0},{4,5},{5,6},{6,7},{7,4},{8,9},{9,10},{10,1... | collective-permute-start | bytes 2162696 | tf_op jit(solution)/shard_map/ppermute | solution.py:54
  310.1 27.6 %collective-permute-start.22 = (bf16[256,1408]{1,0:T(8,128)(2,1)S(1)}, bf16[256,1408]{1,0:T(8,128)(2,1)S(1)}, u32[]{:S(2)}, u32[]{:S(2)}) collective-permute-start(bf16[256,1408]{1,0:T(8,128)(2,1)S(1)} %add_convert_fusion.1), channel_id=1, source_target_pairs={{0,1},{1,2},{2,3},{3,0},{4,5},{5,6},{6,7},{7,4},{8,9},{9,10},{10,1... | collective-permute-start | bytes 2162696 | tf_op jit(solution)/shard_map/ppermute | solution.py:54
  338.7 23.7 %collective-permute-start.23 = (bf16[256,1408]{1,0:T(8,128)(2,1)}, bf16[256,1408]{1,0:T(8,128)(2,1)}, u32[]{:S(2)}, u32[]{:S(2)}) collective-permute-start(bf16[256,1408]{1,0:T(8,128)(2,1)} %add_convert_fusion), channel_id=1, source_target_pairs={{0,1},{1,2},{2,3},{3,0},{4,5},{5,6},{6,7},{7,4},{8,9},{9,10},{10,1... | collective-permute-start | bytes 2162696 | tf_op jit(solution)/shard_map/ppermute | solution.py:54
  365.3 175.8 %reduce-scatter.6.cloned.1.call-start = ((), (), s32[]{:S(2)}) async-start(), calls=%async_computation.9 | async-start | bytes 13381632 | tf_op jit(solution)/shard_map/reduce_scatter | solution.py:1261
  366.4 34.6 %collective-permute-start.24 = (bf16[256,1408]{1,0:T(8,128)(2,1)S(1)}, bf16[256,1408]{1,0:T(8,128)(2,1)S(1)}, u32[]{:S(2)}, u32[]{:S(2)}) collective-permute-start(bf16[256,1408]{1,0:T(8,128)(2,1)S(1)} %copy-done.93), channel_id=1, source_target_pairs={{0,1},{1,2},{2,3},{3,0},{4,5},{5,6},{6,7},{7,4},{8,9},{9,10},{10,1... | collective-permute-start | bytes 2162696 | tf_op jit(solution)/shard_map/ppermute | solution.py:54
  401.1 18.0 %collective-permute-start.26 = (bf16[256,352]{1,0:T(8,128)(2,1)S(1)}, bf16[256,352]{1,0:T(8,128)(2,1)S(1)}, u32[]{:S(2)}, u32[]{:S(2)}) collective-permute-start(bf16[256,352]{1,0:T(8,128)(2,1)S(1)} %copy-done.98), channel_id=1, source_target_pairs={{0,2},{1,3},{2,0},{3,1},{4,6},{5,7},{6,4},{7,5},{8,10},{9,11},{10,... | collective-permute-start | bytes 540680 | tf_op jit(solution)/shard_map/ppermute | solution.py:54
  419.8 243.7 %reduce-scatter.8.cloned.1.call-start = ((), (), s32[]{:S(2)}) async-start(), calls=%async_computation.10 | async-start | bytes 15814656 | tf_op jit(solution)/shard_map/reduce_scatter | solution.py:1301
  425.7 34.4 %collective-permute-start.28 = (bf16[320,704]{1,0:T(8,128)(2,1)}, bf16[320,704]{1,0:T(8,128)(2,1)S(1)}, u32[]{:S(2)}, u32[]{:S(2)}) collective-permute-start(bf16[320,704]{1,0:T(8,128)(2,1)} %get-tuple-element.159), channel_id=1, source_target_pairs={{0,3},{1,0},{2,1},{3,2},{4,7},{5,4},{6,5},{7,6},{8,11},{9,8},{10,9... | collective-permute-start | bytes 1351688 | tf_op jit(solution)/shard_map/ppermute | solution.py:54
  425.7 34.3 %collective-permute-start.29 = (bf16[320,704]{1,0:T(8,128)(2,1)}, bf16[320,704]{1,0:T(8,128)(2,1)}, u32[]{:S(2)}, u32[]{:S(2)}) collective-permute-start(bf16[320,704]{1,0:T(8,128)(2,1)} %get-tuple-element.175), channel_id=1, source_target_pairs={{0,2},{1,3},{2,0},{3,1},{4,6},{5,7},{6,4},{7,5},{8,10},{9,11},{10,... | collective-permute-start | bytes 1351688 | tf_op jit(solution)/shard_map/ppermute | solution.py:54
  425.8 34.3 %collective-permute-start.30 = (bf16[320,704]{1,0:T(8,128)(2,1)}, bf16[320,704]{1,0:T(8,128)(2,1)}, u32[]{:S(2)}, u32[]{:S(2)}) collective-permute-start(bf16[320,704]{1,0:T(8,128)(2,1)} %get-tuple-element.176), channel_id=1, source_target_pairs={{0,1},{1,2},{2,3},{3,0},{4,5},{5,6},{6,7},{7,4},{8,9},{9,10},{10,1... | collective-permute-start | bytes 1351688 | tf_op jit(solution)/shard_map/ppermute | solution.py:54
  (121 other events, 947.3 us)
Sparse Core Ops, SparseCore 0:
  13.2 68.7 all-gather.3
  96.3 104.5 all-gather.5
  203.4 55.5 all-gather.7
  365.4 72.6 reduce-scatter.3
  441.9 89.7 reduce-scatter.5
  541.3 103.5 reduce-scatter.7

commit v5 on v4

--- a/solution.py
+++ b/solution.py
@@ -1125,7 +1125,6 @@
         axis=1,
     )
 
-    cot_blocks = [out_grad, rot(after(out_grad, all_one, full_blocks[-1], text_blocks[-1]), 1)]
 
     text_length = own_text * split
     text_full = jnp.zeros((text_length, width), BFLOAT)
@@ -1171,7 +1170,7 @@
     turn = grid_rel[:, None, :] * rate[None]
     turns = jnp.stack([jnp.cos(turn[0]), jnp.sin(turn[0]), jnp.cos(turn[1]), jnp.sin(turn[1])])
 
-    silu_mine = lax.dynamic_slice_in_dim(silu_all, me * part, part, 1)
+    silu_mine = after(lax.dynamic_slice_in_dim(silu_all, me * part, part, 1), full_blocks[1])
     shift_terms = dot(silu_mine, mod_weight)
     shift = jnp.sum(lax.all_to_all(shift_terms, "dp", 0, 0, tiled=True), axis=0, keepdims=True) + table[5]
 
@@ -1180,17 +1179,18 @@
     joined_bias = jnp.concatenate([table[2], table[3]])
     normed_low = layer_norm(joined, joined_gain, joined_bias).astype(BFLOAT)
     normed_perm = normed_low.reshape(own_rows, shards, 2, part).transpose(0, 2, 1, 3).reshape(own_rows, 2 * width)
+    stream_one = (
+        dot(normed_perm[:, :width], w_skip[:, :width]) + dot(normed_perm[:, width:], w_skip[:, width:]) + table[4]
+    )
     packed_two = after(packed_two, normed_perm, shift, turns)
     all_two = lax.all_gather(packed_two, "dp", axis=0, tiled=True)
     packed_three = jnp.concatenate([up_weight, down_weight.T], axis=1)
     all_three = lax.all_gather(packed_three, "dp", axis=0, tiled=True)
     w_up, w_down_t = all_three[:, :hidden], all_three[:, hidden:]
 
-    stream_one = (
-        dot(normed_perm[:, :width], w_skip[:, :width]) + dot(normed_perm[:, width:], w_skip[:, width:]) + table[4]
-    )
     attn_low = (layer_norm(stream_one, table[6], table[7]) + shift).astype(BFLOAT)
-    attn_blocks = ring_gather(after(attn_low, cot_blocks[1]))
+    attn_blocks = ring_gather(attn_low)
+    cot_blocks = [out_grad, rot(after(out_grad, attn_blocks[-1]), 1)]
     qkv_bias = deepen(jnp.stack([head_slice(8), head_slice(9), head_slice(10)]))[:, None]
     raws = [dot(w_qkv, block, ((0,), (1,))) + qkv_bias for block in attn_blocks]
     zero_slice = jnp.zeros((span,), FLOAT)
@@ -1199,6 +1199,7 @@
     block = min(512, length)
     kept = attend_forward(raws, turns, gains, heads, block)
     mixed, kept = kept[:split], kept[split:]
+    *mixed, cot_blocks[1] = lax.optimization_barrier((*mixed, cot_blocks[1]))
 
     def blocks_of(values, rows):
         return [values[r * rows : (r + 1) * rows] for r in range(split)]

time: 751 us -> 749 us (level)
    unnamed x225 -> x227, local copies, waits for them, and re-layouts: 40.2 us -> 38.2 us
  transfers between devices with their start and end apart: 39 -> 39, of which waited for: 17 -> 16; matrix products, arithmetic and copies ran while one was open for 19% -> 19% of each run, Pallas kernels for 40% -> 41%
where the time goes in v5:
time: 749 us; the launch traced here: 740 us
  Pallas kernels  355 us (47%)
  waiting for transfers between devices  108 us (14%)
  local copies, waits for them, and re-layouts  91.1 us (12%)
  starting transfers between devices  70 us (9%)
  matrix products  69.3 us (9%)
  other arithmetic  29.5 us (4%)
  between operations  17.1 us (2%)
    pallas_call x1, Pallas kernels, side_sums(): pl.pallas_call(functools.partial(side_kernel, shards, split, hops, text_s...  107 us
    ppermute x28, waiting for transfers between devices, rot(): lax.ppermute(values, 'tensor', [(i, (i + step) % count) for i in range(co...  77.5 us
    dot_general x25, matrix products, dot(): lax.dot_general(left, right, (contract, ((), ())), preferred_element_type...  65.5 us
    pallas_call x1, Pallas kernels, ring_sum(): pl.pallas_call(functools.partial(ring_kernel, split, start, places), in_s...  62.6 us
    ppermute x28, starting transfers between devices, rot(): lax.ppermute(values, 'tensor', [(i, (i + step) % count) for i in range(co...  58.2 us
    pallas_call x1, Pallas kernels, spread_sum(): pl.pallas_call(functools.partial(spread_kernel, split, starts), in_specs=...  54.8 us
    unnamed x227, local copies, waits for them, and re-layouts  38.2 us
    pallas_call x1, Pallas kernels, middle_backward(): pl.pallas_call(functools.partial(middle_backward_kernel, heads, len(text)...  30.2 us
  transfers between devices with their start and end apart: 39, of which 16 were waited for; matrix products, arithmetic and copies ran while one was open for 19% of the time, Pallas kernels for 41%

profile of v5, /device:TPU:24, one launch (start us, length us, event | category | flops | bytes accessed | tf_op | source)
XLA Modules:
  0.0 739.7 jit_solution(5839317254062692850)
XLA Ops:
  58.4 10.7 %collective-permute-done.10 = bf16[80,1408]{1,0:T(8,128)(2,1)S(1)} collective-permute-done((bf16[80,1408]{1,0:T(8,128)(2,1)}, bf16[80,1408]{1,0:T(8,128)(2,1)S(1)}, u32[]{:S(2)}, u32[]{:S(2)}) %collective-permute-start.10) | collective-permute-done | bytes 225312 | tf_op jit(solution)/shard_map/ppermute | solution.py:54
  77.2 7.9 %collective-permute-done.13 = bf16[5,176,352]{2,1,0:T(8,128)(2,1)S(1)} collective-permute-done((bf16[5,176,352]{2,1,0:T(8,128)(2,1)}, bf16[5,176,352]{2,1,0:T(8,128)(2,1)S(1)}, u32[]{:S(2)}, u32[]{:S(2)}) %collective-permute-start.13) | collective-permute-done | bytes 619552 | tf_op jit(solution)/shard_map/ppermute | solution.py:54
  85.9 5.3 concatenate.149
  118.0 10.2 %collective-permute-done.4.refs_2_ = bf16[256,1408]{1,0:T(8,128)(2,1)} collective-permute-done((bf16[256,1408]{1,0:T(8,128)(2,1)}, bf16[256,1408]{1,0:T(8,128)(2,1)}, u32[]{:S(2)}, u32[]{:S(2)}) %collective-permute-start.4) | collective-permute-done | bytes 720928 | tf_op jit(solution)/shard_map/ppermute | solution.py:54
  137.5 7.3 collective-permute-done.5.refs_3_
  155.5 5.3 collective-permute-done.6.refs_4_
  168.4 14.8 %shard_map.324 = (bf16[256,352]{1,0:T(8,128)(2,1)}, bf16[256,352]{1,0:T(8,128)(2,1)}, bf16[256,352]{1,0:T(8,128)(2,1)}, bf16[256,352]{1,0:T(8,128)(2,1)}, bf16[4...) custom-call(f32[1152,256]{1,0:T(8,128)} %convolution_add_fusion.3.re, ...), custom_call_target="tpu_custom_call" | custom-call | flops 20000000000 | bytes 12000000 | tf_op jit(solution)/shard_map/pallas_call | solution.py:758
  187.1 9.5 %all-gather.6.cloned.1.call-done.packed_ref.refs_11_.refs_12_ = bf16[1408,7040]{1,0:T(8,128)(2,1)} async-done(((bf16[176,7040]{1,0:T(8,128)(2,1)}), bf16[1408,7040]{1,0:T(8,128)(2,1)}) %all-gather.6.cloned.1.call-update) | async-done | bytes 19824656 | tf_op jit(solution)/shard_map/all_gather | solution.py:1186
  196.6 9.2 %shard_map.325 = (f32[320,704]{1,0:T(8,128)S(1)}, bf16[320,704]{1,0:T(8,128)(2,1)S(1)}, bf16[320,704]{1,0:T(8,128)(2,1)S(1)}, bf16[320,704]{1,0:T(8,128)(2,1)S(1)}, bf16[320,704]{1,0:T(8,128)(2,1)S(1)}) custom-call(bf16[320,1408]{1,0:T(8,128)(2,1)S(1)} %constant_dynamic-update-slice_fusion.text_ref.refs_5_, f32[4,704]{1,0:T(4,128)S(1)} %reshape.395.bias_ref, ...), custom_call_target="tpu_custom_call" | custom-call | flops 12000000000 | bytes 10000000 | tf_op jit(solution)/shard_map/pallas_call | solution.py:615
  211.6 23.7 %shard_map.326 = (f32[256,1408]{1,0:T(8,128)}, f32[256,1408]{1,0:T(8,128)}, f32[256,1408]{1,0:T(8,128)}, bf16[256,1408]{1,0:T(8,128)(2,1)}, bf16[256,1408]{1,0:T...) custom-call(bf16[256,352]{1,0:T(8,128)(2,1)} %get-tuple-element.138.refs_0_, ...), custom_call_target="tpu_custom_call" | custom-call | flops 25999998976 | bytes 24000000 | tf_op jit(solution)/shard_map/pallas_call | solution.py:957
  238.3 16.3 %all-gather.8.cloned.1.call-done = bf16[1408,3072]{1,0:T(8,128)(2,1)} async-done(((bf16[176,3072]{1,0:T(8,128)(2,1)}), bf16[1408,3072]{1,0:T(8,128)(2,1)}) %all-gather.8.cloned.1.call-update) | async-done | bytes 8650768 | tf_op jit(solution)/shard_map/all_gather | solution.py:1188
  282.3 7.0 collective-permute-done.19.refs_2_
  299.1 5.6 collective-permute-done.21
  313.0 7.2 collective-permute-done.20.refs_3_
  327.2 6.5 collective-permute-done.22
  338.9 8.4 %shard_map.327.refs_8_ = bf16[1408,3072]{1,0:T(8,128)(2,1)} custom-call(bf16[256,1408]{1,0:T(8,128)(2,1)S(1)} %copy-done.16, bf16[256,1408]{1,0:T(8,128)(2,1)} %collective-permute-done.18.refs_1_, bf16[256,1408]{1,0:T(8,128)(2,1)S(1)} %collective-permute-done.19.refs_2_, bf16[256,1408]{1,0:T(8,128)(2,1)S(1)} %collective-permute-done.20.refs_3_, ...), custom_call_target="tpu_custom_call" | custom-call | flops 8858370048 | bytes 10354688 | tf_op jit(solution)/shard_map/pallas_call | solution.py:146
  349.9 8.6 %shard_map.328 = bf16[1408,3072]{1,0:T(8,128)(2,1)} custom-call(bf16[256,1408]{1,0:T(8,128)(2,1)S(1)} %copy-done.8, bf16[256,1408]{1,0:T(8,128)(2,1)S(1)} %collective-permute-done.7.refs_1_, bf16[256,1408]{1,0:T(8,128)(2,1)} %collective-permute-done.16.refs_2_, bf16[256,1408]{1,0:T(8,128)(2,1)} %collective-permute-done.17.refs_3_, ...), custom_call_target="tpu_custom_call", output_to_operand_aliasing={{}: (8, {})} | custom-call | flops 8858370048 | bytes 10354688 | tf_op jit(solution)/shard_map/pallas_call | solution.py:146
  362.6 30.2 %shard_map.329 = (bf16[256,1408]{1,0:T(8,128)(2,1)}, bf16[256,1408]{1,0:T(8,128)(2,1)}, bf16[256,1408]{1,0:T(8,128)(2,1)}, f32[256,1408]{1,0:T(8,128)}, f32[8,14...) custom-call(bf16[320,704]{1,0:T(8,128)(2,1)} %copy-done.26, ...), custom_call_target="tpu_custom_call" | custom-call | flops 32999999488 | bytes 28000000 | tf_op jit(solution)/shard_map/pallas_call | solution.py:1044
  407.4 7.7 %collective-permute-done.26.refs_14_ = bf16[256,352]{1,0:T(8,128)(2,1)S(1)} collective-permute-done((bf16[256,352]{1,0:T(8,128)(2,1)S(1)}, bf16[256,352]{1,0:T(8,128)(2,1)S(1)}, u32[]{:S(2)}, u32[]{:S(2)}) %collective-permute-start.26) | collective-permute-done | bytes 180256 | tf_op jit(solution)/shard_map/ppermute | solution.py:54
  424.4 21.8 %shard_map.333 = (bf16[1152,1024]{1,0:T(8,128)(2,1)}, f32[768,128]{1,0:T(8,128)}, f32[1152,128]{1,0:T(8,128)}) custom-call(f32[1152,256]{1,0:T(8,128)} %convolution_add_fusion.3.refs_0_, f32[1152,256]{1,0:T(8,128)} %convolution_add_fusion.2.refs_1_, f32[1152,256]{1,0:T(8,128)} %convolution_add_fusion.1.refs_2_, f32[1152,256]{1,0:T(8,128)} %convolution_add_fusion.refs_3_, ...), custom_call_target="tpu_custom_call" | custom-call | flops 28000000000 | bytes 16000000 | tf_op jit(solution)/shard_map/pallas_call | solution.py:845
  463.7 62.6 %shard_map.335 = (f32[256,1408]{1,0:T(8,128)S(1)}, f32[8,1408]{1,0:T(8,128)S(1)}, bf16[1408,4992]{1,0:T(8,128)(2,1)}) custom-call(bf16[1152,1024]{1,0:T(8,128)(2,1)} %get-tuple-element.182.refs_0_, bf16[256,1408]{1,0:T(8,128)(2,1)} %add_convert_fusion.2.refs_1_, bf16[256,1408]{1,0:T(8,128)(2,1)} %collective-permute-done.4.refs_2_, ...), custom_call_target="tpu_custom_call" | custom-call | flops 60000002048 | bytes 10000000 | tf_op jit(solution)/shard_map/pallas_call | solution.py:257
  527.4 6.1 shard_map.336
  538.2 106.8 %shard_map.337 = (f32[256,1408]{1,0:T(8,128)}, f32[256,1408]{1,0:T(8,128)}, f32[16,1408]{1,0:T(8,128)}, f32[176,1056]{1,0:T(8,128)}, f32[80,1408]{1,0:T(8,128)}, /*index=5*/bf16[256,1408]{1,0:T(8,128)(2,1)}) custom-call(bf16[256,1408]{1,0:T(8,128)(2,1)} %copy-done.22, f32[8,1408]{1,0:T(8,128)} %copy-done.30, f32[8,1408]{1,0:T(8,128)} %copy-done.31, ...), custom_call_target="tpu_custom_call" | custom-call | flops 89999998976 | bytes 30000000 | tf_op jit(solution)/shard_map/pallas_call | solution.py:486
  663.9 54.8 %shard_map.338 = (f32[352,1408]{1,0:T(8,128)S(1)}, f32[176,128]{1,0:T(8,128)S(1)}) custom-call(bf16[176,2944]{1,0:T(8,128)(2,1)S(1)} %slice.519.in_ref), custom_call_target="tpu_custom_call" | custom-call | flops 40000000000 | bytes 4000000 | tf_op jit(solution)/shard_map/pallas_call | solution.py:573
  (530 shorter events, 269.0 us)
Async XLA Ops:
  7.2 90.0 %all-gather.4.cloned.1.call-start = ((), (), s32[]{:S(2)}) async-start(), calls=%async_computation.5 | async-start | bytes 12570624 | tf_op jit(solution)/shard_map/all_gather | solution.py:1112
  18.9 29.7 %collective-permute-start.9 = (bf16[80,1408]{1,0:T(8,128)(2,1)}, bf16[80,1408]{1,0:T(8,128)(2,1)}, u32[]{:S(2)}, u32[]{:S(2)}) collective-permute-start(bf16[80,1408]{1,0:T(8,128)(2,1)} %param.23), channel_id=1, source_target_pairs={{0,1},{1,2},{2,3},{3,0},{4,5},{5,6},{6,7},{7,4},{8,9},{9,10},{10,1... | collective-permute-start | bytes 675848 | tf_op jit(solution)/shard_map/ppermute | solution.py:54
  18.9 29.7 %collective-permute-start.3 = (bf16[5,176,352]{2,1,0:T(8,128)(2,1)}, bf16[5,176,352]{2,1,0:T(8,128)(2,1)}, u32[]{:S(2)}, u32[]{:S(2)}) collective-permute-start(bf16[5,176,352]{2,1,0:T(8,128)(2,1)} %bitcast_dynamic-update-slice_fusion.2), channel_id=1, source_target_pairs={{0,1},{1,2},{2,3},{3,0},{4,5},{5,6},{6,7},{7,4},{8,9},{9,10},{10,1... | collective-permute-start | bytes 1858568 | tf_op jit(solution)/shard_map/ppermute | solution.py:54
  58.3 138.3 %all-gather.6.cloned.1.call-start = ((), (), s32[]{:S(2)}) async-start(), calls=%async_computation.6 | async-start | bytes 22302720 | tf_op jit(solution)/shard_map/all_gather | solution.py:1186
  91.3 163.3 %all-gather.8.cloned.1.call-start = ((), (), s32[]{:S(2)}) async-start(), calls=%async_computation.7 | async-start | bytes 9732096 | tf_op jit(solution)/shard_map/all_gather | solution.py:1188
  93.7 357.7 %reduce-scatter.4.cloned.1.call-start = ((), (), s32[]{:S(2)}) async-start(), calls=%async_computation.8 | async-start | bytes 9732096 | tf_op jit(solution)/shard_map/reduce_scatter | solution.py:1244
  106.8 21.4 %collective-permute-start.4 = (bf16[256,1408]{1,0:T(8,128)(2,1)}, bf16[256,1408]{1,0:T(8,128)(2,1)}, u32[]{:S(2)}, u32[]{:S(2)}) collective-permute-start(bf16[256,1408]{1,0:T(8,128)(2,1)} %add_convert_fusion.2.refs_1_), channel_id=1, source_target_pairs={{0,1},{1,2},{2,3},{3,0},{4,5},{5,6},{6,7},{7,4},{8,9},{9,10},{10,1... | collective-permute-start | bytes 2162696 | tf_op jit(solution)/shard_map/ppermute | solution.py:54
  160.8 22.4 %collective-permute-start.7 = (bf16[256,1408]{1,0:T(8,128)(2,1)S(1)}, bf16[256,1408]{1,0:T(8,128)(2,1)S(1)}, u32[]{:S(2)}, u32[]{:S(2)}) collective-permute-start(bf16[256,1408]{1,0:T(8,128)(2,1)S(1)} %copy-done.8), channel_id=1, source_target_pairs={{0,1},{1,2},{2,3},{3,0},{4,5},{5,6},{6,7},{7,4},{8,9},{9,10},{10,1... | collective-permute-start | bytes 2162696 | tf_op jit(solution)/shard_map/ppermute | solution.py:54
  183.2 26.7 %collective-permute-start.8 = (bf16[256,352]{1,0:T(8,128)(2,1)}, bf16[256,352]{1,0:T(8,128)(2,1)S(1)}, u32[]{:S(2)}, u32[]{:S(2)}) collective-permute-start(bf16[256,352]{1,0:T(8,128)(2,1)} %get-tuple-element.125), channel_id=1, source_target_pairs={{0,3},{1,0},{2,1},{3,2},{4,7},{5,4},{6,5},{7,6},{8,11},{9,8},{10,9... | collective-permute-start | bytes 540680 | tf_op jit(solution)/shard_map/ppermute | solution.py:54
  183.3 27.6 %collective-permute-start.14 = (bf16[256,352]{1,0:T(8,128)(2,1)}, bf16[256,352]{1,0:T(8,128)(2,1)S(1)}, u32[]{:S(2)}, u32[]{:S(2)}) collective-permute-start(bf16[256,352]{1,0:T(8,128)(2,1)} %get-tuple-element.139), channel_id=1, source_target_pairs={{0,1},{1,2},{2,3},{3,0},{4,5},{5,6},{6,7},{7,4},{8,9},{9,10},{10,1... | collective-permute-start | bytes 540680 | tf_op jit(solution)/shard_map/ppermute | solution.py:54
  187.1 23.8 %collective-permute-start.15 = (bf16[256,352]{1,0:T(8,128)(2,1)}, bf16[256,352]{1,0:T(8,128)(2,1)}, u32[]{:S(2)}, u32[]{:S(2)}) collective-permute-start(bf16[256,352]{1,0:T(8,128)(2,1)} %get-tuple-element.140), channel_id=1, source_target_pairs={{0,2},{1,3},{2,0},{3,1},{4,6},{5,7},{6,4},{7,5},{8,10},{9,11},{10,... | collective-permute-start | bytes 540680 | tf_op jit(solution)/shard_map/ppermute | solution.py:54
  210.0 25.3 %collective-permute-start.16 = (bf16[256,1408]{1,0:T(8,128)(2,1)S(1)}, bf16[256,1408]{1,0:T(8,128)(2,1)}, u32[]{:S(2)}, u32[]{:S(2)}) collective-permute-start(bf16[256,1408]{1,0:T(8,128)(2,1)S(1)} %collective-permute-done.7.refs_1_), channel_id=1, source_target_pairs={{0,1},{1,2},{2,3},{3,0},{4,5},{5,6},{6,7},{7,4},{8,9},{9,10},{10,1... | collective-permute-start | bytes 2162696 | tf_op jit(solution)/shard_map/ppermute | solution.py:54
  235.3 86.6 %collective-permute-start.17 = (bf16[256,1408]{1,0:T(8,128)(2,1)}, bf16[256,1408]{1,0:T(8,128)(2,1)}, u32[]{:S(2)}, u32[]{:S(2)}) collective-permute-start(bf16[256,1408]{1,0:T(8,128)(2,1)} %collective-permute-done.16.refs_2_), channel_id=1, source_target_pairs={{0,1},{1,2},{2,3},{3,0},{4,5},{5,6},{6,7},{7,4},{8,9},{9,10},{10,1... | collective-permute-start | bytes 2162696 | tf_op jit(solution)/shard_map/ppermute | solution.py:54
  236.8 32.3 %collective-permute-start.18 = (bf16[256,1408]{1,0:T(8,128)(2,1)}, bf16[256,1408]{1,0:T(8,128)(2,1)}, u32[]{:S(2)}, u32[]{:S(2)}) collective-permute-start(bf16[256,1408]{1,0:T(8,128)(2,1)} %get-tuple-element.144.refs_0_), channel_id=1, source_target_pairs={{0,1},{1,2},{2,3},{3,0},{4,5},{5,6},{6,7},{7,4},{8,9},{9,10},{10,1... | collective-permute-start | bytes 2162696 | tf_op jit(solution)/shard_map/ppermute | solution.py:54
  279.5 25.1 %collective-permute-start.21 = (bf16[256,1408]{1,0:T(8,128)(2,1)S(1)}, bf16[256,1408]{1,0:T(8,128)(2,1)S(1)}, u32[]{:S(2)}, u32[]{:S(2)}) collective-permute-start(bf16[256,1408]{1,0:T(8,128)(2,1)S(1)} %convolution_convert_fusion), channel_id=1, source_target_pairs={{0,1},{1,2},{2,3},{3,0},{4,5},{5,6},{6,7},{7,4},{8,9},{9,10},{10,1... | collective-permute-start | bytes 2162696 | tf_op jit(solution)/shard_map/ppermute | solution.py:54
  289.3 30.8 %collective-permute-start.20 = (bf16[256,1408]{1,0:T(8,128)(2,1)S(1)}, bf16[256,1408]{1,0:T(8,128)(2,1)S(1)}, u32[]{:S(2)}, u32[]{:S(2)}) collective-permute-start(bf16[256,1408]{1,0:T(8,128)(2,1)S(1)} %collective-permute-done.19.refs_2_), channel_id=1, source_target_pairs={{0,1},{1,2},{2,3},{3,0},{4,5},{5,6},{6,7},{7,4},{8,9},{9,10},{10,1... | collective-permute-start | bytes 2162696 | tf_op jit(solution)/shard_map/ppermute | solution.py:54
  306.1 27.6 %collective-permute-start.22 = (bf16[256,1408]{1,0:T(8,128)(2,1)S(1)}, bf16[256,1408]{1,0:T(8,128)(2,1)S(1)}, u32[]{:S(2)}, u32[]{:S(2)}) collective-permute-start(bf16[256,1408]{1,0:T(8,128)(2,1)S(1)} %add_convert_fusion.1), channel_id=1, source_target_pairs={{0,1},{1,2},{2,3},{3,0},{4,5},{5,6},{6,7},{7,4},{8,9},{9,10},{10,1... | collective-permute-start | bytes 2162696 | tf_op jit(solution)/shard_map/ppermute | solution.py:54
  334.6 23.8 %collective-permute-start.23 = (bf16[256,1408]{1,0:T(8,128)(2,1)}, bf16[256,1408]{1,0:T(8,128)(2,1)}, u32[]{:S(2)}, u32[]{:S(2)}) collective-permute-start(bf16[256,1408]{1,0:T(8,128)(2,1)} %add_convert_fusion), channel_id=1, source_target_pairs={{0,1},{1,2},{2,3},{3,0},{4,5},{5,6},{6,7},{7,4},{8,9},{9,10},{10,1... | collective-permute-start | bytes 2162696 | tf_op jit(solution)/shard_map/ppermute | solution.py:54
  361.3 173.7 %reduce-scatter.6.cloned.1.call-start = ((), (), s32[]{:S(2)}) async-start(), calls=%async_computation.9 | async-start | bytes 13381632 | tf_op jit(solution)/shard_map/reduce_scatter | solution.py:1262
  362.4 34.7 %collective-permute-start.24 = (bf16[256,1408]{1,0:T(8,128)(2,1)S(1)}, bf16[256,1408]{1,0:T(8,128)(2,1)S(1)}, u32[]{:S(2)}, u32[]{:S(2)}) collective-permute-start(bf16[256,1408]{1,0:T(8,128)(2,1)S(1)} %copy-done.95), channel_id=1, source_target_pairs={{0,1},{1,2},{2,3},{3,0},{4,5},{5,6},{6,7},{7,4},{8,9},{9,10},{10,1... | collective-permute-start | bytes 2162696 | tf_op jit(solution)/shard_map/ppermute | solution.py:54
  415.8 243.2 %reduce-scatter.8.cloned.1.call-start = ((), (), s32[]{:S(2)}) async-start(), calls=%async_computation.10 | async-start | bytes 15814656 | tf_op jit(solution)/shard_map/reduce_scatter | solution.py:1302
  420.6 34.2 %collective-permute-start.28 = (bf16[320,704]{1,0:T(8,128)(2,1)}, bf16[320,704]{1,0:T(8,128)(2,1)S(1)}, u32[]{:S(2)}, u32[]{:S(2)}) collective-permute-start(bf16[320,704]{1,0:T(8,128)(2,1)} %get-tuple-element.169), channel_id=1, source_target_pairs={{0,3},{1,0},{2,1},{3,2},{4,7},{5,4},{6,5},{7,6},{8,11},{9,8},{10,9... | collective-permute-start | bytes 1351688 | tf_op jit(solution)/shard_map/ppermute | solution.py:54
  420.6 34.1 %collective-permute-start.29 = (bf16[320,704]{1,0:T(8,128)(2,1)}, bf16[320,704]{1,0:T(8,128)(2,1)}, u32[]{:S(2)}, u32[]{:S(2)}) collective-permute-start(bf16[320,704]{1,0:T(8,128)(2,1)} %get-tuple-element.185), channel_id=1, source_target_pairs={{0,2},{1,3},{2,0},{3,1},{4,6},{5,7},{6,4},{7,5},{8,10},{9,11},{10,... | collective-permute-start | bytes 1351688 | tf_op jit(solution)/shard_map/ppermute | solution.py:54
  420.7 34.0 %collective-permute-start.30 = (bf16[320,704]{1,0:T(8,128)(2,1)}, bf16[320,704]{1,0:T(8,128)(2,1)}, u32[]{:S(2)}, u32[]{:S(2)}) collective-permute-start(bf16[320,704]{1,0:T(8,128)(2,1)} %get-tuple-element.186), channel_id=1, source_target_pairs={{0,1},{1,2},{2,3},{3,0},{4,5},{5,6},{6,7},{7,4},{8,9},{9,10},{10,1... | collective-permute-start | bytes 1351688 | tf_op jit(solution)/shard_map/ppermute | solution.py:54
  (122 other events, 1070.5 us)
Sparse Core Ops, SparseCore 0:
  13.2 68.7 all-gather.3
  91.4 105.1 all-gather.5
  199.1 55.4 all-gather.7
  361.4 72.6 reduce-scatter.3
  437.9 89.7 reduce-scatter.5
  535.2 103.8 reduce-scatter.7

commit v6 on v5

--- a/solution.py
+++ b/solution.py
@@ -1223,6 +1223,7 @@
     while len(cot_blocks) < split:
         cot_blocks.append(rot(cot_blocks[-1], 1))
     mlp_blocks = ring_gather(mlp_low)
+    w_up, w_down_t, mlp_blocks[1] = lax.optimization_barrier((w_up, w_down_t, mlp_blocks[1]))
     hidden_bias = lax.dynamic_slice_in_dim(bias_all, place * hidden, hidden, 0)
 
     hidden_lows, pre_lows, out_parts, back_parts = [], [], [], []

time: 749 us -> 751 us (level)
  waiting for transfers between devices: 108 us -> 125 us
  Pallas kernels: 355 us -> 346 us
    pallas_call x1, Pallas kernels: 107 us -> 88.1 us  [side_sums(): pl.pallas_call(functools.partial(side_kernel, shards, split, hops, text_s...]
    ppermute x28, waiting for transfers between devices: 77.5 us -> 93.8 us  [rot(): lax.ppermute(values, 'tensor', [(i, (i + step) % count) for i in range(co...]
    pallas_call x1, Pallas kernels: 54.8 us -> 65.7 us  [spread_sum(): pl.pallas_call(functools.partial(spread_kernel, split, starts), in_specs=...]
    unnamed x227 -> x233, local copies, waits for them, and re-layouts: 38.2 us -> 38.5 us
  transfers between devices with their start and end apart: 39 -> 39, of which waited for: 16 -> 14; matrix products, arithmetic and copies ran while one was open for 19% -> 18% of each run, Pallas kernels for 41% -> 38%
where the time goes in v6:
time: 751 us; the launch traced here: 742 us
  Pallas kernels  346 us (46%)
  waiting for transfers between devices  125 us (17%)
  local copies, waits for them, and re-layouts  94.9 us (13%)
  starting transfers between devices  67.2 us (9%)
  matrix products  66.6 us (9%)
  other arithmetic  25.5 us (3%)
  between operations  17.1 us (2%)
    ppermute x28, waiting for transfers between devices, rot(): lax.ppermute(values, 'tensor', [(i, (i + step) % count) for i in range(co...  93.8 us
    pallas_call x1, Pallas kernels, side_sums(): pl.pallas_call(functools.partial(side_kernel, shards, split, hops, text_s...  88.1 us
    pallas_call x1, Pallas kernels, spread_sum(): pl.pallas_call(functools.partial(spread_kernel, split, starts), in_specs=...  65.7 us
    dot_general x25, matrix products, dot(): lax.dot_general(left, right, (contract, ((), ())), preferred_element_type...  62.8 us
    pallas_call x1, Pallas kernels, ring_sum(): pl.pallas_call(functools.partial(ring_kernel, split, start, places), in_s...  61.2 us
    ppermute x28, starting transfers between devices, rot(): lax.ppermute(values, 'tensor', [(i, (i + step) % count) for i in range(co...  52.7 us
    unnamed x233, local copies, waits for them, and re-layouts  38.5 us
    pallas_call x1, Pallas kernels, middle_backward(): pl.pallas_call(functools.partial(middle_backward_kernel, heads, len(text)...  31.3 us
  transfers between devices with their start and end apart: 39, of which 14 were waited for; matrix products, arithmetic and copies ran while one was open for 18% of the time, Pallas kernels for 38%

profile of v6, /device:TPU:24, one launch (start us, length us, event | category | flops | bytes accessed | tf_op | source)
XLA Modules:
  0.0 742.0 jit_solution(4945889669905069041)
XLA Ops:
  58.0 10.7 %collective-permute-done.10 = bf16[80,1408]{1,0:T(8,128)(2,1)S(1)} collective-permute-done((bf16[80,1408]{1,0:T(8,128)(2,1)}, bf16[80,1408]{1,0:T(8,128)(2,1)S(1)}, u32[]{:S(2)}, u32[]{:S(2)}) %collective-permute-start.10) | collective-permute-done | bytes 225312 | tf_op jit(solution)/shard_map/ppermute | solution.py:54
  76.7 7.9 %collective-permute-done.13 = bf16[5,176,352]{2,1,0:T(8,128)(2,1)S(1)} collective-permute-done((bf16[5,176,352]{2,1,0:T(8,128)(2,1)}, bf16[5,176,352]{2,1,0:T(8,128)(2,1)S(1)}, u32[]{:S(2)}, u32[]{:S(2)}) %collective-permute-start.13) | collective-permute-done | bytes 619552 | tf_op jit(solution)/shard_map/ppermute | solution.py:54
  85.5 5.3 concatenate.149
  117.6 10.2 %collective-permute-done.4.refs_2_ = bf16[256,1408]{1,0:T(8,128)(2,1)} collective-permute-done((bf16[256,1408]{1,0:T(8,128)(2,1)}, bf16[256,1408]{1,0:T(8,128)(2,1)}, u32[]{:S(2)}, u32[]{:S(2)}) %collective-permute-start.4) | collective-permute-done | bytes 720928 | tf_op jit(solution)/shard_map/ppermute | solution.py:54
  137.0 7.4 collective-permute-done.5.refs_3_
  155.1 5.3 collective-permute-done.6.refs_4_
  167.9 14.8 %shard_map.324 = (bf16[256,352]{1,0:T(8,128)(2,1)}, bf16[256,352]{1,0:T(8,128)(2,1)}, bf16[256,352]{1,0:T(8,128)(2,1)}, bf16[256,352]{1,0:T(8,128)(2,1)}, bf16[4...) custom-call(f32[1152,256]{1,0:T(8,128)} %convolution_add_fusion.3.re, ...), custom_call_target="tpu_custom_call" | custom-call | flops 20000000000 | bytes 12000000 | tf_op jit(solution)/shard_map/pallas_call | solution.py:758
  186.7 9.5 %all-gather.6.cloned.1.call-done.packed_ref.refs_11_.refs_12_ = bf16[1408,7040]{1,0:T(8,128)(2,1)} async-done(((bf16[176,7040]{1,0:T(8,128)(2,1)}), bf16[1408,7040]{1,0:T(8,128)(2,1)}) %all-gather.6.cloned.1.call-update) | async-done | bytes 19824656 | tf_op jit(solution)/shard_map/all_gather | solution.py:1186
  196.2 9.2 %shard_map.325 = (f32[320,704]{1,0:T(8,128)S(1)}, bf16[320,704]{1,0:T(8,128)(2,1)S(1)}, bf16[320,704]{1,0:T(8,128)(2,1)S(1)}, bf16[320,704]{1,0:T(8,128)(2,1)S(1)}, bf16[320,704]{1,0:T(8,128)(2,1)S(1)}) custom-call(bf16[320,1408]{1,0:T(8,128)(2,1)S(1)} %constant_dynamic-update-slice_fusion.text_ref.refs_5_, f32[4,704]{1,0:T(4,128)S(1)} %reshape.395.bias_ref, ...), custom_call_target="tpu_custom_call" | custom-call | flops 12000000000 | bytes 10000000 | tf_op jit(solution)/shard_map/pallas_call | solution.py:615
  211.2 23.7 %shard_map.326 = (f32[256,1408]{1,0:T(8,128)}, f32[256,1408]{1,0:T(8,128)}, f32[256,1408]{1,0:T(8,128)}, bf16[256,1408]{1,0:T(8,128)(2,1)}, bf16[256,1408]{1,0:T...) custom-call(bf16[256,352]{1,0:T(8,128)(2,1)} %get-tuple-element.141.refs_0_, ...), custom_call_target="tpu_custom_call" | custom-call | flops 25999998976 | bytes 24000000 | tf_op jit(solution)/shard_map/pallas_call | solution.py:957
  237.2 17.0 %all-gather.8.cloned.1.call-done = bf16[1408,3072]{1,0:T(8,128)(2,1)} async-done(((bf16[176,3072]{1,0:T(8,128)(2,1)}), bf16[1408,3072]{1,0:T(8,128)(2,1)}) %all-gather.8.cloned.1.call-update) | async-done | bytes 8650768 | tf_op jit(solution)/shard_map/all_gather | solution.py:1188
  280.6 26.8 %collective-permute-done.19.refs_2_ = bf16[256,1408]{1,0:T(8,128)(2,1)S(1)} collective-permute-done((bf16[256,1408]{1,0:T(8,128)(2,1)}, bf16[256,1408]{1,0:T(8,128)(2,1)S(1)}, u32[]{:S(2)}, u32[]{:S(2)}) %collective-permute-start.19) | collective-permute-done | bytes 720928 | tf_op jit(solution)/shard_map/ppermute | solution.py:54
  316.5 10.0 %collective-permute-done.20.refs_3_ = bf16[256,1408]{1,0:T(8,128)(2,1)S(1)} collective-permute-done((bf16[256,1408]{1,0:T(8,128)(2,1)S(1)}, bf16[256,1408]{1,0:T(8,128)(2,1)S(1)}, u32[]{:S(2)}, u32[]{:S(2)}) %collective-permute-start.20) | collective-permute-done | bytes 720928 | tf_op jit(solution)/shard_map/ppermute | solution.py:54
  331.7 8.6 %collective-permute-done.22 = bf16[256,1408]{1,0:T(8,128)(2,1)S(1)} collective-permute-done((bf16[256,1408]{1,0:T(8,128)(2,1)S(1)}, bf16[256,1408]{1,0:T(8,128)(2,1)S(1)}, u32[]{:S(2)}, u32[]{:S(2)}) %collective-permute-start.22) | collective-permute-done | bytes 720928 | tf_op jit(solution)/shard_map/ppermute | solution.py:54
  346.7 8.4 %shard_map.327.refs_8_ = bf16[1408,3072]{1,0:T(8,128)(2,1)} custom-call(bf16[256,1408]{1,0:T(8,128)(2,1)S(1)} %copy-done.18, bf16[256,1408]{1,0:T(8,128)(2,1)} %collective-permute-done.18.refs_1_, bf16[256,1408]{1,0:T(8,128)(2,1)S(1)} %collective-permute-done.19.refs_2_, bf16[256,1408]{1,0:T(8,128)(2,1)S(1)} %collective-permute-done.20.refs_3_, ...), custom_call_target="tpu_custom_call" | custom-call | flops 8858370048 | bytes 10354688 | tf_op jit(solution)/shard_map/pallas_call | solution.py:146
  355.1 7.4 shard_map.328
  371.8 31.3 %shard_map.329 = (bf16[256,1408]{1,0:T(8,128)(2,1)}, bf16[256,1408]{1,0:T(8,128)(2,1)}, bf16[256,1408]{1,0:T(8,128)(2,1)}, f32[256,1408]{1,0:T(8,128)}, f32[8,14...) custom-call(bf16[320,704]{1,0:T(8,128)(2,1)} %copy-done.29, ...), custom_call_target="tpu_custom_call" | custom-call | flops 32999999488 | bytes 28000000 | tf_op jit(solution)/shard_map/pallas_call | solution.py:1044
  415.6 6.5 collective-permute-done.26.refs_14_
  433.0 22.2 %shard_map.333 = (bf16[1152,1024]{1,0:T(8,128)(2,1)}, f32[768,128]{1,0:T(8,128)}, f32[1152,128]{1,0:T(8,128)}) custom-call(f32[1152,256]{1,0:T(8,128)} %convolution_add_fusion.3.refs_0_, f32[1152,256]{1,0:T(8,128)} %convolution_add_fusion.2.refs_1_, f32[1152,256]{1,0:T(8,128)} %convolution_add_fusion.1.refs_2_, f32[1152,256]{1,0:T(8,128)} %convolution_add_fusion.refs_3_, ...), custom_call_target="tpu_custom_call" | custom-call | flops 28000000000 | bytes 16000000 | tf_op jit(solution)/shard_map/pallas_call | solution.py:845
  472.3 61.2 %shard_map.335 = (f32[256,1408]{1,0:T(8,128)S(1)}, f32[8,1408]{1,0:T(8,128)S(1)}, bf16[1408,4992]{1,0:T(8,128)(2,1)}) custom-call(bf16[1152,1024]{1,0:T(8,128)(2,1)} %get-tuple-element.188.refs_0_, bf16[256,1408]{1,0:T(8,128)(2,1)} %add_convert_fusion.2.refs_1_, bf16[256,1408]{1,0:T(8,128)(2,1)} %collective-permute-done.4.refs_2_, ...), custom_call_target="tpu_custom_call" | custom-call | flops 60000002048 | bytes 10000000 | tf_op jit(solution)/shard_map/pallas_call | solution.py:257
  534.6 6.2 shard_map.336
  545.5 88.1 %shard_map.337 = (f32[256,1408]{1,0:T(8,128)}, f32[256,1408]{1,0:T(8,128)}, f32[16,1408]{1,0:T(8,128)}, f32[176,1056]{1,0:T(8,128)}, f32[80,1408]{1,0:T(8,128)}, /*index=5*/bf16[256,1408]{1,0:T(8,128)(2,1)}) custom-call(bf16[256,1408]{1,0:T(8,128)(2,1)} %copy-done.25, f32[8,1408]{1,0:T(8,128)} %copy-done.33, f32[8,1408]{1,0:T(8,128)} %copy-done.34, ...), custom_call_target="tpu_custom_call" | custom-call | flops 89999998976 | bytes 30000000 | tf_op jit(solution)/shard_map/pallas_call | solution.py:486
  636.4 7.6 %all-to-all-start.1 = ((f32[8,1,176]{2,1,0:T(1,128)}), f32[8,1,176]{2,1,0:T(1,128)S(1)}, u32[]{:S(2)}, u32[]{:S(2)}) async-start(f32[8,1,176]{2,1,0:T(1,128)} %copy.123), calls=%async_computation.3 | async-start | bytes 16384 | tf_op jit(solution)/shard_map/all_to_all | solution.py:1317
  655.2 65.7 %shard_map.338 = (f32[352,1408]{1,0:T(8,128)S(1)}, f32[176,128]{1,0:T(8,128)S(1)}) custom-call(bf16[176,2944]{1,0:T(8,128)(2,1)S(1)} %slice.519.in_ref), custom_call_target="tpu_custom_call" | custom-call | flops 40000000000 | bytes 4000000 | tf_op jit(solution)/shard_map/pallas_call | solution.py:573
  (535 shorter events, 253.8 us)
Async XLA Ops:
  7.2 89.6 %all-gather.4.cloned.1.call-start = ((), (), s32[]{:S(2)}) async-start(), calls=%async_computation.5 | async-start | bytes 12570624 | tf_op jit(solution)/shard_map/all_gather | solution.py:1112
  18.9 29.3 %collective-permute-start.9 = (bf16[80,1408]{1,0:T(8,128)(2,1)}, bf16[80,1408]{1,0:T(8,128)(2,1)}, u32[]{:S(2)}, u32[]{:S(2)}) collective-permute-start(bf16[80,1408]{1,0:T(8,128)(2,1)} %param.23), channel_id=1, source_target_pairs={{0,1},{1,2},{2,3},{3,0},{4,5},{5,6},{6,7},{7,4},{8,9},{9,10},{10,1... | collective-permute-start | bytes 675848 | tf_op jit(solution)/shard_map/ppermute | solution.py:54
  18.9 29.3 %collective-permute-start.3 = (bf16[5,176,352]{2,1,0:T(8,128)(2,1)}, bf16[5,176,352]{2,1,0:T(8,128)(2,1)}, u32[]{:S(2)}, u32[]{:S(2)}) collective-permute-start(bf16[5,176,352]{2,1,0:T(8,128)(2,1)} %bitcast_dynamic-update-slice_fusion.2), channel_id=1, source_target_pairs={{0,1},{1,2},{2,3},{3,0},{4,5},{5,6},{6,7},{7,4},{8,9},{9,10},{10,1... | collective-permute-start | bytes 1858568 | tf_op jit(solution)/shard_map/ppermute | solution.py:54
  48.2 21.2 %collective-permute-start.11 = (bf16[5,176,352]{2,1,0:T(8,128)(2,1)}, bf16[5,176,352]{2,1,0:T(8,128)(2,1)}, u32[]{:S(2)}, u32[]{:S(2)}) collective-permute-start(bf16[5,176,352]{2,1,0:T(8,128)(2,1)} %collective-permute-done.3), channel_id=1, source_target_pairs={{0,1},{1,2},{2,3},{3,0},{4,5},{5,6},{6,7},{7,4},{8,9},{9,10},{10,1... | collective-permute-start | bytes 1858568 | tf_op jit(solution)/shard_map/ppermute | solution.py:54
  58.0 138.2 %all-gather.6.cloned.1.call-start = ((), (), s32[]{:S(2)}) async-start(), calls=%async_computation.6 | async-start | bytes 22302720 | tf_op jit(solution)/shard_map/all_gather | solution.py:1186
  90.9 163.3 %all-gather.8.cloned.1.call-start = ((), (), s32[]{:S(2)}) async-start(), calls=%async_computation.7 | async-start | bytes 9732096 | tf_op jit(solution)/shard_map/all_gather | solution.py:1188
  93.2 367.0 %reduce-scatter.4.cloned.1.call-start = ((), (), s32[]{:S(2)}) async-start(), calls=%async_computation.8 | async-start | bytes 9732096 | tf_op jit(solution)/shard_map/reduce_scatter | solution.py:1245
  106.4 21.4 %collective-permute-start.4 = (bf16[256,1408]{1,0:T(8,128)(2,1)}, bf16[256,1408]{1,0:T(8,128)(2,1)}, u32[]{:S(2)}, u32[]{:S(2)}) collective-permute-start(bf16[256,1408]{1,0:T(8,128)(2,1)} %add_convert_fusion.2.refs_1_), channel_id=1, source_target_pairs={{0,1},{1,2},{2,3},{3,0},{4,5},{5,6},{6,7},{7,4},{8,9},{9,10},{10,1... | collective-permute-start | bytes 2162696 | tf_op jit(solution)/shard_map/ppermute | solution.py:54
  160.4 22.4 %collective-permute-start.7 = (bf16[256,1408]{1,0:T(8,128)(2,1)S(1)}, bf16[256,1408]{1,0:T(8,128)(2,1)S(1)}, u32[]{:S(2)}, u32[]{:S(2)}) collective-permute-start(bf16[256,1408]{1,0:T(8,128)(2,1)S(1)} %copy-done.8), channel_id=1, source_target_pairs={{0,1},{1,2},{2,3},{3,0},{4,5},{5,6},{6,7},{7,4},{8,9},{9,10},{10,1... | collective-permute-start | bytes 2162696 | tf_op jit(solution)/shard_map/ppermute | solution.py:54
  182.8 26.8 %collective-permute-start.8 = (bf16[256,352]{1,0:T(8,128)(2,1)}, bf16[256,352]{1,0:T(8,128)(2,1)S(1)}, u32[]{:S(2)}, u32[]{:S(2)}) collective-permute-start(bf16[256,352]{1,0:T(8,128)(2,1)} %get-tuple-element.128), channel_id=1, source_target_pairs={{0,3},{1,0},{2,1},{3,2},{4,7},{5,4},{6,5},{7,6},{8,11},{9,8},{10,9... | collective-permute-start | bytes 540680 | tf_op jit(solution)/shard_map/ppermute | solution.py:54
  182.8 27.6 %collective-permute-start.14 = (bf16[256,352]{1,0:T(8,128)(2,1)}, bf16[256,352]{1,0:T(8,128)(2,1)S(1)}, u32[]{:S(2)}, u32[]{:S(2)}) collective-permute-start(bf16[256,352]{1,0:T(8,128)(2,1)} %get-tuple-element.142), channel_id=1, source_target_pairs={{0,1},{1,2},{2,3},{3,0},{4,5},{5,6},{6,7},{7,4},{8,9},{9,10},{10,1... | collective-permute-start | bytes 540680 | tf_op jit(solution)/shard_map/ppermute | solution.py:54
  186.7 23.8 %collective-permute-start.15 = (bf16[256,352]{1,0:T(8,128)(2,1)}, bf16[256,352]{1,0:T(8,128)(2,1)}, u32[]{:S(2)}, u32[]{:S(2)}) collective-permute-start(bf16[256,352]{1,0:T(8,128)(2,1)} %get-tuple-element.143), channel_id=1, source_target_pairs={{0,2},{1,3},{2,0},{3,1},{4,6},{5,7},{6,4},{7,5},{8,10},{9,11},{10,... | collective-permute-start | bytes 540680 | tf_op jit(solution)/shard_map/ppermute | solution.py:54
  209.5 25.3 %collective-permute-start.16 = (bf16[256,1408]{1,0:T(8,128)(2,1)S(1)}, bf16[256,1408]{1,0:T(8,128)(2,1)S(1)}, u32[]{:S(2)}, u32[]{:S(2)}) collective-permute-start(bf16[256,1408]{1,0:T(8,128)(2,1)S(1)} %collective-permute-done.7.refs_1_), channel_id=1, source_target_pairs={{0,1},{1,2},{2,3},{3,0},{4,5},{5,6},{6,7},{7,4},{8,9},{9,10},{10,1... | collective-permute-start | bytes 2162696 | tf_op jit(solution)/shard_map/ppermute | solution.py:54
  235.7 22.9 %collective-permute-start.18 = (bf16[256,1408]{1,0:T(8,128)(2,1)}, bf16[256,1408]{1,0:T(8,128)(2,1)}, u32[]{:S(2)}, u32[]{:S(2)}) collective-permute-start(bf16[256,1408]{1,0:T(8,128)(2,1)} %get-tuple-element.147.refs_0_), channel_id=1, source_target_pairs={{0,1},{1,2},{2,3},{3,0},{4,5},{5,6},{6,7},{7,4},{8,9},{9,10},{10,1... | collective-permute-start | bytes 2162696 | tf_op jit(solution)/shard_map/ppermute | solution.py:54
  258.1 21.0 %collective-permute-start.17 = (bf16[256,1408]{1,0:T(8,128)(2,1)S(1)}, bf16[256,1408]{1,0:T(8,128)(2,1)S(1)}, u32[]{:S(2)}, u32[]{:S(2)}) collective-permute-start(bf16[256,1408]{1,0:T(8,128)(2,1)S(1)} %copy-done.17), channel_id=1, source_target_pairs={{0,1},{1,2},{2,3},{3,0},{4,5},{5,6},{6,7},{7,4},{8,9},{9,10},{10,1... | collective-permute-start | bytes 2162696 | tf_op jit(solution)/shard_map/ppermute | solution.py:54
  269.5 42.8 %collective-permute-start.21 = (bf16[256,1408]{1,0:T(8,128)(2,1)S(1)}, bf16[256,1408]{1,0:T(8,128)(2,1)S(1)}, u32[]{:S(2)}, u32[]{:S(2)}) collective-permute-start(bf16[256,1408]{1,0:T(8,128)(2,1)S(1)} %convolution_convert_fusion), channel_id=1, source_target_pairs={{0,1},{1,2},{2,3},{3,0},{4,5},{5,6},{6,7},{7,4},{8,9},{9,10},{10,1... | collective-permute-start | bytes 2162696 | tf_op jit(solution)/shard_map/ppermute | solution.py:54
  273.2 34.1 %collective-permute-start.19 = (bf16[256,1408]{1,0:T(8,128)(2,1)}, bf16[256,1408]{1,0:T(8,128)(2,1)S(1)}, u32[]{:S(2)}, u32[]{:S(2)}) collective-permute-start(bf16[256,1408]{1,0:T(8,128)(2,1)} %collective-permute-done.18.refs_1_), channel_id=1, source_target_pairs={{0,1},{1,2},{2,3},{3,0},{4,5},{5,6},{6,7},{7,4},{8,9},{9,10},{10,1... | collective-permute-start | bytes 2162696 | tf_op jit(solution)/shard_map/ppermute | solution.py:54
  313.8 26.5 %collective-permute-start.22 = (bf16[256,1408]{1,0:T(8,128)(2,1)S(1)}, bf16[256,1408]{1,0:T(8,128)(2,1)S(1)}, u32[]{:S(2)}, u32[]{:S(2)}) collective-permute-start(bf16[256,1408]{1,0:T(8,128)(2,1)S(1)} %add_convert_fusion.1), channel_id=1, source_target_pairs={{0,1},{1,2},{2,3},{3,0},{4,5},{5,6},{6,7},{7,4},{8,9},{9,10},{10,1... | collective-permute-start | bytes 2162696 | tf_op jit(solution)/shard_map/ppermute | solution.py:54
  367.7 174.6 %reduce-scatter.6.cloned.1.call-start = ((), (), s32[]{:S(2)}) async-start(), calls=%async_computation.9 | async-start | bytes 13381632 | tf_op jit(solution)/shard_map/reduce_scatter | solution.py:1263
  368.8 38.5 %collective-permute-start.24 = (bf16[256,1408]{1,0:T(8,128)(2,1)S(1)}, bf16[256,1408]{1,0:T(8,128)(2,1)S(1)}, u32[]{:S(2)}, u32[]{:S(2)}) collective-permute-start(bf16[256,1408]{1,0:T(8,128)(2,1)S(1)} %copy-done.98), channel_id=1, source_target_pairs={{0,1},{1,2},{2,3},{3,0},{4,5},{5,6},{6,7},{7,4},{8,9},{9,10},{10,1... | collective-permute-start | bytes 2162696 | tf_op jit(solution)/shard_map/ppermute | solution.py:54
  422.8 227.5 %reduce-scatter.8.cloned.1.call-start = ((), (), s32[]{:S(2)}) async-start(), calls=%async_computation.10 | async-start | bytes 15814656 | tf_op jit(solution)/shard_map/reduce_scatter | solution.py:1303
  427.6 35.9 %collective-permute-start.28 = (bf16[320,704]{1,0:T(8,128)(2,1)}, bf16[320,704]{1,0:T(8,128)(2,1)S(1)}, u32[]{:S(2)}, u32[]{:S(2)}) collective-permute-start(bf16[320,704]{1,0:T(8,128)(2,1)} %get-tuple-element.175), channel_id=1, source_target_pairs={{0,3},{1,0},{2,1},{3,2},{4,7},{5,4},{6,5},{7,6},{8,11},{9,8},{10,9... | collective-permute-start | bytes 1351688 | tf_op jit(solution)/shard_map/ppermute | solution.py:54
  427.9 35.7 %collective-permute-start.29 = (bf16[320,704]{1,0:T(8,128)(2,1)}, bf16[320,704]{1,0:T(8,128)(2,1)}, u32[]{:S(2)}, u32[]{:S(2)}) collective-permute-start(bf16[320,704]{1,0:T(8,128)(2,1)} %get-tuple-element.191), channel_id=1, source_target_pairs={{0,2},{1,3},{2,0},{3,1},{4,6},{5,7},{6,4},{7,5},{8,10},{9,11},{10,... | collective-permute-start | bytes 1351688 | tf_op jit(solution)/shard_map/ppermute | solution.py:54
  430.1 33.4 %collective-permute-start.30 = (bf16[320,704]{1,0:T(8,128)(2,1)}, bf16[320,704]{1,0:T(8,128)(2,1)}, u32[]{:S(2)}, u32[]{:S(2)}) collective-permute-start(bf16[320,704]{1,0:T(8,128)(2,1)} %get-tuple-element.192), channel_id=1, source_target_pairs={{0,1},{1,2},{2,3},{3,0},{4,5},{5,6},{6,7},{7,4},{8,9},{9,10},{10,1... | collective-permute-start | bytes 1351688 | tf_op jit(solution)/shard_map/ppermute | solution.py:54
  (125 other events, 1179.8 us)
Sparse Core Ops, SparseCore 0:
  13.2 68.8 all-gather.3
  91.0 105.1 all-gather.5
  198.6 55.4 all-gather.7
  367.9 72.6 reduce-scatter.3
  444.4 89.7 reduce-scatter.5
  542.5 105.8 reduce-scatter.7

commit v7 on v4

--- a/solution.py
+++ b/solution.py
@@ -1238,7 +1238,7 @@
     grad_bias = sum(jnp.sum(item, axis=0, dtype=FLOAT) for item in pre_lows)
     grads_one = pack_grad(None, mlp_blocks, pre_lows, 2 * hidden, 0, 512)
     grads_one = pack_grad(grads_one, cot_blocks, hidden_lows, 2 * hidden, hidden, 512)
-    grads_one, grad_mlp_in, *out_parts = lax.optimization_barrier((grads_one, grad_mlp_in, *out_parts))
+    grads_one, grad_mlp_in, out_parts[1] = lax.optimization_barrier((grads_one, grad_mlp_in, out_parts[1]))
     out_hop = rot(out_parts[1].astype(BFLOAT), 1)
     summed_one = lax.psum_scatter(grads_one, "dp", scatter_dimension=0, tiled=True).astype(FLOAT)
     cot_here = out_grad.astype(FLOAT)

time: 751 us -> 757 us (level)
  Pallas kernels: 355 us -> 329 us
  starting transfers between devices: 74 us -> 86.3 us
  matrix products: 68.5 us -> 76.7 us
  waiting for transfers between devices: 105 us -> 113 us
    pallas_call x1, Pallas kernels: 62.4 us -> 40.9 us  [ring_sum(): pl.pallas_call(functools.partial(ring_kernel, split, start, places), in_s...]
    ppermute x28, waiting for transfers between devices: 81.2 us -> 96.8 us  [rot(): lax.ppermute(values, 'tensor', [(i, (i + step) % count) for i in range(co...]
    pallas_call x1, Pallas kernels: 106 us -> 91.6 us  [side_sums(): pl.pallas_call(functools.partial(side_kernel, shards, split, hops, text_s...]
    ppermute x28, starting transfers between devices: 63 us -> 75.4 us  [rot(): lax.ppermute(values, 'tensor', [(i, (i + step) % count) for i in range(co...]
    pallas_call x1, Pallas kernels: 54.9 us -> 65.6 us  [spread_sum(): pl.pallas_call(functools.partial(spread_kernel, split, starts), in_specs=...]
    all_gather x1, waiting for transfers between devices: 16.7 us -> 6.41 us  [on_device(): all_three = lax.all_gather(packed_three, 'dp', axis=0, tiled=True)]
    dot_general x25, matrix products: 64.7 us -> 72.9 us  [dot(): lax.dot_general(left, right, (contract, ((), ())), preferred_element_type...]
    unnamed x225 -> x237, local copies, waits for them, and re-layouts: 40.2 us -> 40 us
  transfers between devices with their start and end apart: 39 -> 39, of which waited for: 17 -> 17; matrix products, arithmetic and copies ran while one was open for 19% -> 20% of each run, Pallas kernels for 40% -> 35%
where the time goes in v7:
time: 757 us; the launch traced here: 747 us
  Pallas kernels  329 us (43%)
  waiting for transfers between devices  113 us (15%)
  local copies, waits for them, and re-layouts  92.9 us (12%)
  starting transfers between devices  86.3 us (11%)
  matrix products  76.7 us (10%)
  other arithmetic  31.8 us (4%)
  between operations  17 us (2%)
    ppermute x28, waiting for transfers between devices, rot(): lax.ppermute(values, 'tensor', [(i, (i + step) % count) for i in range(co...  96.8 us
    pallas_call x1, Pallas kernels, side_sums(): pl.pallas_call(functools.partial(side_kernel, shards, split, hops, text_s...  91.6 us
    ppermute x28, starting transfers between devices, rot(): lax.ppermute(values, 'tensor', [(i, (i + step) % count) for i in range(co...  75.4 us
    dot_general x25, matrix products, dot(): lax.dot_general(left, right, (contract, ((), ())), preferred_element_type...  72.9 us
    pallas_call x1, Pallas kernels, spread_sum(): pl.pallas_call(functools.partial(spread_kernel, split, starts), in_specs=...  65.6 us
    pallas_call x1, Pallas kernels, ring_sum(): pl.pallas_call(functools.partial(ring_kernel, split, start, places), in_s...  40.9 us
    unnamed x237, local copies, waits for them, and re-layouts  40 us
    pallas_call x1, Pallas kernels, middle_backward(): pl.pallas_call(functools.partial(middle_backward_kernel, heads, len(text)...  30.2 us
  transfers between devices with their start and end apart: 39, of which 17 were waited for; matrix products, arithmetic and copies ran while one was open for 20% of the time, Pallas kernels for 35%

profile of v7, /device:TPU:24, one launch (start us, length us, event | category | flops | bytes accessed | tf_op | source)
XLA Modules:
  0.0 747.3 jit_solution(1250817288945821895)
XLA Ops:
  60.5 11.6 %collective-permute-done.3 = bf16[80,1408]{1,0:T(8,128)(2,1)} collective-permute-done((bf16[80,1408]{1,0:T(8,128)(2,1)}, bf16[80,1408]{1,0:T(8,128)(2,1)}, u32[]{:S(2)}, u32[]{:S(2)}) %collective-permute-start.3) | collective-permute-done | bytes 225312 | tf_op jit(solution)/shard_map/ppermute | solution.py:54
  78.8 11.0 %collective-permute-done.4 = bf16[5,176,352]{2,1,0:T(8,128)(2,1)S(1)} collective-permute-done((bf16[5,176,352]{2,1,0:T(8,128)(2,1)}, bf16[5,176,352]{2,1,0:T(8,128)(2,1)S(1)}, u32[]{:S(2)}, u32[]{:S(2)}) %collective-permute-start.4) | collective-permute-done | bytes 619552 | tf_op jit(solution)/shard_map/ppermute | solution.py:54
  90.7 5.5 concatenate.149
  109.0 15.4 %collective-permute-start.6 = (bf16[256,1408]{1,0:T(8,128)(2,1)}, bf16[256,1408]{1,0:T(8,128)(2,1)S(1)}, u32[]{:S(2)}, u32[]{:S(2)}) collective-permute-start(bf16[256,1408]{1,0:T(8,128)(2,1)} %refs_5_.2), channel_id=1, source_target_pairs={{0,1},{1,2},{2,3},{3,0},{4,5},{5,6},{6,7},{7,4},{8,9},{9,10},{10,1... | collective-permute-start | bytes 2162696 | tf_op jit(solution)/shard_map/ppermute | solution.py:54
  149.4 5.6 collective-permute-done.10.refs_2_
  165.1 6.2 collective-permute-done.11.refs_3_
  188.9 14.8 %shard_map.324 = (bf16[256,352]{1,0:T(8,128)(2,1)}, bf16[256,352]{1,0:T(8,128)(2,1)}, bf16[256,352]{1,0:T(8,128)(2,1)}, bf16[256,352]{1,0:T(8,128)(2,1)}, bf16[4...) custom-call(f32[1152,256]{1,0:T(8,128)} %convolution_add_fusion.3.re, ...), custom_call_target="tpu_custom_call" | custom-call | flops 20000000000 | bytes 12000000 | tf_op jit(solution)/shard_map/pallas_call | solution.py:758
  209.0 10.0 %shard_map.325 = (f32[320,704]{1,0:T(8,128)S(1)}, bf16[320,704]{1,0:T(8,128)(2,1)S(1)}, bf16[320,704]{1,0:T(8,128)(2,1)S(1)}, bf16[320,704]{1,0:T(8,128)(2,1)S(1)}, bf16[320,704]{1,0:T(8,128)(2,1)S(1)}) custom-call(bf16[320,1408]{1,0:T(8,128)(2,1)S(1)} %constant_dynamic-update-slice_fusion.text_ref.refs_5_, f32[4,704]{1,0:T(4,128)S(1)} %reshape.395.bias_ref, ...), custom_call_target="tpu_custom_call" | custom-call | flops 12000000000 | bytes 10000000 | tf_op jit(solution)/shard_map/pallas_call | solution.py:615
  225.4 23.7 %shard_map.326 = (f32[256,1408]{1,0:T(8,128)}, f32[256,1408]{1,0:T(8,128)}, f32[256,1408]{1,0:T(8,128)}, bf16[256,1408]{1,0:T(8,128)(2,1)}, bf16[256,1408]{1,0:T...) custom-call(bf16[256,352]{1,0:T(8,128)(2,1)} %get-tuple-element.125.refs_0_, ...), custom_call_target="tpu_custom_call" | custom-call | flops 25999998976 | bytes 24000000 | tf_op jit(solution)/shard_map/pallas_call | solution.py:957
  252.6 6.4 all-gather.8.cloned.1.call-done
  270.3 8.5 %collective-permute-done.18.refs_1_ = bf16[256,1408]{1,0:T(8,128)(2,1)} collective-permute-done((bf16[256,1408]{1,0:T(8,128)(2,1)}, bf16[256,1408]{1,0:T(8,128)(2,1)}, u32[]{:S(2)}, u32[]{:S(2)}) %collective-permute-start.18) | collective-permute-done | bytes 720928 | tf_op jit(solution)/shard_map/ppermute | solution.py:54
  292.6 7.4 collective-permute-done.19.refs_2_
  321.2 8.0 %collective-permute-done.20.refs_3_ = bf16[256,1408]{1,0:T(8,128)(2,1)S(1)} collective-permute-done((bf16[256,1408]{1,0:T(8,128)(2,1)S(1)}, bf16[256,1408]{1,0:T(8,128)(2,1)S(1)}, u32[]{:S(2)}, u32[]{:S(2)}) %collective-permute-start.20) | collective-permute-done | bytes 720928 | tf_op jit(solution)/shard_map/ppermute | solution.py:54
  335.1 5.4 collective-permute-done.22
  345.8 8.4 %shard_map.327.refs_8_ = bf16[1408,3072]{1,0:T(8,128)(2,1)} custom-call(bf16[256,1408]{1,0:T(8,128)(2,1)S(1)} %copy-done.18, bf16[256,1408]{1,0:T(8,128)(2,1)} %collective-permute-done.18.refs_1_, bf16[256,1408]{1,0:T(8,128)(2,1)S(1)} %collective-permute-done.19.refs_2_, bf16[256,1408]{1,0:T(8,128)(2,1)S(1)} %collective-permute-done.20.refs_3_, ...), custom_call_target="tpu_custom_call" | custom-call | flops 8858370048 | bytes 10354688 | tf_op jit(solution)/shard_map/pallas_call | solution.py:146
  354.2 8.6 %shard_map.328 = bf16[1408,3072]{1,0:T(8,128)(2,1)} custom-call(bf16[256,1408]{1,0:T(8,128)(2,1)} %refs_5_.2, bf16[256,1408]{1,0:T(8,128)(2,1)S(1)} %copy-done.17, bf16[256,1408]{1,0:T(8,128)(2,1)} %collective-permute-done.16.refs_2_, bf16[256,1408]{1,0:T(8,128)(2,1)S(1)} %collective-permute-done.17.refs_3_, ...), custom_call_target="tpu_custom_call", output_to_operand_aliasing={{}: (8, {})} | custom-call | flops 8858370048 | bytes 10354688 | tf_op jit(solution)/shard_map/pallas_call | solution.py:146
  367.1 30.2 %shard_map.329 = (bf16[256,1408]{1,0:T(8,128)(2,1)}, bf16[256,1408]{1,0:T(8,128)(2,1)}, bf16[256,1408]{1,0:T(8,128)(2,1)}, f32[256,1408]{1,0:T(8,128)}, f32[8,14...) custom-call(bf16[320,704]{1,0:T(8,128)(2,1)} %copy-done.34, ...), custom_call_target="tpu_custom_call" | custom-call | flops 32999999488 | bytes 28000000 | tf_op jit(solution)/shard_map/pallas_call | solution.py:1044
  410.6 16.6 %collective-permute-done.26.refs_14_ = bf16[256,352]{1,0:T(8,128)(2,1)S(1)} collective-permute-done((bf16[256,352]{1,0:T(8,128)(2,1)S(1)}, bf16[256,352]{1,0:T(8,128)(2,1)S(1)}, u32[]{:S(2)}, u32[]{:S(2)}) %collective-permute-start.26) | collective-permute-done | bytes 180256 | tf_op jit(solution)/shard_map/ppermute | solution.py:54
  437.7 22.1 %shard_map.333 = (bf16[1152,1024]{1,0:T(8,128)(2,1)}, f32[768,128]{1,0:T(8,128)}, f32[1152,128]{1,0:T(8,128)}) custom-call(f32[1152,256]{1,0:T(8,128)} %convolution_add_fusion.3.refs_0_, f32[1152,256]{1,0:T(8,128)} %convolution_add_fusion.2.refs_1_, f32[1152,256]{1,0:T(8,128)} %convolution_add_fusion.1.refs_2_, f32[1152,256]{1,0:T(8,128)} %convolution_add_fusion.refs_3_, ...), custom_call_target="tpu_custom_call" | custom-call | flops 28000000000 | bytes 16000000 | tf_op jit(solution)/shard_map/pallas_call | solution.py:845
  477.9 40.9 %shard_map.335 = (f32[256,1408]{1,0:T(8,128)S(1)}, f32[8,1408]{1,0:T(8,128)S(1)}, bf16[1408,4992]{1,0:T(8,128)(2,1)}) custom-call(bf16[1152,1024]{1,0:T(8,128)(2,1)} %get-tuple-element.169.refs_0_, bf16[256,1408]{1,0:T(8,128)(2,1)} %add_convert_fusion.2.refs_1_, bf16[256,1408]{1,0:T(8,128)(2,1)S(1)} %copy-done.11, bf16[256,1408]{1,0:T(8,128)(2,1)S(1)} %copy-done.13, ...), custom_call_target="tpu_custom_call" | custom-call | flops 60000002048 | bytes 10000000 | tf_op jit(solution)/shard_map/pallas_call | solution.py:257
  519.9 6.1 shard_map.336
  544.0 5.9 fusion.54.refs_14_
  551.4 91.6 %shard_map.337 = (f32[256,1408]{1,0:T(8,128)}, f32[256,1408]{1,0:T(8,128)}, f32[16,1408]{1,0:T(8,128)}, f32[176,1056]{1,0:T(8,128)}, f32[80,1408]{1,0:T(8,128)}, /*index=5*/bf16[256,1408]{1,0:T(8,128)(2,1)}) custom-call(bf16[256,1408]{1,0:T(8,128)(2,1)} %copy-done.30, f32[8,1408]{1,0:T(8,128)} %copy-done.38, f32[8,1408]{1,0:T(8,128)} %copy-done.39, ...), custom_call_target="tpu_custom_call" | custom-call | flops 89999998976 | bytes 30000000 | tf_op jit(solution)/shard_map/pallas_call | solution.py:486
  660.7 65.6 %shard_map.338 = (f32[352,1408]{1,0:T(8,128)S(1)}, f32[176,128]{1,0:T(8,128)S(1)}) custom-call(bf16[176,2944]{1,0:T(8,128)(2,1)S(1)} %slice.519.in_ref), custom_call_target="tpu_custom_call" | custom-call | flops 40000000000 | bytes 4000000 | tf_op jit(solution)/shard_map/pallas_call | solution.py:573
  (539 shorter events, 294.6 us)
Async XLA Ops:
  7.2 101.8 %all-gather.4.cloned.1.call-start = ((), (), s32[]{:S(2)}) async-start(), calls=%async_computation.5 | async-start | bytes 12570624 | tf_op jit(solution)/shard_map/all_gather | solution.py:1112
  18.9 30.7 %collective-permute-start.1 = (bf16[80,1408]{1,0:T(8,128)(2,1)}, bf16[80,1408]{1,0:T(8,128)(2,1)}, u32[]{:S(2)}, u32[]{:S(2)}) collective-permute-start(bf16[80,1408]{1,0:T(8,128)(2,1)} %param.23), channel_id=1, source_target_pairs={{0,1},{1,2},{2,3},{3,0},{4,5},{5,6},{6,7},{7,4},{8,9},{9,10},{10,1... | collective-permute-start | bytes 675848 | tf_op jit(solution)/shard_map/ppermute | solution.py:54
  18.9 30.7 %collective-permute-start = (bf16[5,176,352]{2,1,0:T(8,128)(2,1)}, bf16[5,176,352]{2,1,0:T(8,128)(2,1)}, u32[]{:S(2)}, u32[]{:S(2)}) collective-permute-start(bf16[5,176,352]{2,1,0:T(8,128)(2,1)} %bitcast_dynamic-update-slice_fusion.2), channel_id=1, source_target_pairs={{0,1},{1,2},{2,3},{3,0},{4,5},{5,6},{6,7},{7,4},{8,9},{9,10},{10,1... | collective-permute-start | bytes 1858568 | tf_op jit(solution)/shard_map/ppermute | solution.py:54
  47.6 161.4 %all-gather.6.cloned.1.call-start = ((), (), s32[]{:S(2)}) async-start(), calls=%async_computation.6 | async-start | bytes 22302720 | tf_op jit(solution)/shard_map/all_gather | solution.py:1184
  49.6 22.6 %collective-permute-start.2 = (bf16[5,176,352]{2,1,0:T(8,128)(2,1)}, bf16[5,176,352]{2,1,0:T(8,128)(2,1)}, u32[]{:S(2)}, u32[]{:S(2)}) collective-permute-start(bf16[5,176,352]{2,1,0:T(8,128)(2,1)} %collective-permute-done), channel_id=1, source_target_pairs={{0,1},{1,2},{2,3},{3,0},{4,5},{5,6},{6,7},{7,4},{8,9},{9,10},{10,1... | collective-permute-start | bytes 1858568 | tf_op jit(solution)/shard_map/ppermute | solution.py:54
  96.3 162.7 %all-gather.8.cloned.1.call-start = ((), (), s32[]{:S(2)}) async-start(), calls=%async_computation.7 | async-start | bytes 9732096 | tf_op jit(solution)/shard_map/all_gather | solution.py:1186
  98.6 366.2 %reduce-scatter.4.cloned.1.call-start = ((), (), s32[]{:S(2)}) async-start(), calls=%async_computation.8 | async-start | bytes 9732096 | tf_op jit(solution)/shard_map/reduce_scatter | solution.py:1243
  109.0 28.7 %collective-permute-start.6 = (bf16[256,1408]{1,0:T(8,128)(2,1)}, bf16[256,1408]{1,0:T(8,128)(2,1)S(1)}, u32[]{:S(2)}, u32[]{:S(2)}) collective-permute-start(bf16[256,1408]{1,0:T(8,128)(2,1)} %refs_5_.2), channel_id=1, source_target_pairs={{0,1},{1,2},{2,3},{3,0},{4,5},{5,6},{6,7},{7,4},{8,9},{9,10},{10,1... | collective-permute-start | bytes 2162696 | tf_op jit(solution)/shard_map/ppermute | solution.py:54
  223.1 26.0 %collective-permute-start.16 = (bf16[256,1408]{1,0:T(8,128)(2,1)S(1)}, bf16[256,1408]{1,0:T(8,128)(2,1)}, u32[]{:S(2)}, u32[]{:S(2)}) collective-permute-start(bf16[256,1408]{1,0:T(8,128)(2,1)S(1)} %copy-done.17), channel_id=1, source_target_pairs={{0,1},{1,2},{2,3},{3,0},{4,5},{5,6},{6,7},{7,4},{8,9},{9,10},{10,1... | collective-permute-start | bytes 2162696 | tf_op jit(solution)/shard_map/ppermute | solution.py:54
  249.1 81.8 %collective-permute-start.17 = (bf16[256,1408]{1,0:T(8,128)(2,1)}, bf16[256,1408]{1,0:T(8,128)(2,1)S(1)}, u32[]{:S(2)}, u32[]{:S(2)}) collective-permute-start(bf16[256,1408]{1,0:T(8,128)(2,1)} %collective-permute-done.16.refs_2_), channel_id=1, source_target_pairs={{0,1},{1,2},{2,3},{3,0},{4,5},{5,6},{6,7},{7,4},{8,9},{9,10},{10,1... | collective-permute-start | bytes 2162696 | tf_op jit(solution)/shard_map/ppermute | solution.py:54
  251.6 27.3 %collective-permute-start.18 = (bf16[256,1408]{1,0:T(8,128)(2,1)}, bf16[256,1408]{1,0:T(8,128)(2,1)}, u32[]{:S(2)}, u32[]{:S(2)}) collective-permute-start(bf16[256,1408]{1,0:T(8,128)(2,1)} %get-tuple-element.131.refs_0_), channel_id=1, source_target_pairs={{0,1},{1,2},{2,3},{3,0},{4,5},{5,6},{6,7},{7,4},{8,9},{9,10},{10,1... | collective-permute-start | bytes 2162696 | tf_op jit(solution)/shard_map/ppermute | solution.py:54
  278.9 21.2 %collective-permute-start.19 = (bf16[256,1408]{1,0:T(8,128)(2,1)}, bf16[256,1408]{1,0:T(8,128)(2,1)S(1)}, u32[]{:S(2)}, u32[]{:S(2)}) collective-permute-start(bf16[256,1408]{1,0:T(8,128)(2,1)} %collective-permute-done.18.refs_1_), channel_id=1, source_target_pairs={{0,1},{1,2},{2,3},{3,0},{4,5},{5,6},{6,7},{7,4},{8,9},{9,10},{10,1... | collective-permute-start | bytes 2162696 | tf_op jit(solution)/shard_map/ppermute | solution.py:54
  290.3 25.1 %collective-permute-start.21 = (bf16[256,1408]{1,0:T(8,128)(2,1)S(1)}, bf16[256,1408]{1,0:T(8,128)(2,1)S(1)}, u32[]{:S(2)}, u32[]{:S(2)}) collective-permute-start(bf16[256,1408]{1,0:T(8,128)(2,1)S(1)} %convolution_convert_fusion), channel_id=1, source_target_pairs={{0,1},{1,2},{2,3},{3,0},{4,5},{5,6},{6,7},{7,4},{8,9},{9,10},{10,1... | collective-permute-start | bytes 2162696 | tf_op jit(solution)/shard_map/ppermute | solution.py:54
  300.1 29.1 %collective-permute-start.20 = (bf16[256,1408]{1,0:T(8,128)(2,1)S(1)}, bf16[256,1408]{1,0:T(8,128)(2,1)S(1)}, u32[]{:S(2)}, u32[]{:S(2)}) collective-permute-start(bf16[256,1408]{1,0:T(8,128)(2,1)S(1)} %collective-permute-done.19.refs_2_), channel_id=1, source_target_pairs={{0,1},{1,2},{2,3},{3,0},{4,5},{5,6},{6,7},{7,4},{8,9},{9,10},{10,1... | collective-permute-start | bytes 2162696 | tf_op jit(solution)/shard_map/ppermute | solution.py:54
  316.8 23.7 %collective-permute-start.22 = (bf16[256,1408]{1,0:T(8,128)(2,1)S(1)}, bf16[256,1408]{1,0:T(8,128)(2,1)S(1)}, u32[]{:S(2)}, u32[]{:S(2)}) collective-permute-start(bf16[256,1408]{1,0:T(8,128)(2,1)S(1)} %add_convert_fusion.1), channel_id=1, source_target_pairs={{0,1},{1,2},{2,3},{3,0},{4,5},{5,6},{6,7},{7,4},{8,9},{9,10},{10,1... | collective-permute-start | bytes 2162696 | tf_op jit(solution)/shard_map/ppermute | solution.py:54
  341.5 21.3 %collective-permute-start.23 = (bf16[256,1408]{1,0:T(8,128)(2,1)}, bf16[256,1408]{1,0:T(8,128)(2,1)}, u32[]{:S(2)}, u32[]{:S(2)}) collective-permute-start(bf16[256,1408]{1,0:T(8,128)(2,1)} %add_convert_fusion), channel_id=1, source_target_pairs={{0,1},{1,2},{2,3},{3,0},{4,5},{5,6},{6,7},{7,4},{8,9},{9,10},{10,1... | collective-permute-start | bytes 2162696 | tf_op jit(solution)/shard_map/ppermute | solution.py:54
  365.6 167.2 %reduce-scatter.6.cloned.1.call-start = ((), (), s32[]{:S(2)}) async-start(), calls=%async_computation.9 | async-start | bytes 13381632 | tf_op jit(solution)/shard_map/reduce_scatter | solution.py:1261
  366.7 34.7 %collective-permute-start.24 = (bf16[256,1408]{1,0:T(8,128)(2,1)S(1)}, bf16[256,1408]{1,0:T(8,128)(2,1)S(1)}, u32[]{:S(2)}, u32[]{:S(2)}) collective-permute-start(bf16[256,1408]{1,0:T(8,128)(2,1)S(1)} %copy-done.99), channel_id=1, source_target_pairs={{0,1},{1,2},{2,3},{3,0},{4,5},{5,6},{6,7},{7,4},{8,9},{9,10},{10,1... | collective-permute-start | bytes 2162696 | tf_op jit(solution)/shard_map/ppermute | solution.py:54
  401.6 25.6 %collective-permute-start.26 = (bf16[256,352]{1,0:T(8,128)(2,1)S(1)}, bf16[256,352]{1,0:T(8,128)(2,1)S(1)}, u32[]{:S(2)}, u32[]{:S(2)}) collective-permute-start(bf16[256,352]{1,0:T(8,128)(2,1)S(1)} %copy-done.104), channel_id=1, source_target_pairs={{0,2},{1,3},{2,0},{3,1},{4,6},{5,7},{6,4},{7,5},{8,10},{9,11},{10,... | collective-permute-start | bytes 540680 | tf_op jit(solution)/shard_map/ppermute | solution.py:54
  404.6 22.6 %collective-permute-start.27 = (bf16[256,352]{1,0:T(8,128)(2,1)S(1)}, bf16[256,352]{1,0:T(8,128)(2,1)S(1)}, u32[]{:S(2)}, u32[]{:S(2)}) collective-permute-start(bf16[256,352]{1,0:T(8,128)(2,1)S(1)} %copy-done.103), channel_id=1, source_target_pairs={{0,3},{1,0},{2,1},{3,2},{4,7},{5,4},{6,5},{7,6},{8,11},{9,8},{10,9... | collective-permute-start | bytes 540680 | tf_op jit(solution)/shard_map/ppermute | solution.py:54
  427.9 227.9 %reduce-scatter.8.cloned.1.call-start = ((), (), s32[]{:S(2)}) async-start(), calls=%async_computation.10 | async-start | bytes 15814656 | tf_op jit(solution)/shard_map/reduce_scatter | solution.py:1301
  433.8 34.0 %collective-permute-start.28 = (bf16[320,704]{1,0:T(8,128)(2,1)}, bf16[320,704]{1,0:T(8,128)(2,1)S(1)}, u32[]{:S(2)}, u32[]{:S(2)}) collective-permute-start(bf16[320,704]{1,0:T(8,128)(2,1)} %get-tuple-element.156), channel_id=1, source_target_pairs={{0,3},{1,0},{2,1},{3,2},{4,7},{5,4},{6,5},{7,6},{8,11},{9,8},{10,9... | collective-permute-start | bytes 1351688 | tf_op jit(solution)/shard_map/ppermute | solution.py:54
  433.9 33.9 %collective-permute-start.29 = (bf16[320,704]{1,0:T(8,128)(2,1)}, bf16[320,704]{1,0:T(8,128)(2,1)}, u32[]{:S(2)}, u32[]{:S(2)}) collective-permute-start(bf16[320,704]{1,0:T(8,128)(2,1)} %get-tuple-element.172), channel_id=1, source_target_pairs={{0,2},{1,3},{2,0},{3,1},{4,6},{5,7},{6,4},{7,5},{8,10},{9,11},{10,... | collective-permute-start | bytes 1351688 | tf_op jit(solution)/shard_map/ppermute | solution.py:54
  433.9 33.9 %collective-permute-start.30 = (bf16[320,704]{1,0:T(8,128)(2,1)}, bf16[320,704]{1,0:T(8,128)(2,1)}, u32[]{:S(2)}, u32[]{:S(2)}) collective-permute-start(bf16[320,704]{1,0:T(8,128)(2,1)} %get-tuple-element.173), channel_id=1, source_target_pairs={{0,1},{1,2},{2,3},{3,0},{4,5},{5,6},{6,7},{7,4},{8,9},{9,10},{10,1... | collective-permute-start | bytes 1351688 | tf_op jit(solution)/shard_map/ppermute | solution.py:54
  (127 other events, 1105.9 us)
Sparse Core Ops, SparseCore 0:
  13.2 68.7 all-gather.3
  96.4 104.5 all-gather.5
  203.5 55.4 all-gather.7
  365.8 73.4 reduce-scatter.3
  443.0 89.7 reduce-scatter.5
  536.3 102.6 reduce-scatter.7
